TPU v7x, 256 devices: a whole 4x4x8 slice. The times are simulated.
256 devices in a mesh: lat: 16 (over z_lo, x, core), ord: 16 (over z_hi, y).
Axes of the slice: x: 4, y: 4, z: 8 (z_hi: 4, z_lo: 2; z = z_hi * 2 + z_lo), core: 2. Of those that a mesh axis runs over, the one named last changes fastest.
Arguments:
- altitude_grids: bfloat16 [2, 3072, 21600], P(None, 'lat', 'ord'), may hold values from -6 to 6
- polynomial_values: bfloat16 [32, 3072, 10802], P('ord', 'lat'), may hold values from -6 to 6
- span_azimuthal_modes: int32 [64], replicated, may hold values from 0 to 10800, as said below
- slot_mapping: int32 [64], replicated, may hold values from 0 to 63, as said below
Outputs:
- steepness: bfloat16 [2, 3072, 21600], P(None, 'lat', 'ord')
- curvature: bfloat16 [2, 3072, 21600], P(None, 'lat', 'ord')
Inputs may be any that keep to these rules, and one draw needn't show every extreme that they name: `span_azimuthal_modes`: rising and distinct; the first 32 entries lie below 5400 and the first is 0; entry 63-i is 10800 minus entry i. `slot_mapping`: A permutation; slot 2k holds an entry below 32 and slot 2k+1 holds 63 minus it, so slots 2k and 2k+1 take orders m and 10800-m. Slot s lies on index s // 4 of ord.
All inputs are finite; a program needn't handle non-finite values.
Results may differ from a plain program's by a relative error of at most 0.0079.
Values sent between devices are 32-bit elements; how exact they have to be, the bound alone decides.
No kernel may reach another device: no remote copies, remote signals or barrier semaphores. Data moves between devices by JAX's collectives and lax.ppermute only.
A program may use at most 64 MiB of HBM per device.

v0:
```python
import math

import jax
import jax.numpy as jnp
from jax import lax
from jax.sharding import PartitionSpec as P

LMAX = 10800
MERIDIAN_AMOUNT = 21600
BAND = 64
NLAT = 10801


def slot_orders(span_azimuthal_modes, slot_mapping):
    match = slot_mapping[:, None] == jnp.arange(BAND, dtype=jnp.int32)[None, :]
    return jnp.sum(jnp.where(match, span_azimuthal_modes[None, :], 0), axis=1)


def phases(orders, longitude):
    turns = orders[:, None] * longitude[None, :] % MERIDIAN_AMOUNT
    return turns.astype(jnp.float32) * (2.0 * math.pi / MERIDIAN_AMOUNT)


def colatitude(cycles, nring):
    return math.pi * (cycles.astype(jnp.float32) + 0.5 * (NLAT - nring + 1)) / NLAT


def variants(coeffs, first_order):
    pack = coeffs.shape[-1]
    position = jnp.arange(pack, dtype=jnp.int32)[None, :]
    first_len = (LMAX + 1 - first_order)[:, None]
    in_upper = position >= first_len
    degree = jnp.where(in_upper, position - 1, first_order[:, None] + position).astype(jnp.float32)
    order_val = jnp.where(in_upper, LMAX - first_order[:, None], first_order[:, None]).astype(
        jnp.float32
    )
    length = jnp.where(in_upper, first_order[:, None] + 1, first_len).astype(jnp.float32)
    scaling = 1.0 / jnp.sqrt(length)
    shifted = jnp.concatenate([coeffs[..., 1:], jnp.zeros_like(coeffs[..., :1])], axis=-1)
    shifted = jnp.where((position == first_len - 1)[:, None, None, :], 0.0, shifted)

    def spread(values):
        return values[:, None, None, :]

    stacked = jnp.stack(
        [
            coeffs * spread(scaling),
            coeffs * spread(degree * scaling / LMAX),
            shifted * spread((degree + 1.0 + order_val) * scaling / LMAX),
            coeffs * spread(degree * (degree + 1.0) * scaling / (LMAX * LMAX)),
        ],
        axis=1,
    )
    upper_mask = in_upper[:, None, None, None, :]
    return jnp.stack(
        [jnp.where(upper_mask, 0.0, stacked), jnp.where(upper_mask, stacked, 0.0)], axis=1
    ).astype(jnp.bfloat16)


def syntheses(synth, cycle_sine, cycle_cosine):
    slope_part = (cycle_cosine * synth[:, 1] - synth[:, 2]) / cycle_sine
    return jnp.stack([synth[:, 0], slope_part, synth[:, 3]], axis=1)


def derive(spectra, order_frac, cycle_sine):
    first = spectra[:, 0]
    slope_part = spectra[:, 1]
    laplace = spectra[:, 2]
    factor = order_frac[:, None, None] / cycle_sine
    square = factor * factor
    phi_grad = jnp.stack([-factor * first[:, 1], factor * first[:, 0]], axis=1)
    theta_theta = square[:, None] * first - laplace
    theta_phi = jnp.stack([-factor * slope_part[:, 1], factor * slope_part[:, 0]], axis=1)
    phi_phi = -square[:, None] * first
    return jnp.stack([slope_part, phi_grad, theta_theta, theta_phi, phi_phi], axis=1)


def surface(grid_fields):
    theta_grad = grid_fields[0]
    phi_grad = grid_fields[1]
    theta_theta = grid_fields[2]
    theta_phi = grid_fields[3]
    phi_phi = grid_fields[4]
    area = 1.0 + theta_grad * theta_grad + phi_grad * phi_grad
    steepness = jnp.sqrt(area)
    bending = (
        (1.0 + phi_grad * phi_grad) * theta_theta
        - 2.0 * theta_grad * phi_grad * theta_phi
        + (1.0 + theta_grad * theta_grad) * phi_phi
    ) / (2.0 * area * steepness)
    return (steepness.astype(jnp.bfloat16), bending.astype(jnp.bfloat16))


def on_device(altitude_grids, polynomial_values, span_azimuthal_modes, slot_mapping):
    altitude_maps, period_index, meridian_index = altitude_grids.shape
    pair_count = polynomial_values.shape[0]
    pack = polynomial_values.shape[2]
    slot_count = 2 * pair_count
    nring = period_index * lax.axis_size("lat")
    orders = slot_orders(span_azimuthal_modes, slot_mapping)
    longitude = lax.axis_index("ord") * meridian_index + jnp.arange(meridian_index, dtype=jnp.int32)
    cycles = lax.axis_index("lat") * period_index + jnp.arange(period_index, dtype=jnp.int32)
    colat = colatitude(cycles, nring)
    cycle_sine = jnp.sin(colat)
    cycle_cosine = jnp.cos(colat)
    altitude_lines = altitude_grids.reshape(altitude_maps * period_index, meridian_index)
    angles = phases(orders, longitude)
    trig_rows = (
        jnp.stack([jnp.cos(angles), -jnp.sin(angles)], axis=1) / math.sqrt(MERIDIAN_AMOUNT)
    ).astype(jnp.bfloat16)
    product = lax.dot_general(
        trig_rows.reshape(slot_count * lax.axis_size("ord") * 2, meridian_index),
        altitude_lines,
        (((1,), (1,)), ((), ())),
        preferred_element_type=jnp.float32,
    )
    cycle_coefficient = lax.psum_scatter(
        product.reshape(slot_count * lax.axis_size("ord"), 2 * altitude_maps * period_index),
        "ord",
        scatter_dimension=0,
        tiled=True,
    )
    cycle_coefficient = cycle_coefficient.reshape(slot_count, 2, altitude_maps, period_index)
    weighted = (cycle_coefficient * cycle_sine / math.sqrt(nring)).astype(jnp.bfloat16)
    product = jnp.einsum(
        "puxfr,prk->puxfk",
        weighted.reshape(pair_count, 2, 2, altitude_maps, period_index),
        polynomial_values,
        preferred_element_type=jnp.float32,
    )
    local_orders = lax.dynamic_slice_in_dim(orders, lax.axis_index("ord") * slot_count, slot_count)
    first_order = local_orders.reshape(pair_count, 2)[:, 0]
    position = jnp.arange(pack, dtype=jnp.int32)[None, :]
    in_upper = (position >= (LMAX + 1 - first_order)[:, None])[:, None, None, :]
    partial_value = jnp.where(in_upper, product[:, 1], product[:, 0])
    coeffs = lax.psum(partial_value, "lat")
    weights = variants(coeffs, first_order)
    synth = jnp.einsum(
        "prk,pujxfk->pujxfr", polynomial_values, weights, preferred_element_type=jnp.float32
    )
    synth = synth.reshape(slot_count, 4, 2, altitude_maps, period_index)
    spectra = syntheses(synth, cycle_sine, cycle_cosine)
    order_frac = orders.astype(jnp.float32) / LMAX
    angles = phases(orders, longitude)
    inv_table = jnp.stack([jnp.cos(angles), -jnp.sin(angles)], axis=1) / math.sqrt(BAND)
    local_frac = lax.dynamic_slice_in_dim(
        order_frac, lax.axis_index("ord") * slot_count, slot_count
    )
    spectral = derive(spectra, local_frac, cycle_sine)
    grid_fields = jnp.einsum(
        "scxfr,sxj->cfrj",
        lax.all_gather(spectral, "ord", axis=0, tiled=True),
        inv_table,
        precision=lax.Precision.HIGHEST,
    )
    return surface(grid_fields)


def solution(mesh):
    return jax.shard_map(
        on_device,
        mesh=mesh,
        in_specs=(P(None, "lat", "ord"), P("ord", "lat", None), P(), P()),
        out_specs=(P(None, "lat", "ord"), P(None, "lat", "ord")),
        check_vma=False,
    )
```

profile of v0, /device:TPU:6, one launch (start us, length us, event | category | flops | bytes accessed | tf_op | source)
XLA Modules:
  0.0 380.1 jit_solution(9268967327565148664)
XLA Ops:
  7.2 0.0 copy-start
  7.2 0.0 all-reduce.7.cloned.1.call-start
  7.2 0.9 select_reduce_fusion
  8.2 1.5 fusion.22
  9.7 0.1 multiply_convert_fusion
  9.8 0.0 copy-start.1
  9.8 0.4 copy.37
  10.2 0.3 convert_element_type.95
  10.5 0.0 copy-done
  10.5 0.4 fusion.44
  10.9 0.7 reshape.726
  11.7 0.0 all-reduce.7.cloned.1.call-update
  11.7 0.0 all-reduce.5.cloned.1.call-start
  11.8 0.1 dynamic_slice.6
  11.8 0.1 reshape.724
  11.9 0.1 subtract_reduce_fusion
  12.1 0.1 iota_compare_fusion.1
  12.2 0.3 multiply_multiply_fusion
  12.5 0.1 iota_compare_fusion
  12.6 0.0 copy-done.1
  12.6 0.6 dynamic-slice
  13.9 158.6 %all-reduce.7.cloned.1.call-done = f32[64,768]{1,0:T(8,128)} async-done(((f32[64,768]{1,0:T(8,128)}), f32[64,768]{1,0:T(8,128)}) %all-reduce.7.cloned.1.call-update) | async-done | bytes 196624
  172.5 0.7 constant_dynamic-slice_fusion
  173.3 0.1 reshape.727
  173.4 4.6 %fusion.2 = f32[2,2,2,2,10802]{4,3,2,1,0:T(2,128)S(1)} fusion(bf16[2,192,10802]{2,1,0:T(8,128)(2,1)} %param.5, f32[2,2,2,2,192]{4,3,2,1,0:T(2,128)S(1)} %reshape.727, f32[192]{0:T(256)S(1)} %fusion.35), kind=kOutput, calls=%fused_computation.2 | convolution fusion | flops 66376704 | bytes 9000320 | tf_op jit(solution)/shard_map/puxfr,prk->puxfk/dot_general | solution.py:125
  177.9 1.0 fusion.24
  178.9 0.0 all-reduce.5.cloned.1.call-update
  179.0 0.1 dynamic_slice.7
  179.1 0.1 fusion.42
  179.2 116.2 %all-reduce.5.cloned.1.call-done = f32[2,2,2,10802]{3,2,1,0:T(2,128)} async-done(((f32[2,2,2,10802]{3,2,1,0:T(2,128)}), f32[2,2,2,10802]{3,2,1,0:T(2,128)}) %all-reduce.5.cloned.1.call-update) | async-done | bytes 345680 | tf_op jit(solution)/shard_map/psum | solution.py:136
  295.3 1.4 slice.70
  296.7 1.6 multiply_bitcast_fusion.3
  298.3 1.1 select_convert_fusion.1
  299.4 0.7 select_convert_fusion
  300.1 6.1 %fusion = f32[2,2,4,2,2,192]{5,4,3,2,1,0:T(2,128)S(1)} fusion(bf16[2,192,10802]{2,1,0:T(8,128)(2,1)} %param.5, bf16[2,1,4,2,2,10802]{5,4,3,0,2,1:T(2,128)(2,1)S(1)} %select_convert_fusion, bf16[2,1,4,2,2,10802]{5,4,3,0,2,1:T(2,128)(2,1)S(1)} %get-tuple-element.6), kind=kOutput, calls=%fused_computation | convolution fusion | flops 266161280 | bytes 9727744 | tf_op jit(solution)/shard_map/prk,pujxfk->pujxfr/dot_general | solution.py:138
  306.4 54.8 %all_gather.3 = f32[64,5,2,2,192]{4,3,2,1,0:T(2,128)S(1)} all-gather(f32[4,5,2,2,192]{4,3,2,1,0:T(2,128)S(1)} %copy.41), channel_id=1, replica_groups=mesh['lat'=16,'ord'=16] {'ord'}, dimensions={0}, use_global_device_ids=true | all-gather | bytes 1044480 | tf_op jit(solution)/shard_map/all_gather | solution.py:152
  361.2 9.3 %convolution_bitcast_fusion = f32[5,2,192,1350]{3,2,1,0:T(8,128)S(1)} fusion(f32[64,5,2,2,192]{4,3,2,1,0:T(2,128)S(1)} %all_gather.3, f32[64,1,1350]{2,0,1:T(8,128)S(1)} %get-tuple-element.25, f32[64,1,1350]{2,0,1:T(8,128)S(1)} %get-tuple-element.24), kind=kOutput, calls=%fused_computation.4 | convolution fusion | flops 3981657600 | bytes 12042240 | tf_op jit(solution)/shard_map/scxfr,sxj->cfrj/dot_general | solution.py:150
  370.5 2.7 fusion.14
  (15 shorter events, 0.3 us)
Async XLA Ops:
  7.2 3.3 copy-start
  7.2 165.4 %all-reduce.7.cloned.1.call-start = ((), (), s32[]{:S(2)}) async-start(), calls=%async_computation.1 | async-start | bytes 393216
  9.8 2.8 copy-start.1
  11.7 283.7 %all-reduce.5.cloned.1.call-start = ((), (), s32[]{:S(2)}) async-start(), calls=%async_computation | async-start | bytes 696320 | tf_op jit(solution)/shard_map/psum | solution.py:136
Sparse Core Ops, SparseCore 0:
  11.8 160.6 all-reduce.6
  179.1 116.2 all-reduce.4
where the time goes:
time: 387 us; the launch traced here: 380 us
  waiting for transfers between devices  275 us (71%)
  blocking collectives  54.8 us (14%)
  matrix products  20.4 us (5%)
  between operations  14.9 us (4%)
  other arithmetic  10.5 us (3%)
  local copies, waits for them, and re-layouts  4.51 us (1%)
    unnamed x3, waiting for transfers between devices  159 us
    psum x1, waiting for transfers between devices, on_device(): coeffs = lax.psum(partial_value, 'lat')  116 us
    all_gather x1, blocking collectives, on_device(): lax.all_gather(spectral, 'ord', axis=0, tiled=True)  54.8 us
    dot_general x1, matrix products, on_device(): jnp.einsum('scxfr,sxj->cfrj', lax.all_gather(spectral, 'ord', axis=0, til...  9.31 us
  transfers between devices with their start and end apart: 2, of which 2 were waited for; matrix products, arithmetic and copies ran while one was open for 0% of the time, Pallas kernels for 0%

commit v1 on v0

v1 whole, which is shorter than its diff:
```python
import math

import jax
import jax.numpy as jnp
from jax import lax
from jax.sharding import PartitionSpec as P

LMAX = 10800
MERIDIAN_AMOUNT = 21600
BAND = 64
NLAT = 10801


def slot_orders(span_azimuthal_modes, slot_mapping):
    match = slot_mapping[:, None] == jnp.arange(BAND, dtype=jnp.int32)[None, :]
    return jnp.sum(jnp.where(match, span_azimuthal_modes[None, :], 0), axis=1)


def phases(orders, longitude):
    turns = orders[:, None] * longitude[None, :] % MERIDIAN_AMOUNT
    return turns.astype(jnp.float32) * (2.0 * math.pi / MERIDIAN_AMOUNT)


def colatitude(cycles, nring):
    return math.pi * (cycles.astype(jnp.float32) + 0.5 * (NLAT - nring + 1)) / NLAT


def variants(coeffs, first_order):
    pack = coeffs.shape[-1]
    position = jnp.arange(pack, dtype=jnp.int32)
    first_len = LMAX + 1 - first_order
    in_upper = position >= first_len
    degree = jnp.where(in_upper, position - 1, first_order + position).astype(jnp.float32)
    order_val = jnp.where(in_upper, LMAX - first_order, first_order).astype(jnp.float32)
    length = jnp.where(in_upper, first_order + 1, first_len).astype(jnp.float32)
    scaling = 1.0 / jnp.sqrt(length)
    shifted = jnp.concatenate([coeffs[..., 1:], jnp.zeros_like(coeffs[..., :1])], axis=-1)
    shifted = jnp.where(position == first_len - 1, 0.0, shifted)
    stacked = jnp.stack(
        [
            coeffs * scaling,
            coeffs * (degree * scaling / LMAX),
            shifted * ((degree + 1.0 + order_val) * scaling / LMAX),
            coeffs * (degree * (degree + 1.0) * scaling / (LMAX * LMAX)),
        ]
    )
    return jnp.stack(
        [jnp.where(in_upper, 0.0, stacked), jnp.where(in_upper, stacked, 0.0)]
    ).astype(jnp.bfloat16)


def surface(p, q, r, s, t):
    area = 1.0 + p * p + q * q
    steepness = jnp.sqrt(area)
    bending = ((1.0 + q * q) * r - 2.0 * p * q * s + (1.0 + p * p) * t) / (2.0 * area * steepness)
    return steepness.astype(jnp.bfloat16), bending.astype(jnp.bfloat16)


def swap(value, axis, mask):
    return lax.ppermute(value, axis, [(k, k ^ mask) for k in range(lax.axis_size(axis))])


def on_device(altitude_grids, polynomial_values, span_azimuthal_modes, slot_mapping):
    layers, rings, meridians = altitude_grids.shape
    pack = polynomial_values.shape[2]
    n_ord = lax.axis_size("ord")
    nring = rings * lax.axis_size("lat")
    orders = slot_orders(span_azimuthal_modes, slot_mapping)
    longitude = lax.axis_index("ord") * meridians + jnp.arange(meridians, dtype=jnp.int32)
    cycles = lax.axis_index("lat") * rings + jnp.arange(rings, dtype=jnp.int32)
    colat = colatitude(cycles, nring)
    sine = jnp.sin(colat)
    cosine = jnp.cos(colat)
    angles = phases(orders, longitude)
    wave = jnp.stack([jnp.cos(angles), -jnp.sin(angles)], axis=1).reshape(2 * BAND, meridians)
    product = lax.dot_general(
        (wave / math.sqrt(MERIDIAN_AMOUNT)).astype(jnp.bfloat16),
        altitude_grids.reshape(layers * rings, meridians),
        (((1,), (1,)), ((), ())),
        preferred_element_type=jnp.float32,
    )
    parts = lax.all_to_all(
        product.reshape(n_ord, 8, layers * rings), "ord", 0, 0, tiled=True
    )
    cycle_coefficient = jnp.sum(parts, axis=0).reshape(2, 2, 2, layers, rings)
    weighted = (cycle_coefficient * sine / math.sqrt(nring)).astype(jnp.bfloat16)

    core = lax.axis_index("lat") % 2
    local_orders = lax.dynamic_slice_in_dim(orders, lax.axis_index("ord") * 4, 4)

    def analysis(pair):
        rows = lax.dynamic_index_in_dim(weighted, pair, 0, False)
        table = lax.dynamic_index_in_dim(polynomial_values, pair, 0, False)
        first_order = lax.dynamic_index_in_dim(local_orders, 2 * pair, 0, False)
        product = jnp.einsum("uxfr,rk->uxfk", rows, table, preferred_element_type=jnp.float32)
        in_upper = jnp.arange(pack, dtype=jnp.int32) >= LMAX + 1 - first_order
        return jnp.where(in_upper, product[1], product[0]).reshape(4, pack)

    coeffs = analysis(core) + swap(analysis(1 - core), "lat", 1)
    for mask in (2, 6, 8):
        coeffs = coeffs + swap(coeffs, "lat", mask)
    both = [coeffs, swap(coeffs, "lat", 1)]

    def synthesis(pair, coeffs):
        table = lax.dynamic_index_in_dim(polynomial_values, pair, 0, False)
        first_order = lax.dynamic_index_in_dim(local_orders, 2 * pair, 0, False)
        weights = variants(coeffs.reshape(2, layers, pack), first_order)
        synth = jnp.einsum("rk,ujxfk->juxfr", table, weights, preferred_element_type=jnp.float32)
        return jnp.stack([synth[0], (cosine * synth[1] - synth[2]) / sine, synth[3]])

    fields = jnp.stack([synthesis(core, both[0]), synthesis(1 - core, both[1])], axis=1)
    fields = fields.reshape(24, layers * rings)
    everything = lax.all_to_all(
        jnp.broadcast_to(fields[None], (n_ord,) + fields.shape), "ord", 0, 0, tiled=True
    ).reshape(n_ord, 3, 8, layers, rings)
    spectra = [everything[:, i].reshape(2 * BAND, layers, rings) for i in range(3)]

    def in_order(rows):
        split = rows.reshape(n_ord, 2, 4, -1)
        return jnp.where(core == 1, split[:, ::-1], split).reshape(rows.shape)

    fraction = in_order(jnp.repeat(orders.astype(jnp.float32) / LMAX, 2)[:, None])
    wave = in_order(wave) / math.sqrt(BAND)
    turned = wave.reshape(BAND, 2, meridians)
    turned = jnp.stack([turned[:, 1], -turned[:, 0]], axis=1).reshape(2 * BAND, meridians)

    def to_grid(rows, table):
        return jnp.einsum("kfr,kj->frj", rows, table, precision=lax.Precision.HIGH)

    first, slope, laplace = spectra
    p = to_grid(slope, wave)
    q = to_grid(first / sine, fraction * turned)
    t = -to_grid(first / (sine * sine), fraction * fraction * wave)
    r = -t - to_grid(laplace, wave)
    s = to_grid(slope / sine, fraction * turned)
    return surface(p, q, r, s, t)


def solution(mesh):
    return jax.shard_map(
        on_device,
        mesh=mesh,
        in_specs=(P(None, "lat", "ord"), P("ord", "lat", None), P(), P()),
        out_specs=(P(None, "lat", "ord"), P(None, "lat", "ord")),
        check_vma=False,
    )
```

time: 387 us -> 105 us (0.27); the launches traced: 380 us -> 104 us
  waiting for transfers between devices: 275 us -> 32.3 us
  blocking collectives: 54.8 us -> 0 us
  starting transfers between devices: 0.08 us -> 20.5 us
  between operations: 14.9 us -> 4.87 us
  local copies, waits for them, and re-layouts: 4.51 us -> 11.1 us
    unnamed x3 -> x0, waiting for transfers between devices: 159 us -> none
    psum x1 -> x0, waiting for transfers between devices: 116 us -> none  [on_device(): coeffs = lax.psum(partial_value, 'lat')]
    all_gather x1 -> x0, blocking collectives: 54.8 us -> none  [on_device(): lax.all_gather(spectral, 'ord', axis=0, tiled=True)]
    all_to_all x0 -> x2, starting transfers between devices: none -> 17.5 us  [the longest x1 11.2 us: on_device(): lax.all_to_all(product.reshape(n_ord, 8, layers * rings), 'ord', 0, 0, ti...]
    ppermute x0 -> x5, waiting for transfers between devices: none -> 16.3 us  [swap(): lax.ppermute(value, axis, [(k, k ^ mask) for k in range(lax.axis_size(axi...]
    all_to_all x0 -> x2, waiting for transfers between devices: none -> 16 us  [the longest x1 12.4 us: on_device(): lax.all_to_all(jnp.broadcast_to(fields[None], (n_ord,) + fields.shape), '...]
    dot_general x4 -> x10, matrix products: 20.4 us -> 24.1 us  [the longest x5 9.81 us: to_grid(): return jnp.einsum('kfr,kj->frj', rows, table, precision=lax.Precision.HIGH)]
  transfers between devices with their start and end apart: 2 -> 7, of which waited for: 2 -> 5; matrix products, arithmetic and copies ran while one was open for 0% -> 19% of each run, Pallas kernels for 0% -> 0%
where the time goes in v1:
time: 105 us; the launch traced here: 104 us
  waiting for transfers between devices  32.3 us (31%)
  matrix products  24.1 us (23%)
  starting transfers between devices  20.5 us (20%)
  other arithmetic  11.5 us (11%)
  local copies, waits for them, and re-layouts  11.1 us (11%)
  between operations  4.87 us (5%)
    ppermute x5, waiting for transfers between devices, swap(): lax.ppermute(value, axis, [(k, k ^ mask) for k in range(lax.axis_size(axi...  16.3 us
    all_to_all x1, waiting for transfers between devices, on_device(): lax.all_to_all(jnp.broadcast_to(fields[None], (n_ord,) + fields.shape), '...  12.4 us
    all_to_all x1, starting transfers between devices, on_device(): lax.all_to_all(product.reshape(n_ord, 8, layers * rings), 'ord', 0, 0, ti...  11.2 us
    dot_general x5, matrix products, to_grid(): return jnp.einsum('kfr,kj->frj', rows, table, precision=lax.Precision.HIGH)  9.81 us
    dot_general x2, matrix products, synthesis(): jnp.einsum('rk,ujxfk->juxfr', table, weights, preferred_element_type=jnp....  7.45 us
    all_to_all x1, starting transfers between devices, on_device(): lax.all_to_all(jnp.broadcast_to(fields[None], (n_ord,) + fields.shape), '...  6.26 us
    dot_general x2, matrix products, analysis(): jnp.einsum('uxfr,rk->uxfk', rows, table, preferred_element_type=jnp.float32)  5.71 us
    all_to_all x1, waiting for transfers between devices, on_device(): lax.all_to_all(product.reshape(n_ord, 8, layers * rings), 'ord', 0, 0, ti...  3.61 us
  transfers between devices with their start and end apart: 7, of which 5 were waited for; matrix products, arithmetic and copies ran while one was open for 19% of the time, Pallas kernels for 0%

profile of v1, /device:TPU:6, one launch (start us, length us, event | category | flops | bytes accessed | tf_op | source)
XLA Modules:
  0.0 104.4 jit_solution(3545404883038200085)
XLA Ops:
  0.7 0.9 select_reduce_fusion
  1.6 1.5 %fusion.45 = (f32[64,1,1350]{2,0,1:T(8,128)S(1)}, f32[64,1,1350]{2,0,1:T(8,128)S(1)}) fusion(s32[1350]{0:T(1024)S(1)} %iota_add_fusion.1, s32[64]{0:T(128)S(1)} %select_reduce_fusion), kind=kLoop, calls=%fused_computation.59 | loop fusion | flops 864000 | bytes 696856 | tf_op jit(solution)/shard_map/cos | solution.py:75
  3.2 0.4 copy.98
  3.6 0.3 convert_element_type.138
  3.9 1.1 %fusion.84 = f32[16,8,384]{2,1,0:T(8,128)} fusion(bf16[16,8,1350]{2,1,0:T(8,128)(2,1)S(1)} %convert_element_type.138, bf16[384,1350,1]{1,0,2:T(8,128)(2,1)S(1)} %bitcast.102), kind=kOutput, calls=%fused_computation.142 | convolution fusion | flops 132710400 | bytes 1579008 | tf_op jit(solution)/shard_map/dot_general | solution.py:76
  5.0 11.2 %all-to-all-start = ((f32[16,8,384]{2,1,0:T(8,128)}), f32[16,8,384]{2,1,0:T(8,128)S(1)}, u32[]{:S(2)}, u32[]{:S(2)}) async-start(f32[16,8,384]{2,1,0:T(8,128)} %fusion.84), calls=%async_computation | async-start | bytes 393216 | tf_op jit(solution)/shard_map/all_to_all | solution.py:82
  16.3 0.6 fusion.83
  19.4 0.7 fusion.57
  20.1 0.1 div.129
  20.3 0.6 fusion.61
  22.2 0.1 copy.119
  22.3 0.6 copy.109
  22.8 0.6 reshape_reshape.3
  23.5 0.6 fusion.59
  24.1 3.6 %all-to-all-done = f32[16,8,384]{2,1,0:T(8,128)S(1)} async-done(((f32[16,8,384]{2,1,0:T(8,128)}), f32[16,8,384]{2,1,0:T(8,128)S(1)}, u32[]{:S(2)}, u32[]{:S(2)}) %all-to-all-start) | async-done | bytes 196640 | tf_op jit(solution)/shard_map/all_to_all | solution.py:82
  27.9 2.9 %fusion.4 = f32[2,2,2,10802]{3,2,1,0:T(2,128)S(1)} fusion(bf16[2,192,10802]{2,1,0:T(8,128)(2,1)} %param.5, s32[]{:T(128)S(6)} %select_n.218, bf16[2,2,2,2,192]{4,3,2,1,0:T(2,128)(2,1)S(1)} %multiply_convert_fusion.1), kind=kOutput, calls=%fused_computation.4 | convolution fusion | flops 33183744 | bytes 4528704 | tf_op jit(solution)/shard_map/uxfr,rk->uxfk/dot_general | solution.py:95
  30.8 0.2 squeeze.51
  30.9 0.2 squeeze.50
  31.2 0.1 collective-permute-start
  31.3 2.9 %fusion.6 = f32[2,2,2,10802]{3,2,1,0:T(2,128)S(1)} fusion(bf16[2,192,10802]{2,1,0:T(8,128)(2,1)} %param.5, s32[]{:T(128)S(6)} %select_n.214, bf16[2,2,2,2,192]{4,3,2,1,0:T(2,128)(2,1)S(1)} %multiply_convert_fusion.1), kind=kOutput, calls=%fused_computation.6 | convolution fusion | flops 33183744 | bytes 4528704 | tf_op jit(solution)/shard_map/uxfr,rk->uxfk/dot_general | solution.py:95
  34.2 0.2 squeeze.46
  34.3 0.2 squeeze.45
  34.6 0.9 collective-permute-start.1
  35.5 0.7 fusion.55
  36.2 5.3 %collective-permute-done.1 = f32[4,10802]{1,0:T(4,128)S(1)} collective-permute-done((f32[4,10802]{1,0:T(4,128)S(1)}, f32[4,10802]{1,0:T(4,128)S(1)}, u32[]{:S(2)}, u32[]{:S(2)}) %collective-permute-start.1) | collective-permute-done | bytes 172864 | tf_op jit(solution)/shard_map/ppermute | solution.py:60
  41.5 0.6 collective-permute-start.2
  42.1 6.8 %collective-permute-done.2 = f32[4,10802]{1,0:T(4,128)S(1)} collective-permute-done((f32[4,10802]{1,0:T(4,128)S(1)}, f32[4,10802]{1,0:T(4,128)S(1)}, u32[]{:S(2)}, u32[]{:S(2)}) %collective-permute-start.2) | collective-permute-done | bytes 172864 | tf_op jit(solution)/shard_map/ppermute | solution.py:60
  48.9 1.2 %collective-permute-start.3 = (f32[4,10802]{1,0:T(4,128)S(1)}, f32[4,10802]{1,0:T(4,128)S(1)}, u32[]{:S(2)}, u32[]{:S(2)}) collective-permute-start(f32[4,10802]{1,0:T(4,128)S(1)} %add.248), channel_id=1, source_target_pairs={{0,128},{16,144},{32,160},{48,176},{64,192},{80,208},{96,224},{112... | collective-permute-start | bytes 518504 | tf_op jit(solution)/shard_map/ppermute | solution.py:60
  50.2 4.3 %collective-permute-done.3 = f32[4,10802]{1,0:T(4,128)S(1)} collective-permute-done((f32[4,10802]{1,0:T(4,128)S(1)}, f32[4,10802]{1,0:T(4,128)S(1)}, u32[]{:S(2)}, u32[]{:S(2)}) %collective-permute-start.3) | collective-permute-done | bytes 172864 | tf_op jit(solution)/shard_map/ppermute | solution.py:60
  54.5 0.1 reshape.621
  54.6 0.1 reshape.620
  54.8 0.3 collective-permute-start.4
  55.1 0.2 slice.80
  55.3 0.1 multiply_bitcast_fusion.4
  55.4 0.2 multiply_bitcast_fusion.6
  55.6 0.5 select_convert_fusion.2
  56.1 0.1 copy.103
  56.3 0.2 fusion.38
  56.5 3.7 %fusion.18 = f32[4,2,2,2,192]{4,0,3,2,1:T(4,128)S(1)} fusion(bf16[2,192,10802]{2,1,0:T(8,128)(2,1)} %param.5, s32[]{:T(128)S(6)} %select_n.214, bf16[1,4,2,2,10802]{4,1,3,2,0:T(4,128)(2,1)S(1)} %fusion.38, bf16[1,4,2,2,10802]{4,1,3,2,0:T(4,128)(2,1)S(1)} %copy.103), kind=kOutput, calls=%fused_computation.22 | convolution fusion | flops 134117632 | bytes 4893828 | tf_op jit(solution)/shard_map/rk,ujxfk->juxfr/dot_general | solution.py:108
  60.3 0.1 reshape.623
  60.4 0.2 slice.85
  60.7 0.1 select_multiply_fusion
  60.9 0.2 reshape.622
  61.1 0.3 multiply_bitcast_fusion.2
  61.4 1.0 select_convert_fusion.1
  62.4 3.7 %fusion.21 = f32[4,2,2,2,192]{4,0,3,2,1:T(4,128)S(1)} fusion(bf16[2,192,10802]{2,1,0:T(8,128)(2,1)} %param.5, s32[]{:T(128)S(6)} %select_n.218, bf16[1,4,2,2,10802]{4,1,3,2,0:T(4,128)(2,1)S(1)} %get-tuple-element.16, bf16[1,4,2,2,10802]{4,1,3,2,0:T(4,128)(2,1)S(1)} %get-tuple-element.15), kind=kOutput, calls=%fused_computation.23 | convolution fusion | flops 134117632 | bytes 4893828 | tf_op jit(solution)/shard_map/rk,ujxfk->juxfr/dot_general | solution.py:108
  66.4 0.9 broadcast_in_dim.109
  67.3 6.3 %all-to-all-start.1 = ((f32[16,24,384]{2,1,0:T(8,128)}), f32[16,24,384]{2,1,0:T(8,128)}, u32[]{:S(2)}, u32[]{:S(2)}) async-start(f32[16,24,384]{2,1,0:T(8,128)} %broadcast_in_dim.109), calls=%async_computation.1 | async-start | bytes 1179648 | tf_op jit(solution)/shard_map/all_to_all | solution.py:113
  73.5 0.3 fusion.39
  73.8 0.2 div.123
  74.1 1.4 %div.130 = f32[64,2,1350]{2,1,0:T(2,128)} reshape(f32[16,2,4,1350]{3,2,1,0:T(4,128)S(1)} %get-tuple-element.10) | data formatting | bytes 1382400 | tf_op jit(solution)/shard_map/div | solution.py:123
  75.5 0.1 copy.115
  75.7 1.1 %mul.438 = f32[128,1350]{1,0:T(8,128)} reshape(f32[16,2,4,1350]{3,2,1,0:T(4,128)S(1)} %get-tuple-element.9) | data formatting | bytes 1382400 | tf_op jit(solution)/shard_map/mul | solution.py:133
  76.8 2.2 %fusion.78 = (f32[64,1,1350]{2,1,0:T(1,128)S(1)}, f32[64,1,1350]{2,1,0:T(1,128)S(1)}) fusion(f32[64,2,1350]{2,1,0:T(2,128)} %div.130), kind=kLoop, calls=%fused_computation.136 | loop fusion | flops 86400 | bytes 1382400 | tf_op jit(solution)/shard_map/slice | solution.py:125
  79.0 0.7 maximum_multiply_fusion
  79.7 0.5 mul.430
  80.2 12.4 %all-to-all-done.1 = f32[16,24,384]{2,1,0:T(8,128)} async-done(((f32[16,24,384]{2,1,0:T(8,128)}), f32[16,24,384]{2,1,0:T(8,128)}, u32[]{:S(2)}, u32[]{:S(2)}) %all-to-all-start.1) | async-done | bytes 589856 | tf_op jit(solution)/shard_map/all_to_all | solution.py:113
  92.6 1.6 %reshape.624 = f32[16,3,8,2,192]{4,3,2,1,0:T(2,128)S(1)} reshape(f32[16,24,384]{2,1,0:T(8,128)} %all-to-all-done.1) | data formatting | bytes 1179648 | tf_op jit(solution)/shard_map/reshape | solution.py:115
  94.2 0.3 fusion.77
  94.5 1.1 %fusion.30 = f32[2,192,1350]{2,1,0:T(8,128)S(1)} fusion(f32[128,1350]{1,0:T(8,128)S(1)} %div.123, f32[16,1,8,2,192]{4,3,2,1,0:T(2,128)S(1)} %get-tuple-element.7), kind=kOutput, calls=%fused_computation.33 | convolution fusion | flops 398131200 | bytes 2961408 | tf_op jit(solution)/shard_map/kfr,kj->frj/dot_general | solution.py:128
  95.7 1.1 %fusion.24 = f32[2,192,1350]{2,1,0:T(8,128)S(1)} fusion(f32[128,1350]{1,0:T(8,128)S(1)} %copy-done.1, f32[16,1,8,2,192]{4,2,3,1,0:T(8,128)S(1)} %get-tuple-element.21), kind=kOutput, calls=%fused_computation.27 | convolution fusion | flops 398131200 | bytes 2961408 | tf_op jit(solution)/shard_map/kfr,kj->frj/dot_general | solution.py:128
  96.8 2.7 %sqrt_convert_fusion = (bf16[2,192,1350]{2,1,0:T(8,128)(2,1)}, f32[2,192,1350]{2,1,0:T(8,128)S(1)}) fusion(f32[2,192,1350]{2,1,0:T(8,128)S(1)} %fusion.30, f32[128,1350]{1,0:T(8,128)S(1)} %mul.430, f32[16,1,8,2,192]{4,2,3,1,0:T(8,128)S(1)} %get-tuple-element.22), kind=kOutput, calls=%fused_computation.21 | convolution fusion | flops 400723200 | bytes 6071808 | tf_op jit(solution)/shard_map/kfr,kj->frj/dot_general | solution.py:128
  99.5 1.4 %fusion.13 = f32[2,192,1350]{2,1,0:T(8,128)S(1)} fusion(f32[2,192,1350]{2,1,0:T(8,128)S(1)} %fusion.24, f32[2,192,1350]{2,1,0:T(8,128)S(1)} %get-tuple-element.41, f32[128,1350]{1,0:T(8,128)S(1)} %div.123, f32[128,2,192]{2,1,0:T(2,128)S(1)} %bitcast.103), kind=kOutput, calls=%fused_computation.15 | convolution fusion | flops 400204800 | bytes 7108608 | tf_op jit(solution)/shard_map/kfr,kj->frj/dot_general | solution.py:128
  100.9 3.5 %fusion.16 = bf16[2,192,1350]{2,1,0:T(8,128)(2,1)} fusion(f32[2,192,1350]{2,1,0:T(8,128)S(1)} %fusion.13, f32[2,192,1350]{2,1,0:T(8,128)S(1)} %fusion.24, f32[2,192,1350]{2,1,0:T(8,128)S(1)} %get-tuple-element.41, f32[2,192,1350]{2,1,0:T(8,128)S(1)} %fusion.30, f32[128,1350]{1,0:T(8,128)S(1)} %mul.430, f32[16,1,8,2,192]{4,2,3,1,0:T(8,128)S(1)} %get-tuple-element.37), kind=kOutput, calls=%fused_computation.18 | convolution fusion | flops 405907200 | bytes 10219008 | tf_op jit(solution)/shard_map/kfr,kj->frj/dot_general | solution.py:128
  (39 shorter events, 1.4 us)
Async XLA Ops:
  0.6 3.3 %copy-start = (bf16[2,192,1350]{2,1,0:T(8,128)(2,1)S(1)}, bf16[2,192,1350]{2,1,0:T(8,128)(2,1)}, u32[]{:S(2)}) copy-start(bf16[2,192,1350]{2,1,0:T(8,128)(2,1)} %param.4) | copy-start | bytes 3110404
  5.0 22.7 %all-to-all-start = ((f32[16,8,384]{2,1,0:T(8,128)}), f32[16,8,384]{2,1,0:T(8,128)S(1)}, u32[]{:S(2)}, u32[]{:S(2)}) async-start(f32[16,8,384]{2,1,0:T(8,128)} %fusion.84), calls=%async_computation | async-start | bytes 393216 | tf_op jit(solution)/shard_map/all_to_all | solution.py:82
  31.2 3.3 %collective-permute-start = (f32[4,10802]{1,0:T(4,128)S(1)}, f32[4,10802]{1,0:T(4,128)S(1)}, u32[]{:S(2)}, u32[]{:S(2)}) collective-permute-start(f32[4,10802]{1,0:T(4,128)S(1)} %broadcast_select_fusion), channel_id=1, source_target_pairs={{0,16},{16,0},{32,48},{48,32},{64,80},{80,64},{96,112},{112,96},{1... | collective-permute-start | bytes 518504 | tf_op jit(solution)/shard_map/ppermute | solution.py:60
  34.6 6.9 %collective-permute-start.1 = (f32[4,10802]{1,0:T(4,128)S(1)}, f32[4,10802]{1,0:T(4,128)S(1)}, u32[]{:S(2)}, u32[]{:S(2)}) collective-permute-start(f32[4,10802]{1,0:T(4,128)S(1)} %select_add_fusion), channel_id=1, source_target_pairs={{0,32},{16,48},{32,0},{48,16},{64,96},{80,112},{96,64},{112,80},{1... | collective-permute-start | bytes 518504 | tf_op jit(solution)/shard_map/ppermute | solution.py:60
  41.5 7.3 %collective-permute-start.2 = (f32[4,10802]{1,0:T(4,128)S(1)}, f32[4,10802]{1,0:T(4,128)S(1)}, u32[]{:S(2)}, u32[]{:S(2)}) collective-permute-start(f32[4,10802]{1,0:T(4,128)S(1)} %add.247), channel_id=1, source_target_pairs={{0,96},{16,112},{32,64},{48,80},{64,32},{80,48},{96,0},{112,16},{1... | collective-permute-start | bytes 518504 | tf_op jit(solution)/shard_map/ppermute | solution.py:60
  48.9 5.5 %collective-permute-start.3 = (f32[4,10802]{1,0:T(4,128)S(1)}, f32[4,10802]{1,0:T(4,128)S(1)}, u32[]{:S(2)}, u32[]{:S(2)}) collective-permute-start(f32[4,10802]{1,0:T(4,128)S(1)} %add.248), channel_id=1, source_target_pairs={{0,128},{16,144},{32,160},{48,176},{64,192},{80,208},{96,224},{112... | collective-permute-start | bytes 518504 | tf_op jit(solution)/shard_map/ppermute | solution.py:60
  54.8 5.5 %collective-permute-start.4 = (f32[4,10802]{1,0:T(4,128)S(1)}, f32[4,10802]{1,0:T(4,128)S(1)}, u32[]{:S(2)}, u32[]{:S(2)}) collective-permute-start(f32[4,10802]{1,0:T(4,128)S(1)} %add.249), channel_id=1, source_target_pairs={{0,16},{16,0},{32,48},{48,32},{64,80},{80,64},{96,112},{112,96},{1... | collective-permute-start | bytes 518504 | tf_op jit(solution)/shard_map/ppermute | solution.py:60
  67.3 25.3 %all-to-all-start.1 = ((f32[16,24,384]{2,1,0:T(8,128)}), f32[16,24,384]{2,1,0:T(8,128)}, u32[]{:S(2)}, u32[]{:S(2)}) async-start(f32[16,24,384]{2,1,0:T(8,128)} %broadcast_in_dim.109), calls=%async_computation.1 | async-start | bytes 1179648 | tf_op jit(solution)/shard_map/all_to_all | solution.py:113
  94.5 1.2 %copy-start.1 = (f32[128,1350]{1,0:T(8,128)S(1)}, f32[128,1350]{1,0:T(8,128)}, u32[]{:S(2)}) copy-start(f32[128,1350]{1,0:T(8,128)} %mul.438) | copy-start | bytes 2073604

commit v2 on v1

v2 whole, which is shorter than its diff:
```python
import functools
import math

import jax
import jax.numpy as jnp
from jax import lax
from jax.experimental import pallas as pl
from jax.experimental.pallas import tpu as pltpu
from jax.sharding import PartitionSpec as P

LMAX = 10800
MERIDIAN_AMOUNT = 21600
BAND = 64
NLAT = 10801
PACK = 10802
PADDED = 10880
WHOLE = 10752
RINGS = 192
MERIDIANS = 1350
ROWS = 2 * BAND

SINE_SERIES = tuple(
    (-1.0) ** n * (2.0 * math.pi) ** (2 * n + 1) / math.factorial(2 * n + 1) for n in range(8)
)


def swap(value, axis, mask):
    return lax.ppermute(value, axis, [(k, k ^ mask) for k in range(lax.axis_size(axis))])


def row_orders(modes, mapping, slot):
    lane = lax.broadcasted_iota(jnp.int32, (slot.shape[0], BAND), 1)
    entry = jnp.sum(
        jnp.where(lane == slot, mapping.astype(jnp.float32), 0.0), axis=1, keepdims=True
    ).astype(jnp.int32)
    return jnp.sum(
        jnp.where(lane == entry, modes.astype(jnp.float32), 0.0), axis=1, keepdims=True
    ).astype(jnp.int32)


def sine_turns(v):
    square = v * v
    total = SINE_SERIES[-1]
    for coefficient in SINE_SERIES[-2::-1]:
        total = total * square + coefficient
    return v * total


def cosine_of(orders, quarter, first):
    longitude = first + lax.broadcasted_iota(jnp.int32, (1, MERIDIANS), 1)
    product = orders * longitude
    cycles = (product.astype(jnp.float32) * (1.0 / MERIDIAN_AMOUNT)).astype(jnp.int32)
    turns = (product - cycles * MERIDIAN_AMOUNT + quarter * (MERIDIAN_AMOUNT // 4)).astype(
        jnp.float32
    ) * (1.0 / MERIDIAN_AMOUNT)
    turns = turns - jnp.round(turns)
    return sine_turns(0.25 - jnp.abs(turns))


def prepare_kernel(
    modes_ref,
    mapping_ref,
    table_ref,
    wave_ref,
    info_ref,
    orders_ref,
    held_ref,
    small_ref,
    sems,
    table_sems,
):
    copies = [
        pltpu.make_async_copy(modes_ref, small_ref.at[0], sems.at[0]),
        pltpu.make_async_copy(mapping_ref, small_ref.at[1], sems.at[1]),
    ]
    for copy in copies:
        copy.start()
    table_copies = []
    for pair in range(2):
        for block in range(4):
            rows = pl.ds(block * (RINGS // 4), RINGS // 4)
            copy = pltpu.make_async_copy(
                table_ref.at[pair, rows, :], held_ref.at[pair, rows, :], table_sems.at[pair * 4 + block]
            )
            copy.start()
            table_copies.append(copy)
    ord_index, lat_index = lax.axis_index("ord"), lax.axis_index("lat")
    core = lat_index % 2
    copies[0].wait()
    copies[1].wait()
    modes, mapping = small_ref[0], small_ref[1]
    row = lax.broadcasted_iota(jnp.int32, (ROWS, 1), 0)
    wave = cosine_of(row_orders(modes, mapping, row // 2), row % 2, ord_index * MERIDIANS)
    wave_ref[...] = (wave * (1.0 / math.sqrt(MERIDIAN_AMOUNT))).astype(jnp.bfloat16)

    row = lax.broadcasted_iota(jnp.int32, (8, 1), 0)
    slot = ord_index * 4 + (core + row) % 2 * 2
    first_orders = row_orders(modes, mapping, slot).astype(jnp.float32)
    lane = lax.broadcasted_iota(jnp.int32, (8, 2 * RINGS), 1)
    cycle = lat_index * RINGS + jnp.where(lane >= RINGS, lane - RINGS, lane)
    v = ((NLAT - 16 * RINGS * 1.0 + 1.0) * -0.5 + 0.5 * NLAT - cycle.astype(jnp.float32)) * (0.5 / NLAT)
    sine, cosine = sine_turns(0.25 - jnp.abs(v)), sine_turns(v)
    info_ref[...] = jnp.where(row == 0, sine, jnp.where(row == 1, cosine, first_orders))

    row = lax.broadcasted_iota(jnp.int32, (ROWS, 1), 0)
    slot = (row // 8) * 4 + ((row // 4) % 2 + core) % 2 * 2 + (row // 2) % 2
    orders_ref[...] = jnp.broadcast_to(row_orders(modes, mapping, slot), (ROWS, 128))

    for copy in table_copies:
        copy.wait()


def forward_kernel(wave_ref, grids_ref, out_ref):
    lines = grids_ref[...].reshape(2 * RINGS, MERIDIANS)
    out_ref[...] = lax.dot_general(
        wave_ref[...], lines, (((1,), (1,)), ((), ())), preferred_element_type=jnp.float32
    )


def table_kernel(orders_ref, after_ref, out_ref):
    row = lax.broadcasted_iota(jnp.int32, (ROWS, 1), 0)
    first = lax.axis_index("ord") * MERIDIANS
    orders = orders_ref[:, 0:1]
    fraction = orders.astype(jnp.float32) * (1.0 / LMAX)
    wave = cosine_of(orders, row % 2, first) * (1.0 / math.sqrt(BAND))
    turned = cosine_of(orders, row % 2 + 1, first) * (1.0 / math.sqrt(BAND))
    for index, table in enumerate((wave, fraction * turned, fraction * fraction * wave)):
        high = table.astype(jnp.bfloat16)
        low = (table - high.astype(jnp.float32)).astype(jnp.bfloat16)
        out_ref[index, 0:ROWS, :] = high
        out_ref[index, ROWS : 2 * ROWS, :] = high
        out_ref[index, 2 * ROWS :, :] = low


def analysis_kernel(which, parts_ref, info_ref, table_ref, out_ref):
    pair = (lax.axis_index("lat") + which) % 2
    first_len = LMAX + 1 - info_ref[2 + which : 3 + which, 0:1].astype(jnp.int32)
    total = parts_ref[0]
    for index in range(1, parts_ref.shape[0]):
        total = total + parts_ref[index]
    weighted = total * (info_ref[0:1, :] * (1.0 / math.sqrt(16 * RINGS)))
    mine = jnp.where(pair == 1, weighted[4:8], weighted[0:4])
    left, right = mine[:, :RINGS], mine[:, RINGS:]
    rows = jnp.concatenate([left[0:2], right[0:2], left[2:4], right[2:4]], axis=0).astype(
        jnp.bfloat16
    )
    step = 1536
    for start in range(0, PACK, step):
        size = min(step, PACK - start)
        product = jnp.dot(
            rows, table_ref[pair, :, start : start + size], preferred_element_type=jnp.float32
        )
        position = start + lax.broadcasted_iota(jnp.int32, (4, size), 1)
        out_ref[:, start : start + size] = jnp.where(
            position >= first_len, product[4:8], product[0:4]
        )
    out_ref[:, PACK:] = jnp.zeros((4, PADDED - PACK), jnp.float32)


def add_kernel(first_ref, second_ref, third_ref, fourth_ref, _, out_ref):
    out_ref[...] = (first_ref[...] + second_ref[...]) + (third_ref[...] + fourth_ref[...])


def synthesis_kernel(which, coeffs_ref, info_ref, table_ref, *rest):
    pair = (lax.axis_index("lat") + which) % 2
    order = info_ref[2 + which : 3 + which, 0:1].astype(jnp.int32)
    row = lax.broadcasted_iota(jnp.int32, (8, 1), 0)
    upper = (row // 2) % 2 == 1
    first_len = LMAX + 1 - order
    base = jnp.where(upper, -1, order)
    own_order = jnp.where(upper, LMAX - order, order)
    length = jnp.where(upper, order + 1, first_len).astype(jnp.float32)
    begin = jnp.where(upper, first_len, 0)
    end = jnp.where(upper, PACK, first_len)
    scaling = 1.0 / jnp.sqrt(length)
    step = 1536
    synth = jnp.zeros((32, RINGS), jnp.float32)
    for start in range(0, PADDED, step):
        size = min(step, PADDED - start)
        own = coeffs_ref[:, start : start + size]
        if start + size < PADDED:
            ahead = coeffs_ref[:, start + size : start + size + 128]
        else:
            ahead = jnp.zeros((4, 128), jnp.float32)
        wide = jnp.concatenate([own, ahead], axis=1)
        after = pltpu.roll(wide, size + 127, axis=1)[:, :size]
        spread = [jnp.concatenate([a[0:2], a[0:2], a[2:4], a[2:4]], axis=0) for a in (own, after)]
        position = start + lax.broadcasted_iota(jnp.int32, (8, size), 1)
        inside = (position >= begin) & (position < end)
        degree = (base + position).astype(jnp.float32)
        plain = jnp.where(inside, scaling, 0.0)
        sloped = plain * (degree * (1.0 / LMAX))
        ahead_factor = jnp.where(
            inside & (position < end - 1),
            (degree + (1.0 + own_order.astype(jnp.float32))) * (scaling * (1.0 / LMAX)),
            0.0,
        )
        curved = sloped * ((degree + 1.0) * (1.0 / LMAX))
        weights = jnp.concatenate(
            [spread[0] * plain, spread[0] * sloped, spread[1] * ahead_factor, spread[0] * curved],
            axis=0,
        ).astype(jnp.bfloat16)
        held = min(size, PACK - start)
        synth = synth + lax.dot_general(
            weights[:, :held],
            table_ref[pair, :, start : start + held],
            (((1,), (1,)), ((), ())),
            preferred_element_type=jnp.float32,
        )
    sine, cosine = info_ref[0:1, :RINGS], info_ref[1:2, :RINGS]
    fields = [synth[0:8], (cosine * synth[8:16] - synth[16:24]) / sine, synth[24:32]]
    fields = [jnp.concatenate([a[0:4], a[4:8]], axis=1) for a in fields]
    if which == 0:
        (out_ref,) = rest
        for index in range(3):
            out_ref[4 * index : 4 * index + 4, :] = fields[index]
    else:
        other_ref, _, out_ref = rest
        for index in range(3):
            rows = jnp.concatenate([other_ref[4 * index : 4 * index + 4, :], fields[index]], axis=0)
            for target in range(out_ref.shape[0]):
                out_ref[target, 8 * index : 8 * index + 8, :] = rows


def inverse_kernel(fields_ref, info_ref, table_ref, steep_ref, bend_ref, left_ref):
    @pl.when(pl.program_id(0) == 0)
    def _():
        inverse = (1.0 / info_ref[...]).T[:, 0:1]
        first, slope, laplace = [
            fields_ref[:, 8 * index : 8 * index + 8, :].reshape(ROWS, 2 * RINGS).T for index in range(3)
        ]
        scaled = first * inverse
        half = (0.5 * scaled) * inverse
        for index, rows in enumerate((slope, scaled, half, slope * inverse, 0.5 * laplace)):
            high = rows.astype(jnp.bfloat16)
            low = (rows - high.astype(jnp.float32)).astype(jnp.bfloat16)
            left_ref[index, :, 0:ROWS] = high
            left_ref[index, :, ROWS : 2 * ROWS] = low
            left_ref[index, :, 2 * ROWS :] = high

    chunk = 96
    base = pl.program_id(0) * RINGS
    for start in range(0, RINGS, chunk):
        rows_here = pl.ds(pl.multiple_of(base + start, chunk), chunk)

        def to_grid(rows, table):
            return jnp.dot(
                left_ref[rows, rows_here, :], table_ref[table], preferred_element_type=jnp.float32
            )

        p = to_grid(0, 0)
        q = to_grid(1, 1)
        half_t = to_grid(2, 2)
        s = to_grid(3, 1)
        half_l = to_grid(4, 0)
        p2, q2 = p * p, q * q
        outer = 1.0 + q2
        area = outer + p2
        root = lax.rsqrt(area)
        steep_ref[0, start : start + chunk, :] = (area * root).astype(jnp.bfloat16)
        top = (q2 - p2) * half_t - outer * half_l - (p * q) * s
        bend_ref[0, start : start + chunk, :] = (top * (root * root * root)).astype(jnp.bfloat16)


VMEM = pl.BlockSpec(memory_space=pltpu.VMEM)
SMEM = pl.BlockSpec(memory_space=pltpu.SMEM)


ANY = pl.BlockSpec(memory_space=pl.ANY)


COST = pl.CostEstimate(flops=1000000000, bytes_accessed=4000000, transcendentals=0)


def call(kernel, shape, dtype, in_specs, limit=24, **kwargs):
    return pl.pallas_call(
        kernel,
        out_shape=jax.ShapeDtypeStruct(shape, dtype),
        in_specs=in_specs,
        out_specs=VMEM,
        compiler_params=pltpu.CompilerParams(vmem_limit_bytes=limit << 20),
        **kwargs,
    )


def on_device(altitude_grids, polynomial_values, span_azimuthal_modes, slot_mapping):
    layers, rings, meridians = altitude_grids.shape
    n_ord = lax.axis_size("ord")
    modes, mapping = span_azimuthal_modes[None, :], slot_mapping[None, :]

    wave, info, orders, held = pl.pallas_call(
        prepare_kernel,
        out_shape=[
            jax.ShapeDtypeStruct((ROWS, meridians), jnp.bfloat16),
            jax.ShapeDtypeStruct((8, layers * rings), jnp.float32),
            jax.ShapeDtypeStruct((ROWS, 128), jnp.int32),
            jax.ShapeDtypeStruct(polynomial_values.shape, jnp.bfloat16),
        ],
        in_specs=[ANY] * 3,
        out_specs=[VMEM] * 4,
        scratch_shapes=[
            pltpu.VMEM((2, 1, BAND), jnp.int32),
            pltpu.SemaphoreType.DMA((2,)),
            pltpu.SemaphoreType.DMA((8,)),
        ],
        compiler_params=pltpu.CompilerParams(vmem_limit_bytes=40 << 20),
    )(modes, mapping, polynomial_values)
    product = call(forward_kernel, (ROWS, layers * rings), jnp.float32, [VMEM] * 2)(
        wave, altitude_grids
    )
    parts = lax.all_to_all(product.reshape(n_ord, 8, layers * rings), "ord", 0, 0, tiled=True)

    def analysis(which):
        return call(
            functools.partial(analysis_kernel, which), (4, PADDED), jnp.float32, [VMEM] * 3
        )(parts, info, held)

    outgoing = analysis(1)
    other = swap(outgoing, "lat", 1)
    coeffs = analysis(0) + other
    tables = call(table_kernel, (3, 3 * ROWS, meridians), jnp.bfloat16, [VMEM, ANY], cost_estimate=COST)(
        orders, outgoing
    )

    def turn(value, step):
        n = lax.axis_size("lat")
        return lax.ppermute(value, "lat", [(k, k // 8 * 8 + (k + 2 * step) % 8) for k in range(n)])

    received = [turn(coeffs, step) for step in (1, 3, 2)]
    coeffs = call(add_kernel, (4, PADDED), jnp.float32, [VMEM] * 4 + [ANY])(
        coeffs, *received, tables
    )
    coeffs = coeffs + swap(coeffs, "lat", 8)
    other = swap(coeffs, "lat", 1)

    mine = call(
        functools.partial(synthesis_kernel, 0), (12, layers * rings), jnp.float32, [VMEM] * 3
    )(coeffs, info, held)
    fields = call(
        functools.partial(synthesis_kernel, 1),
        (n_ord, 24, layers * rings),
        jnp.float32,
        [VMEM] * 4 + [ANY],
    )(other, info, held, mine, tables)
    everything = lax.all_to_all(fields, "ord", 0, 0, tiled=True)

    block = pl.BlockSpec((1, rings, meridians), lambda f: (f, 0, 0))
    return pl.pallas_call(
        inverse_kernel,
        grid=(layers,),
        out_shape=[jax.ShapeDtypeStruct((layers, rings, meridians), jnp.bfloat16)] * 2,
        in_specs=[VMEM] * 3,
        out_specs=[block, block],
        scratch_shapes=[pltpu.VMEM((5, layers * rings, 3 * ROWS), jnp.bfloat16)],
        compiler_params=pltpu.CompilerParams(vmem_limit_bytes=32 << 20),
    )(everything, info, tables)


def solution(mesh):
    return jax.shard_map(
        on_device,
        mesh=mesh,
        in_specs=(P(None, "lat", "ord"), P("ord", "lat", None), P(), P()),
        out_specs=(P(None, "lat", "ord"), P(None, "lat", "ord")),
        check_vma=False,
    )
```

time: 105 us -> 82.8 us (0.79)
  blocking collectives: 0 us -> 46.7 us
  matrix products: 24.1 us -> 0 us
  waiting for transfers between devices: 32.3 us -> 9.94 us
  Pallas kernels: 0 us -> 17.5 us
  starting transfers between devices: 20.5 us -> 6.29 us
  other arithmetic: 11.5 us -> 0.09 us
  local copies, waits for them, and re-layouts: 11.1 us -> 1.42 us
  between operations: 4.87 us -> 0.76 us
    all_to_all x0 -> x2, blocking collectives: none -> 46.7 us  [the longest x1 24.1 us: on_device(): everything = lax.all_to_all(fields, 'ord', 0, 0, tiled=True)]
    dot_general x10 -> x0, matrix products: 24.1 us -> none  [the longest x5 9.81 us: to_grid(): return jnp.einsum('kfr,kj->frj', rows, table, precision=lax.Precision.HIGH)]
    pallas_call x0 -> x9, Pallas kernels: none -> 17.5 us  [the longest x1 5.85 us: on_device(): pl.pallas_call(inverse_kernel, grid=(layers,), out_shape=[jax.ShapeDtypeS...]
    all_to_all x2 -> x0, starting transfers between devices: 17.5 us -> none  [the longest x1 11.2 us: on_device(): lax.all_to_all(product.reshape(n_ord, 8, layers * rings), 'ord', 0, 0, ti...]
    all_to_all x2 -> x0, waiting for transfers between devices: 16 us -> none  [the longest x1 12.4 us: on_device(): lax.all_to_all(jnp.broadcast_to(fields[None], (n_ord,) + fields.shape), '...]
    ppermute x5 -> x3, waiting for transfers between devices: 16.3 us -> 5.86 us  [swap(): lax.ppermute(value, axis, [(k, k ^ mask) for k in range(lax.axis_size(axi...]
    ppermute x0 -> x3, starting transfers between devices: none -> 4.73 us  [turn(): lax.ppermute(value, 'lat', [(k, k // 8 * 8 + (k + 2 * step) % 8) for k in...]
    ppermute x0 -> x3, waiting for transfers between devices: none -> 4.08 us  [turn(): lax.ppermute(value, 'lat', [(k, k // 8 * 8 + (k + 2 * step) % 8) for k in...]
  transfers between devices with their start and end apart: 7 -> 6, of which waited for: 5 -> 4; matrix products, arithmetic and copies ran while one was open for 19% -> 0% of each run, Pallas kernels for 0% -> 6%
where the time goes in v2:
time: 82.8 us; the launch traced here: 82.7 us
  blocking collectives  46.7 us (56%)
  Pallas kernels  17.5 us (21%)
  waiting for transfers between devices  9.94 us (12%)
  starting transfers between devices  6.29 us (8%)
  local copies, waits for them, and re-layouts  1.42 us (2%)
    all_to_all x1, blocking collectives, on_device(): everything = lax.all_to_all(fields, 'ord', 0, 0, tiled=True)  24.1 us
    all_to_all x1, blocking collectives, on_device(): lax.all_to_all(product.reshape(n_ord, 8, layers * rings), 'ord', 0, 0, ti...  22.5 us
    ppermute x3, waiting for transfers between devices, swap(): lax.ppermute(value, axis, [(k, k ^ mask) for k in range(lax.axis_size(axi...  5.86 us
    pallas_call x1, Pallas kernels, on_device(): pl.pallas_call(inverse_kernel, grid=(layers,), out_shape=[jax.ShapeDtypeS...  5.85 us
    ppermute x3, starting transfers between devices, turn(): lax.ppermute(value, 'lat', [(k, k // 8 * 8 + (k + 2 * step) % 8) for k in...  4.73 us
    ppermute x3, waiting for transfers between devices, turn(): lax.ppermute(value, 'lat', [(k, k // 8 * 8 + (k + 2 * step) % 8) for k in...  4.08 us
    pallas_call x1, Pallas kernels, on_device(): pl.pallas_call(prepare_kernel, out_shape=[jax.ShapeDtypeStruct((ROWS, mer...  3.57 us
    pallas_call x1, Pallas kernels, on_device(): call(table_kernel, (3, 3 * ROWS, meridians), jnp.bfloat16, [VMEM, ANY], c...  2.97 us
  transfers between devices with their start and end apart: 6, of which 4 were waited for; matrix products, arithmetic and copies ran while one was open for 0% of the time, Pallas kernels for 6%

profile of v2, /device:TPU:6, one launch (start us, length us, event | category | flops | bytes accessed | tf_op | source)
XLA Modules:
  0.0 82.7 jit_solution(17291063852676309735)
XLA Ops:
  0.6 0.0 copy-start.1
  0.6 0.6 copy-done.1
  1.3 0.0 copy-start.2
  1.3 0.7 copy-done.2
  1.9 0.0 copy-start
  1.9 3.6 %shard_map.59 = (bf16[128,1350]{1,0:T(8,128)(2,1)S(1)}, f32[8,384]{1,0:T(8,128)S(1)}, s32[128,128]{1,0:T(8,128)S(1)}, bf16[2,192,10802]{2,1,0:T(8,128)(2,1)S(1)}) custom-call(s32[1,64]{1,0:T(1,128)S(1)} %bitcast.4, s32[1,64]{1,0:T(1,128)S(1)} %bitcast.5, bf16[2,192,10802]{2,1,0:T(8,128)(2,1)} %table_ref.1), custom_call_target="tpu_custom_call" | custom-call | tf_op jit(solution)/shard_map/pallas_call | solution.py:291
  5.5 0.1 copy-done
  5.6 0.4 shard_map.60
  6.1 22.5 %all_to_all.10.parts_ref = f32[16,8,384]{2,1,0:T(8,128)S(1)} all-to-all(f32[16,8,384]{2,1,0:T(8,128)S(1)} %bitcast.3), channel_id=1, replica_groups=mesh['lat'=16,'ord'=16] {'ord'}, dimensions={0} | all-to-all | bytes 393216 | tf_op jit(solution)/shard_map/all_to_all | solution.py:311
  28.6 0.7 shard_map.62.after_ref
  29.3 0.1 collective-permute-start
  29.4 0.7 shard_map.61
  30.2 0.7 collective-permute-done
  30.9 1.5 %collective-permute-start.3 = (f32[4,10880]{1,0:T(4,128)S(1)}, f32[4,10880]{1,0:T(4,128)S(1)}, u32[]{:S(2)}, u32[]{:S(2)}) collective-permute-start(f32[4,10880]{1,0:T(4,128)S(1)} %add.6.first_ref), channel_id=1, source_target_pairs={{0,64},{16,80},{32,96},{48,112},{64,0},{80,16},{96,32},{112,48},{1... | collective-permute-start | bytes 522248 | tf_op jit(solution)/shard_map/ppermute | solution.py:327
  32.4 0.0 collective-permute-start.2
  32.4 3.2 %collective-permute-start.1 = (f32[4,10880]{1,0:T(4,128)S(1)}, f32[4,10880]{1,0:T(4,128)S(1)}, u32[]{:S(2)}, u32[]{:S(2)}) collective-permute-start(f32[4,10880]{1,0:T(4,128)S(1)} %add.6.first_ref), channel_id=1, source_target_pairs={{0,32},{16,48},{32,64},{48,80},{64,96},{80,112},{96,0},{112,16},{1... | collective-permute-start | bytes 522248 | tf_op jit(solution)/shard_map/ppermute | solution.py:327
  35.6 3.0 %shard_map.63._.rest_1_.table_ref = bf16[3,384,1350]{2,1,0:T(8,128)(2,1)S(1)} custom-call(s32[128,128]{1,0:T(8,128)S(1)} %get-tuple-element.9.orders_ref, f32[4,10880]{1,0:T(4,128)S(1)} %shard_map.62.after_ref), custom_call_target="tpu_custom_call" | custom-call | flops 1000000000 | bytes 4000000 | tf_op jit(solution)/shard_map/pallas_call | solution.py:321
  38.6 1.2 %collective-permute-done.3.fourth_ref = f32[4,10880]{1,0:T(4,128)S(1)} collective-permute-done((f32[4,10880]{1,0:T(4,128)S(1)}, f32[4,10880]{1,0:T(4,128)S(1)}, u32[]{:S(2)}, u32[]{:S(2)}) %collective-permute-start.3) | collective-permute-done | bytes 174112 | tf_op jit(solution)/shard_map/ppermute | solution.py:327
  39.8 2.9 %collective-permute-done.2.third_ref = f32[4,10880]{1,0:T(4,128)S(1)} collective-permute-done((f32[4,10880]{1,0:T(4,128)S(1)}, f32[4,10880]{1,0:T(4,128)S(1)}, u32[]{:S(2)}, u32[]{:S(2)}) %collective-permute-start.2) | collective-permute-done | bytes 174112 | tf_op jit(solution)/shard_map/ppermute | solution.py:327
  42.7 0.0 collective-permute-done.1.second_ref
  42.7 1.2 %collective-permute-start.4 = (f32[4,10880]{1,0:T(4,128)S(1)}, f32[4,10880]{1,0:T(4,128)S(1)}, u32[]{:S(2)}, u32[]{:S(2)}) collective-permute-start(f32[4,10880]{1,0:T(4,128)S(1)} %shard_map.64), channel_id=1, source_target_pairs={{0,128},{16,144},{32,160},{48,176},{64,192},{80,208},{96,224},{112... | collective-permute-start | bytes 522248 | tf_op jit(solution)/shard_map/ppermute | solution.py:28
  43.9 5.2 %collective-permute-done.4 = f32[4,10880]{1,0:T(4,128)S(1)} collective-permute-done((f32[4,10880]{1,0:T(4,128)S(1)}, f32[4,10880]{1,0:T(4,128)S(1)}, u32[]{:S(2)}, u32[]{:S(2)}) %collective-permute-start.4) | collective-permute-done | bytes 174112 | tf_op jit(solution)/shard_map/ppermute | solution.py:28
  49.2 0.3 collective-permute-start.5
  49.5 1.5 %shard_map.65.rest_0_ = f32[12,384]{1,0:T(8,128)S(1)} custom-call(f32[4,10880]{1,0:T(4,128)S(1)} %add.7.coeffs_ref, f32[8,384]{1,0:T(8,128)S(1)} %get-tuple-element.7.info_ref, bf16[2,192,10802]{2,1,0:T(8,128)(2,1)S(1)} %get-tuple-element.8.table_ref), custom_call_target="tpu_custom_call" | custom-call | tf_op jit(solution)/shard_map/pallas_call | solution.py:336
  51.0 0.0 collective-permute-done.5.coeffs_ref
  51.1 1.6 %shard_map.66 = f32[16,24,384]{2,1,0:T(8,128)S(1)} custom-call(f32[4,10880]{1,0:T(4,128)S(1)} %collective-permute-done.5.coeffs_ref, f32[8,384]{1,0:T(8,128)S(1)} %get-tuple-element.7.info_ref, bf16[2,192,10802]{2,1,0:T(8,128)(2,1)S(1)} %get-tuple-element.8.table_ref, f32[12,384]{1,0:T(8,128)S(1)} %shard_map.65.rest_0_, ...), custom_call_target="tpu_custom_call" | custom-call | tf_op jit(solution)/shard_map/pallas_call | solution.py:339
  52.7 24.1 %all_to_all.11.fields_ref = f32[16,24,384]{2,1,0:T(8,128)S(1)} all-to-all(f32[16,24,384]{2,1,0:T(8,128)S(1)} %shard_map.66), channel_id=1, replica_groups=mesh['lat'=16,'ord'=16] {'ord'}, dimensions={0} | all-to-all | bytes 1179648 | tf_op jit(solution)/shard_map/all_to_all | solution.py:345
  76.8 5.8 %shard_map.67 = (bf16[2,192,1350]{2,1,0:T(8,128)(2,1)}, bf16[2,192,1350]{2,1,0:T(8,128)(2,1)}) custom-call(f32[16,24,384]{2,1,0:T(8,128)S(1)} %all_to_all.11.fields_ref, f32[8,384]{1,0:T(8,128)S(1)} %get-tuple-element.7.info_ref, bf16[3,384,1350]{2,1,0:T(8,128)(2,1)S(1)} %shard_map.63._.rest_1_.table_ref), custom_call_target="tpu_custom_call" | custom-call | tf_op jit(solution)/shard_map/pallas_call | solution.py:348
  (3 shorter events, 0.1 us)
Async XLA Ops:
  0.6 0.7 copy-start.1
  1.3 0.7 copy-start.2
  1.9 3.7 %copy-start = (bf16[2,192,1350]{2,1,0:T(8,128)(2,1)S(1)}, bf16[2,192,1350]{2,1,0:T(8,128)(2,1)}, u32[]{:S(2)}) copy-start(bf16[2,192,1350]{2,1,0:T(8,128)(2,1)} %grids_ref.1) | copy-start | bytes 3110404
  29.3 1.5 %collective-permute-start = (f32[4,10880]{1,0:T(4,128)S(1)}, f32[4,10880]{1,0:T(4,128)S(1)}, u32[]{:S(2)}, u32[]{:S(2)}) collective-permute-start(f32[4,10880]{1,0:T(4,128)S(1)} %shard_map.62.after_ref), channel_id=1, source_target_pairs={{0,16},{16,0},{32,48},{48,32},{64,80},{80,64},{96,112},{112,96},{1... | collective-permute-start | bytes 522248 | tf_op jit(solution)/shard_map/ppermute | solution.py:28
  30.9 8.9 %collective-permute-start.3 = (f32[4,10880]{1,0:T(4,128)S(1)}, f32[4,10880]{1,0:T(4,128)S(1)}, u32[]{:S(2)}, u32[]{:S(2)}) collective-permute-start(f32[4,10880]{1,0:T(4,128)S(1)} %add.6.first_ref), channel_id=1, source_target_pairs={{0,64},{16,80},{32,96},{48,112},{64,0},{80,16},{96,32},{112,48},{1... | collective-permute-start | bytes 522248 | tf_op jit(solution)/shard_map/ppermute | solution.py:327
  32.4 10.3 %collective-permute-start.2 = (f32[4,10880]{1,0:T(4,128)S(1)}, f32[4,10880]{1,0:T(4,128)S(1)}, u32[]{:S(2)}, u32[]{:S(2)}) collective-permute-start(f32[4,10880]{1,0:T(4,128)S(1)} %add.6.first_ref), channel_id=1, source_target_pairs={{0,96},{16,112},{32,0},{48,16},{64,32},{80,48},{96,64},{112,80},{1... | collective-permute-start | bytes 522248 | tf_op jit(solution)/shard_map/ppermute | solution.py:327
  32.4 10.3 %collective-permute-start.1 = (f32[4,10880]{1,0:T(4,128)S(1)}, f32[4,10880]{1,0:T(4,128)S(1)}, u32[]{:S(2)}, u32[]{:S(2)}) collective-permute-start(f32[4,10880]{1,0:T(4,128)S(1)} %add.6.first_ref), channel_id=1, source_target_pairs={{0,32},{16,48},{32,64},{48,80},{64,96},{80,112},{96,0},{112,16},{1... | collective-permute-start | bytes 522248 | tf_op jit(solution)/shard_map/ppermute | solution.py:327
  42.7 6.4 %collective-permute-start.4 = (f32[4,10880]{1,0:T(4,128)S(1)}, f32[4,10880]{1,0:T(4,128)S(1)}, u32[]{:S(2)}, u32[]{:S(2)}) collective-permute-start(f32[4,10880]{1,0:T(4,128)S(1)} %shard_map.64), channel_id=1, source_target_pairs={{0,128},{16,144},{32,160},{48,176},{64,192},{80,208},{96,224},{112... | collective-permute-start | bytes 522248 | tf_op jit(solution)/shard_map/ppermute | solution.py:28
  49.2 1.8 %collective-permute-start.5 = (f32[4,10880]{1,0:T(4,128)S(1)}, f32[4,10880]{1,0:T(4,128)S(1)}, u32[]{:S(2)}, u32[]{:S(2)}) collective-permute-start(f32[4,10880]{1,0:T(4,128)S(1)} %add.7.coeffs_ref), channel_id=1, source_target_pairs={{0,16},{16,0},{32,48},{48,32},{64,80},{80,64},{96,112},{112,96},{1... | collective-permute-start | bytes 522248 | tf_op jit(solution)/shard_map/ppermute | solution.py:28

commit v3 on v2

v3 whole, which is shorter than its diff:
```python
import functools
import math

import jax
import jax.numpy as jnp
from jax import lax
from jax.experimental import pallas as pl
from jax.experimental.pallas import tpu as pltpu
from jax.sharding import PartitionSpec as P

LMAX = 10800
MERIDIAN_AMOUNT = 21600
BAND = 64
NLAT = 10801
PACK = 10802
PADDED = 10880
WHOLE = 10752
RINGS = 192
MERIDIANS = 1350
ROWS = 2 * BAND
STEPS = (0, 2, 1, 3)
MASKS = (0, 3, 1, 2)

SINE_SERIES = tuple(
    (-1.0) ** n * (2.0 * math.pi) ** (2 * n + 1) / math.factorial(2 * n + 1) for n in range(8)
)


def swap(value, axis, mask):
    return lax.ppermute(value, axis, [(k, k ^ mask) for k in range(lax.axis_size(axis))])


def row_orders(modes, mapping, slot):
    lane = lax.broadcasted_iota(jnp.int32, (slot.shape[0], BAND), 1)
    entry = jnp.sum(
        jnp.where(lane == slot, mapping.astype(jnp.float32), 0.0), axis=1, keepdims=True
    ).astype(jnp.int32)
    return jnp.sum(
        jnp.where(lane == entry, modes.astype(jnp.float32), 0.0), axis=1, keepdims=True
    ).astype(jnp.int32)


def sine_turns(v):
    square = v * v
    total = SINE_SERIES[-1]
    for coefficient in SINE_SERIES[-2::-1]:
        total = total * square + coefficient
    return v * total


def cosine_of(orders, quarter, first):
    longitude = first + lax.broadcasted_iota(jnp.int32, (1, MERIDIANS), 1)
    product = orders * longitude
    cycles = (product.astype(jnp.float32) * (1.0 / MERIDIAN_AMOUNT)).astype(jnp.int32)
    turns = (product - cycles * MERIDIAN_AMOUNT + quarter * (MERIDIAN_AMOUNT // 4)).astype(
        jnp.float32
    ) * (1.0 / MERIDIAN_AMOUNT)
    turns = turns - jnp.round(turns)
    return sine_turns(0.25 - jnp.abs(turns))


def entry(values, index):
    return jnp.where(
        index >= 2,
        jnp.where(index == 2, values[2], values[3]),
        jnp.where(index == 0, values[0], values[1]),
    )


def prepare_kernel(small_ref, wave_ref, info_ref, orders_ref):
    ord_index, lat_index = lax.axis_index("ord"), lax.axis_index("lat")
    core = lat_index % 2
    modes, mapping = small_ref[0:1, :], small_ref[1:2, :]
    row = lax.broadcasted_iota(jnp.int32, (ROWS, 1), 0)
    step_y, step_z = entry(STEPS, row // 32), entry(STEPS, (row // 8) % 4)
    target = (ord_index // 4 ^ entry(MASKS, (row // 8) % 4)) * 4 + (ord_index + step_y) % 4
    orders = row_orders(modes, mapping, target * 4 + (row // 2) % 4)
    wave = cosine_of(orders, row % 2, ord_index * MERIDIANS)
    wave_ref[...] = (wave * (1.0 / math.sqrt(MERIDIAN_AMOUNT))).astype(jnp.bfloat16)
    source = (ord_index // 4 + 4 - step_z) % 4 * 4 + (ord_index + 4 - step_y) % 4
    slot = source * 4 + ((row // 4) % 2 + core) % 2 * 2 + (row // 2) % 2
    orders_ref[...] = jnp.broadcast_to(row_orders(modes, mapping, slot), (ROWS, 128))

    row = lax.broadcasted_iota(jnp.int32, (8, 1), 0)
    slot = ord_index * 4 + (core + row) % 2 * 2
    first_orders = row_orders(modes, mapping, slot).astype(jnp.float32)
    lane = lax.broadcasted_iota(jnp.int32, (8, 2 * RINGS), 1)
    cycle = lat_index * RINGS + jnp.where(lane >= RINGS, lane - RINGS, lane)
    v = (0.5 * (16 * RINGS - 1) - cycle.astype(jnp.float32)) * (0.5 / NLAT)
    sine, cosine = sine_turns(0.25 - jnp.abs(v)), sine_turns(v)
    info_ref[...] = jnp.where(row == 0, sine, jnp.where(row == 1, cosine, first_orders))


def forward_kernel(wave_ref, grids_ref, *out_refs):
    lines = grids_ref[...].reshape(2 * RINGS, MERIDIANS)
    product = lax.dot_general(
        wave_ref[...], lines, (((1,), (1,)), ((), ())), preferred_element_type=jnp.float32
    )
    for index, ref in enumerate(out_refs):
        ref[...] = product[32 * index : 32 * index + 32, :]


def hold_kernel(which, table_ref, _, held_ref, sems):
    pair = (lax.axis_index("lat") + which) % 2
    copies = []
    for block in range(4):
        rows = pl.ds(block * (RINGS // 4), RINGS // 4)
        copies.append(
            pltpu.make_async_copy(table_ref.at[pair, rows, :], held_ref.at[rows, :], sems.at[block])
        )
    for copy in copies:
        copy.start()
    for copy in copies:
        copy.wait()


def gather_kernel(first_ref, second_ref, third_ref, fourth_ref, _, keep_ref, send_ref):
    total = (first_ref[...] + second_ref[...]) + (third_ref[...] + fourth_ref[...])
    keep_ref[...], send_ref[...] = total[:16], total[16:]


def halve_kernel(first_ref, second_ref, _, keep_ref, send_ref):
    total = first_ref[...] + second_ref[...]
    keep_ref[...], send_ref[...] = total[:8], total[8:]


def table_kernel(orders_ref, after_ref, out_ref):
    row = lax.broadcasted_iota(jnp.int32, (ROWS, 1), 0)
    first = lax.axis_index("ord") * MERIDIANS
    orders = orders_ref[:, 0:1]
    fraction = orders.astype(jnp.float32) * (1.0 / LMAX)
    wave = cosine_of(orders, row % 2, first) * (1.0 / math.sqrt(BAND))
    turned = cosine_of(orders, row % 2 + 1, first) * (1.0 / math.sqrt(BAND))
    for index, table in enumerate((wave, fraction * turned, fraction * fraction * wave)):
        rounded = table.astype(jnp.bfloat16)
        out_ref[index, 0:ROWS, :] = rounded
        out_ref[index, ROWS:, :] = rounded


def analysis_kernel(which, first_ref, second_ref, info_ref, table_ref, out_ref):
    pair = (lax.axis_index("lat") + which) % 2
    first_len = LMAX + 1 - info_ref[2 + which : 3 + which, 0:1].astype(jnp.int32)
    total = first_ref[...] + second_ref[...]
    weighted = total * (info_ref[0:1, :] * (1.0 / math.sqrt(16 * RINGS)))
    mine = jnp.where(pair == 1, weighted[4:8], weighted[0:4])
    left, right = mine[:, :RINGS], mine[:, RINGS:]
    rows = jnp.concatenate([left[0:2], right[0:2], left[2:4], right[2:4]], axis=0).astype(
        jnp.bfloat16
    )
    step = 1536
    for start in range(0, PACK, step):
        size = min(step, PACK - start)
        product = jnp.dot(
            rows, table_ref[:, start : start + size], preferred_element_type=jnp.float32
        )
        position = start + lax.broadcasted_iota(jnp.int32, (4, size), 1)
        out_ref[:, start : start + size] = jnp.where(
            position >= first_len, product[4:8], product[0:4]
        )
    out_ref[:, PACK:] = jnp.zeros((4, PADDED - PACK), jnp.float32)


def add_kernel(first_ref, second_ref, third_ref, fourth_ref, _, out_ref):
    out_ref[...] = (first_ref[...] + second_ref[...]) + (third_ref[...] + fourth_ref[...])


def synthesis_kernel(which, coeffs_ref, info_ref, table_ref, *rest):
    order = info_ref[2 + which : 3 + which, 0:1].astype(jnp.int32)
    row = lax.broadcasted_iota(jnp.int32, (8, 1), 0)
    upper = (row // 2) % 2 == 1
    first_len = LMAX + 1 - order
    base = jnp.where(upper, -1, order)
    own_order = jnp.where(upper, LMAX - order, order)
    length = jnp.where(upper, order + 1, first_len).astype(jnp.float32)
    begin = jnp.where(upper, first_len, 0)
    end = jnp.where(upper, PACK, first_len)
    scaling = 1.0 / jnp.sqrt(length)
    step = 1536
    synth = jnp.zeros((32, RINGS), jnp.float32)
    for start in range(0, PADDED, step):
        size = min(step, PADDED - start)
        own = coeffs_ref[:, start : start + size]
        if start + size < PADDED:
            ahead = coeffs_ref[:, start + size : start + size + 128]
        else:
            ahead = jnp.zeros((4, 128), jnp.float32)
        wide = jnp.concatenate([own, ahead], axis=1)
        after = pltpu.roll(wide, size + 127, axis=1)[:, :size]
        spread = [jnp.concatenate([a[0:2], a[0:2], a[2:4], a[2:4]], axis=0) for a in (own, after)]
        position = start + lax.broadcasted_iota(jnp.int32, (8, size), 1)
        inside = (position >= begin) & (position < end)
        degree = (base + position).astype(jnp.float32)
        plain = jnp.where(inside, scaling, 0.0)
        sloped = plain * (degree * (1.0 / LMAX))
        ahead_factor = jnp.where(
            inside & (position < end - 1),
            (degree + (1.0 + own_order.astype(jnp.float32))) * (scaling * (1.0 / LMAX)),
            0.0,
        )
        curved = sloped * ((degree + 1.0) * (1.0 / LMAX))
        weights = jnp.concatenate(
            [spread[0] * plain, spread[0] * sloped, spread[1] * ahead_factor, spread[0] * curved],
            axis=0,
        ).astype(jnp.bfloat16)
        held = min(size, PACK - start)
        synth = synth + lax.dot_general(
            weights[:, :held],
            table_ref[:, start : start + held],
            (((1,), (1,)), ((), ())),
            preferred_element_type=jnp.float32,
        )
    sine, cosine = info_ref[0:1, :RINGS], info_ref[1:2, :RINGS]
    fields = [synth[0:8], (cosine * synth[8:16] - synth[16:24]) / sine, synth[24:32]]
    fields = [jnp.concatenate([a[0:4], a[4:8]], axis=1) for a in fields]
    if which == 0:
        (out_ref,) = rest
        for index in range(3):
            out_ref[4 * index : 4 * index + 4, :] = fields[index]
    else:
        other_ref, _, out_ref = rest
        for index in range(3):
            rows = jnp.concatenate([other_ref[4 * index : 4 * index + 4, :], fields[index]], axis=0)
            out_ref[8 * index : 8 * index + 8, :] = rows


def inverse_kernel(*refs):
    blocks, (info_ref, table_ref, steep_ref, bend_ref, left_ref) = refs[:4], refs[4:]

    @pl.when(pl.program_id(0) == 0)
    def _():
        inverse = (1.0 / info_ref[...]).T[:, 0:1]
        first, slope, laplace = [
            jnp.concatenate(
                [ref[:, 8 * index : 8 * index + 8, :].reshape(ROWS // 4, 2 * RINGS) for ref in blocks],
                axis=0,
            ).T
            for index in range(3)
        ]
        scaled = first * inverse
        half = (0.5 * scaled) * inverse
        for index, rows in enumerate((slope, scaled, half, slope * inverse, 0.5 * laplace)):
            high = rows.astype(jnp.bfloat16)
            low = (rows - high.astype(jnp.float32)).astype(jnp.bfloat16)
            left_ref[index, :, 0:ROWS] = high
            left_ref[index, :, ROWS:] = low

    rows_here = pl.ds(pl.multiple_of(pl.program_id(0) * RINGS, RINGS), RINGS)

    def to_grid(rows, table):
        return jnp.dot(
            left_ref[rows, rows_here, :], table_ref[table], preferred_element_type=jnp.float32
        )

    p = to_grid(0, 0)
    q = to_grid(1, 1)
    half_t = to_grid(2, 2)
    s = to_grid(3, 1)
    half_l = to_grid(4, 0)
    p2, q2 = p * p, q * q
    outer = 1.0 + q2
    area = outer + p2
    root = lax.rsqrt(area)
    steep_ref[0] = (area * root).astype(jnp.bfloat16)
    top = (q2 - p2) * half_t - outer * half_l - (p * q) * s
    bend_ref[0] = (top * (root * root * root)).astype(jnp.bfloat16)


VMEM = pl.BlockSpec(memory_space=pltpu.VMEM)
SMEM = pl.BlockSpec(memory_space=pltpu.SMEM)


ANY = pl.BlockSpec(memory_space=pl.ANY)


COST = pl.CostEstimate(flops=1000000000, bytes_accessed=4000000, transcendentals=0)


def call(kernel, shape, dtype, in_specs, limit=24, **kwargs):
    return pl.pallas_call(
        kernel,
        out_shape=jax.ShapeDtypeStruct(shape, dtype),
        in_specs=in_specs,
        out_specs=VMEM,
        compiler_params=pltpu.CompilerParams(vmem_limit_bytes=limit << 20),
        **kwargs,
    )


def on_device(altitude_grids, polynomial_values, span_azimuthal_modes, slot_mapping):
    layers, rings, meridians = altitude_grids.shape
    n_ord = lax.axis_size("ord")
    lines = layers * rings

    def from_back(value, stride, step):
        size = 4 * stride
        return lax.ppermute(
            value, "ord", [(k, k // size * size + (k + stride * step) % size) for k in range(n_ord)]
        )

    wave, info, orders = pl.pallas_call(
        prepare_kernel,
        out_shape=[
            jax.ShapeDtypeStruct((ROWS, meridians), jnp.bfloat16),
            jax.ShapeDtypeStruct((8, lines), jnp.float32),
            jax.ShapeDtypeStruct((ROWS, 128), jnp.int32),
        ],
        in_specs=[VMEM],
        out_specs=[VMEM] * 3,
        cost_estimate=COST,
        compiler_params=pltpu.CompilerParams(vmem_limit_bytes=24 << 20),
    )(jnp.stack([span_azimuthal_modes, slot_mapping]))
    product = pl.pallas_call(
        forward_kernel,
        out_shape=[jax.ShapeDtypeStruct((32, lines), jnp.float32)] * 4,
        in_specs=[VMEM] * 2,
        out_specs=[VMEM] * 4,
        compiler_params=pltpu.CompilerParams(vmem_limit_bytes=24 << 20),
    )(wave, altitude_grids)
    parts = [product[0]] + [from_back(product[a], 1, STEPS[a]) for a in (1, 2, 3)]

    def hold(which, after):
        return call(
            functools.partial(hold_kernel, which),
            polynomial_values.shape[1:],
            jnp.bfloat16,
            [ANY, ANY],
            limit=44,
            cost_estimate=COST,
            scratch_shapes=[pltpu.SemaphoreType.DMA((4,))],
        )(polynomial_values, after)

    def summed(kernel, rows, values, after):
        return pl.pallas_call(
            kernel,
            out_shape=[jax.ShapeDtypeStruct((rows, lines), jnp.float32)] * 2,
            in_specs=[VMEM] * len(values) + [ANY],
            out_specs=[VMEM] * 2,
            compiler_params=pltpu.CompilerParams(vmem_limit_bytes=24 << 20),
        )(*values, after)

    other_table = hold(1, info)
    keep, send = summed(gather_kernel, 16, parts, other_table)
    own_table = hold(0, keep)
    keep, send = summed(halve_kernel, 8, [keep, swap(send, "ord", 4)], own_table)
    parts = [keep, swap(send, "ord", 12)]
    tables_held = (own_table, other_table)

    def analysis(which):
        return call(
            functools.partial(analysis_kernel, which), (4, PADDED), jnp.float32, [VMEM] * 4
        )(*parts, info, tables_held[which])

    outgoing = analysis(1)
    other = swap(outgoing, "lat", 1)
    coeffs = analysis(0) + other
    tables = call(table_kernel, (3, 2 * ROWS, meridians), jnp.bfloat16, [VMEM, ANY], cost_estimate=COST)(
        orders, outgoing
    )

    def turn(value, step):
        n = lax.axis_size("lat")
        return lax.ppermute(value, "lat", [(k, k // 8 * 8 + (k + 2 * step) % 8) for k in range(n)])

    received = [turn(coeffs, step) for step in STEPS[1:]]
    coeffs = call(add_kernel, (4, PADDED), jnp.float32, [VMEM] * 4 + [ANY])(
        coeffs, *received, tables
    )
    coeffs = coeffs + swap(coeffs, "lat", 8)
    other = swap(coeffs, "lat", 1)

    mine = call(
        functools.partial(synthesis_kernel, 0), (12, layers * rings), jnp.float32, [VMEM] * 3
    )(coeffs, info, own_table)
    fields = call(
        functools.partial(synthesis_kernel, 1),
        (24, layers * rings),
        jnp.float32,
        [VMEM] * 4 + [ANY],
    )(other, info, other_table, mine, tables)

    column = jnp.stack([fields] + [from_back(fields, 4, step) for step in STEPS[1:]])
    blocks = [column] + [from_back(column, 1, step) for step in STEPS[1:]]

    block = pl.BlockSpec((1, rings, meridians), lambda f: (f, 0, 0))
    return pl.pallas_call(
        inverse_kernel,
        grid=(layers,),
        out_shape=[jax.ShapeDtypeStruct((layers, rings, meridians), jnp.bfloat16)] * 2,
        in_specs=[VMEM] * 6,
        out_specs=[block, block],
        scratch_shapes=[pltpu.VMEM((5, layers * rings, 2 * ROWS), jnp.bfloat16)],
        compiler_params=pltpu.CompilerParams(vmem_limit_bytes=32 << 20),
    )(*blocks, info, tables)


def solution(mesh):
    return jax.shard_map(
        on_device,
        mesh=mesh,
        in_specs=(P(None, "lat", "ord"), P("ord", "lat", None), P(), P()),
        out_specs=(P(None, "lat", "ord"), P(None, "lat", "ord")),
        check_vma=False,
    )
```

time: 82.8 us -> 74.4 us (0.90)
  blocking collectives: 46.7 us -> 0 us
  starting transfers between devices: 6.29 us -> 34.4 us
  waiting for transfers between devices: 9.94 us -> 20 us
  local copies, waits for them, and re-layouts: 1.42 us -> 0.01 us
    all_to_all x2 -> x0, blocking collectives: 46.7 us -> none  [the longest x1 24.1 us: on_device(): everything = lax.all_to_all(fields, 'ord', 0, 0, tiled=True)]
    ppermute x0 -> x9, starting transfers between devices: none -> 20.4 us  [from_back(): lax.ppermute(value, 'ord', [(k, k // size * size + (k + stride * step) %...]
    ppermute x3 -> x5, starting transfers between devices: 1.56 us -> 10.4 us  [swap(): lax.ppermute(value, axis, [(k, k ^ mask) for k in range(lax.axis_size(axi...]
    ppermute x0 -> x9, waiting for transfers between devices: none -> 7.29 us  [from_back(): lax.ppermute(value, 'ord', [(k, k // size * size + (k + stride * step) %...]
    pallas_call x3 -> x7, Pallas kernels: 5.03 us -> 8.94 us  [the longest x2 4.4 us: hold(): call(functools.partial(hold_kernel, which), polynomial_values.shape[1:],...]
    pallas_call x1, Pallas kernels: 3.57 us -> 1.48 us  [on_device(): pl.pallas_call(prepare_kernel, out_shape=[jax.ShapeDtypeStruct((ROWS, mer...]
    pallas_call x1, Pallas kernels: 5.85 us -> 4.19 us  [on_device(): pl.pallas_call(inverse_kernel, grid=(layers,), out_shape=[jax.ShapeDtypeS...]
    ppermute x3, waiting for transfers between devices: 4.08 us -> 5.64 us  [turn(): lax.ppermute(value, 'lat', [(k, k // 8 * 8 + (k + 2 * step) % 8) for k in...]
  transfers between devices with their start and end apart: 6 -> 17, of which waited for: 4 -> 11; matrix products, arithmetic and copies ran while one was open for 0% -> 0% of each run, Pallas kernels for 6% -> 12%
where the time goes in v3:
time: 74.4 us; the launch traced here: 73.8 us
  starting transfers between devices  34.4 us (46%)
  waiting for transfers between devices  20 us (27%)
  Pallas kernels  17.7 us (24%)
  other arithmetic  0.88 us (1%)
  between operations  0.88 us (1%)
    ppermute x9, starting transfers between devices, from_back(): lax.ppermute(value, 'ord', [(k, k // size * size + (k + stride * step) %...  20.4 us
    ppermute x5, starting transfers between devices, swap(): lax.ppermute(value, axis, [(k, k ^ mask) for k in range(lax.axis_size(axi...  10.4 us
    ppermute x9, waiting for transfers between devices, from_back(): lax.ppermute(value, 'ord', [(k, k // size * size + (k + stride * step) %...  7.29 us
    ppermute x5, waiting for transfers between devices, swap(): lax.ppermute(value, axis, [(k, k ^ mask) for k in range(lax.axis_size(axi...  7.04 us
    ppermute x3, waiting for transfers between devices, turn(): lax.ppermute(value, 'lat', [(k, k // 8 * 8 + (k + 2 * step) % 8) for k in...  5.64 us
    pallas_call x2, Pallas kernels, hold(): call(functools.partial(hold_kernel, which), polynomial_values.shape[1:],...  4.4 us
    pallas_call x1, Pallas kernels, on_device(): pl.pallas_call(inverse_kernel, grid=(layers,), out_shape=[jax.ShapeDtypeS...  4.19 us
    ppermute x3, starting transfers between devices, turn(): lax.ppermute(value, 'lat', [(k, k // 8 * 8 + (k + 2 * step) % 8) for k in...  3.59 us
  transfers between devices with their start and end apart: 17, of which 11 were waited for; matrix products, arithmetic and copies ran while one was open for 0% of the time, Pallas kernels for 12%

profile of v3, /device:TPU:6, one launch (start us, length us, event | category | flops | bytes accessed | tf_op | source)
XLA Modules:
  0.0 73.8 jit_solution(2020457196865871476)
XLA Ops:
  0.6 0.0 copy-start
  0.6 0.8 %pad_add_fusion.small_ref = s32[2,64]{1,0:T(2,128)S(1)} fusion(s32[1,64]{1,0:T(1,128)} %bitcast.10, s32[1,64]{1,0:T(1,128)} %bitcast.11), kind=kLoop, calls=%fused_computation.1 | loop fusion | flops 128 | bytes 1024 | tf_op jit(solution)/shard_map/stack | solution.py:311
  1.4 1.5 %shard_map.59 = (bf16[128,1350]{1,0:T(8,128)(2,1)S(1)}, f32[8,384]{1,0:T(8,128)S(1)}, s32[128,128]{1,0:T(8,128)S(1)}) custom-call(s32[2,64]{1,0:T(2,128)S(1)} %pad_add_fusion.small_ref), custom_call_target="tpu_custom_call" | custom-call | flops 1000000000 | bytes 4000000 | tf_op jit(solution)/shard_map/pallas_call | solution.py:300
  2.9 0.0 copy-done
  2.9 0.4 shard_map.60
  3.4 3.3 %collective-permute-start = (f32[32,384]{1,0:T(8,128)S(1)}, f32[32,384]{1,0:T(8,128)S(1)}, u32[]{:S(2)}, u32[]{:S(2)}) collective-permute-start(f32[32,384]{1,0:T(8,128)S(1)} %get-tuple-element.15), channel_id=1, source_target_pairs={{0,2},{1,3},{2,0},{3,1},{4,6},{5,7},{6,4},{7,5},{8,10},{9,11},{10,... | collective-permute-start | bytes 147464 | tf_op jit(solution)/shard_map/ppermute | solution.py:296
  6.6 0.7 collective-permute-start.1
  7.3 2.6 %collective-permute-start.2 = (f32[32,384]{1,0:T(8,128)S(1)}, f32[32,384]{1,0:T(8,128)S(1)}, u32[]{:S(2)}, u32[]{:S(2)}) collective-permute-start(f32[32,384]{1,0:T(8,128)S(1)} %get-tuple-element.17), channel_id=1, source_target_pairs={{0,3},{1,0},{2,1},{3,2},{4,7},{5,4},{6,5},{7,6},{8,11},{9,8},{10,9... | collective-permute-start | bytes 147464 | tf_op jit(solution)/shard_map/ppermute | solution.py:296
  9.9 2.2 %shard_map.61._.table_ref = bf16[192,10802]{1,0:T(8,128)(2,1)S(1)} custom-call(bf16[2,192,10802]{2,1,0:T(8,128)(2,1)} %table_ref.3, f32[8,384]{1,0:T(8,128)S(1)} %get-tuple-element.18._.info_ref.refs_4_), custom_call_target="tpu_custom_call" | custom-call | flops 1000000000 | bytes 4000000 | tf_op jit(solution)/shard_map/pallas_call | solution.py:322
  12.1 0.0 collective-permute-done.second_ref
  12.1 0.0 collective-permute-done.1.third_ref
  12.1 0.0 collective-permute-done.2.fourth_ref
  12.1 3.4 %collective-permute-start.3 = (f32[16,384]{1,0:T(8,128)S(1)}, f32[16,384]{1,0:T(8,128)S(1)}, u32[]{:S(2)}, u32[]{:S(2)}) collective-permute-start(f32[16,384]{1,0:T(8,128)S(1)} %get-tuple-element.20), channel_id=1, source_target_pairs={{0,4},{1,5},{2,6},{3,7},{4,0},{5,1},{6,2},{7,3},{8,12},{9,13},{10,... | collective-permute-start | bytes 73736 | tf_op jit(solution)/shard_map/ppermute | solution.py:30
  15.5 2.2 %shard_map.63._.table_ref = bf16[192,10802]{1,0:T(8,128)(2,1)S(1)} custom-call(bf16[2,192,10802]{2,1,0:T(8,128)(2,1)} %table_ref.3, f32[16,384]{1,0:T(8,128)S(1)} %get-tuple-element.19._.first_ref), custom_call_target="tpu_custom_call" | custom-call | flops 1000000000 | bytes 4000000 | tf_op jit(solution)/shard_map/pallas_call | solution.py:322
  17.7 0.0 collective-permute-done.3.second_ref
  17.7 5.5 %collective-permute-start.4 = (f32[8,384]{1,0:T(8,128)S(1)}, f32[8,384]{1,0:T(8,128)S(1)}, u32[]{:S(2)}, u32[]{:S(2)}) collective-permute-start(f32[8,384]{1,0:T(8,128)S(1)} %get-tuple-element.22), channel_id=1, source_target_pairs={{0,12},{1,13},{2,14},{3,15},{4,8},{5,9},{6,10},{7,11},{8,4},{9,5},... | collective-permute-start | bytes 36872 | tf_op jit(solution)/shard_map/ppermute | solution.py:30
  23.3 1.7 %collective-permute-done.4.second_ref = f32[8,384]{1,0:T(8,128)S(1)} collective-permute-done((f32[8,384]{1,0:T(8,128)S(1)}, f32[8,384]{1,0:T(8,128)S(1)}, u32[]{:S(2)}, u32[]{:S(2)}) %collective-permute-start.4) | collective-permute-done | bytes 12320 | tf_op jit(solution)/shard_map/ppermute | solution.py:30
  24.9 0.7 %shard_map.66.after_ref = f32[4,10880]{1,0:T(4,128)S(1)} custom-call(f32[8,384]{1,0:T(8,128)S(1)} %get-tuple-element.21.first_ref, f32[8,384]{1,0:T(8,128)S(1)} %collective-permute-done.4.second_ref, f32[8,384]{1,0:T(8,128)S(1)} %get-tuple-element.18._.info_ref.refs_4_, bf16[192,10802]{1,0:T(8,128)(2,1)S(1)} %shard_map.61._.table_ref), custom_call_target="tpu_custom_call" | custom-call | tf_op jit(solution)/shard_map/pallas_call | solution.py:349
  25.7 0.1 collective-permute-start.5
  25.7 0.7 %shard_map.65 = f32[4,10880]{1,0:T(4,128)S(1)} custom-call(f32[8,384]{1,0:T(8,128)S(1)} %get-tuple-element.21.first_ref, f32[8,384]{1,0:T(8,128)S(1)} %collective-permute-done.4.second_ref, f32[8,384]{1,0:T(8,128)S(1)} %get-tuple-element.18._.info_ref.refs_4_, bf16[192,10802]{1,0:T(8,128)(2,1)S(1)} %shard_map.63._.table_ref), custom_call_target="tpu_custom_call" | custom-call | tf_op jit(solution)/shard_map/pallas_call | solution.py:349
  26.5 0.7 collective-permute-done.5
  27.2 1.5 %collective-permute-start.6 = (f32[4,10880]{1,0:T(4,128)S(1)}, f32[4,10880]{1,0:T(4,128)S(1)}, u32[]{:S(2)}, u32[]{:S(2)}) collective-permute-start(f32[4,10880]{1,0:T(4,128)S(1)} %add.6.first_ref), channel_id=1, source_target_pairs={{0,64},{16,80},{32,96},{48,112},{64,0},{80,16},{96,32},{112,48},{1... | collective-permute-start | bytes 522248 | tf_op jit(solution)/shard_map/ppermute | solution.py:362
  28.7 2.1 %collective-permute-start.7 = (f32[4,10880]{1,0:T(4,128)S(1)}, f32[4,10880]{1,0:T(4,128)S(1)}, u32[]{:S(2)}, u32[]{:S(2)}) collective-permute-start(f32[4,10880]{1,0:T(4,128)S(1)} %add.6.first_ref), channel_id=1, source_target_pairs={{0,32},{16,48},{32,64},{48,80},{64,96},{80,112},{96,0},{112,16},{1... | collective-permute-start | bytes 522248 | tf_op jit(solution)/shard_map/ppermute | solution.py:362
  30.8 0.0 collective-permute-start.8
  30.8 2.5 %shard_map.67._.rest_1_.refs_5_ = bf16[3,256,1350]{2,1,0:T(8,128)(2,1)S(1)} custom-call(s32[128,128]{1,0:T(8,128)S(1)} %get-tuple-element.23.orders_ref, f32[4,10880]{1,0:T(4,128)S(1)} %shard_map.66.after_ref), custom_call_target="tpu_custom_call" | custom-call | flops 1000000000 | bytes 4000000 | tf_op jit(solution)/shard_map/pallas_call | solution.py:356
  33.3 2.7 %collective-permute-done.6.second_ref = f32[4,10880]{1,0:T(4,128)S(1)} collective-permute-done((f32[4,10880]{1,0:T(4,128)S(1)}, f32[4,10880]{1,0:T(4,128)S(1)}, u32[]{:S(2)}, u32[]{:S(2)}) %collective-permute-start.6) | collective-permute-done | bytes 174112 | tf_op jit(solution)/shard_map/ppermute | solution.py:362
  36.0 0.7 collective-permute-done.7.third_ref
  36.8 2.2 %collective-permute-done.8.fourth_ref = f32[4,10880]{1,0:T(4,128)S(1)} collective-permute-done((f32[4,10880]{1,0:T(4,128)S(1)}, f32[4,10880]{1,0:T(4,128)S(1)}, u32[]{:S(2)}, u32[]{:S(2)}) %collective-permute-start.8) | collective-permute-done | bytes 174112 | tf_op jit(solution)/shard_map/ppermute | solution.py:362
  39.0 1.4 %collective-permute-start.9 = (f32[4,10880]{1,0:T(4,128)S(1)}, f32[4,10880]{1,0:T(4,128)S(1)}, u32[]{:S(2)}, u32[]{:S(2)}) collective-permute-start(f32[4,10880]{1,0:T(4,128)S(1)} %shard_map.68), channel_id=1, source_target_pairs={{0,128},{16,144},{32,160},{48,176},{64,192},{80,208},{96,224},{112... | collective-permute-start | bytes 522248 | tf_op jit(solution)/shard_map/ppermute | solution.py:30
  40.4 4.7 %collective-permute-done.9 = f32[4,10880]{1,0:T(4,128)S(1)} collective-permute-done((f32[4,10880]{1,0:T(4,128)S(1)}, f32[4,10880]{1,0:T(4,128)S(1)}, u32[]{:S(2)}, u32[]{:S(2)}) %collective-permute-start.9) | collective-permute-done | bytes 174112 | tf_op jit(solution)/shard_map/ppermute | solution.py:30
  45.2 0.1 collective-permute-start.10
  45.3 1.5 %shard_map.69.rest_0_ = f32[12,384]{1,0:T(8,128)S(1)} custom-call(f32[4,10880]{1,0:T(4,128)S(1)} %add.7.coeffs_ref, f32[8,384]{1,0:T(8,128)S(1)} %get-tuple-element.18._.info_ref.refs_4_, bf16[192,10802]{1,0:T(8,128)(2,1)S(1)} %shard_map.63._.table_ref), custom_call_target="tpu_custom_call" | custom-call | tf_op jit(solution)/shard_map/pallas_call | solution.py:371
  46.8 0.0 collective-permute-done.10.coeffs_ref
  46.9 1.5 %shard_map.70 = f32[24,384]{1,0:T(8,128)S(1)} custom-call(f32[4,10880]{1,0:T(4,128)S(1)} %collective-permute-done.10.coeffs_ref, f32[8,384]{1,0:T(8,128)S(1)} %get-tuple-element.18._.info_ref.refs_4_, bf16[192,10802]{1,0:T(8,128)(2,1)S(1)} %shard_map.61._.table_ref, f32[12,384]{1,0:T(8,128)S(1)} %shard_map.69.rest_0_, ...), custom_call_target="tpu_custom_call" | custom-call | tf_op jit(solution)/shard_map/pallas_call | solution.py:374
  48.4 5.1 %collective-permute-start.11 = (f32[24,384]{1,0:T(8,128)S(1)}, f32[24,384]{1,0:T(8,128)S(1)}, u32[]{:S(2)}, u32[]{:S(2)}) collective-permute-start(f32[24,384]{1,0:T(8,128)S(1)} %shard_map.70), channel_id=1, source_target_pairs={{0,8},{1,9},{2,10},{3,11},{4,12},{5,13},{6,14},{7,15},{8,0},{9,1},... | collective-permute-start | bytes 110600 | tf_op jit(solution)/shard_map/ppermute | solution.py:296
  53.6 1.5 %collective-permute-start.12 = (f32[24,384]{1,0:T(8,128)S(1)}, f32[24,384]{1,0:T(8,128)S(1)}, u32[]{:S(2)}, u32[]{:S(2)}) collective-permute-start(f32[24,384]{1,0:T(8,128)S(1)} %shard_map.70), channel_id=1, source_target_pairs={{0,4},{1,5},{2,6},{3,7},{4,8},{5,9},{6,10},{7,11},{8,12},{9,13},{1... | collective-permute-start | bytes 110600 | tf_op jit(solution)/shard_map/ppermute | solution.py:296
  55.0 2.7 %collective-permute-start.13 = (f32[24,384]{1,0:T(8,128)S(1)}, f32[24,384]{1,0:T(8,128)S(1)}, u32[]{:S(2)}, u32[]{:S(2)}) collective-permute-start(f32[24,384]{1,0:T(8,128)S(1)} %shard_map.70), channel_id=1, source_target_pairs={{0,12},{1,13},{2,14},{3,15},{4,0},{5,1},{6,2},{7,3},{8,4},{9,5},{1... | collective-permute-start | bytes 110600 | tf_op jit(solution)/shard_map/ppermute | solution.py:296
  57.7 0.0 collective-permute-done.11
  57.7 1.9 %collective-permute-done.12 = f32[24,384]{1,0:T(8,128)S(1)} collective-permute-done((f32[24,384]{1,0:T(8,128)S(1)}, f32[24,384]{1,0:T(8,128)S(1)}, u32[]{:S(2)}, u32[]{:S(2)}) %collective-permute-start.12) | collective-permute-done | bytes 36896 | tf_op jit(solution)/shard_map/ppermute | solution.py:296
  59.6 0.4 collective-permute-done.13
  60.0 1.4 %collective-permute-start.14 = (f32[4,24,384]{2,1,0:T(8,128)S(1)}, f32[4,24,384]{2,1,0:T(8,128)S(1)}, u32[]{:S(2)}, u32[]{:S(2)}) collective-permute-start(f32[4,24,384]{2,1,0:T(8,128)S(1)} %pad_maximum_fusion.refs_0_), channel_id=1, source_target_pairs={{0,2},{1,3},{2,0},{3,1},{4,6},{5,7},{6,4},{7,5},{8,10},{9,11},{10,... | collective-permute-start | bytes 442376 | tf_op jit(solution)/shard_map/ppermute | solution.py:296
  61.4 2.6 %collective-permute-start.15 = (f32[4,24,384]{2,1,0:T(8,128)S(1)}, f32[4,24,384]{2,1,0:T(8,128)S(1)}, u32[]{:S(2)}, u32[]{:S(2)}) collective-permute-start(f32[4,24,384]{2,1,0:T(8,128)S(1)} %pad_maximum_fusion.refs_0_), channel_id=1, source_target_pairs={{0,1},{1,2},{2,3},{3,0},{4,5},{5,6},{6,7},{7,4},{8,9},{9,10},{10,1... | collective-permute-start | bytes 442376 | tf_op jit(solution)/shard_map/ppermute | solution.py:296
  64.0 0.6 collective-permute-start.16
  64.6 3.1 %collective-permute-done.14.refs_1_ = f32[4,24,384]{2,1,0:T(8,128)S(1)} collective-permute-done((f32[4,24,384]{2,1,0:T(8,128)S(1)}, f32[4,24,384]{2,1,0:T(8,128)S(1)}, u32[]{:S(2)}, u32[]{:S(2)}) %collective-permute-start.14) | collective-permute-done | bytes 147488 | tf_op jit(solution)/shard_map/ppermute | solution.py:296
  67.7 1.5 %collective-permute-done.15.refs_2_ = f32[4,24,384]{2,1,0:T(8,128)S(1)} collective-permute-done((f32[4,24,384]{2,1,0:T(8,128)S(1)}, f32[4,24,384]{2,1,0:T(8,128)S(1)}, u32[]{:S(2)}, u32[]{:S(2)}) %collective-permute-start.15) | collective-permute-done | bytes 147488 | tf_op jit(solution)/shard_map/ppermute | solution.py:296
  69.2 0.4 collective-permute-done.16.refs_3_
  69.6 4.2 %shard_map.71 = (bf16[2,192,1350]{2,1,0:T(8,128)(2,1)}, bf16[2,192,1350]{2,1,0:T(8,128)(2,1)}) custom-call(f32[4,24,384]{2,1,0:T(8,128)S(1)} %pad_maximum_fusion.refs_0_, f32[4,24,384]{2,1,0:T(8,128)S(1)} %collective-permute-done.14.refs_1_, f32[4,24,384]{2,1,0:T(8,128)S(1)} %collective-permute-done.15.refs_2_, ...), custom_call_target="tpu_custom_call" | custom-call | tf_op jit(solution)/shard_map/pallas_call | solution.py:385
  (6 shorter events, 0.2 us)
Async XLA Ops:
  0.6 2.3 %copy-start = (bf16[2,192,1350]{2,1,0:T(8,128)(2,1)S(1)}, bf16[2,192,1350]{2,1,0:T(8,128)(2,1)}, u32[]{:S(2)}) copy-start(bf16[2,192,1350]{2,1,0:T(8,128)(2,1)} %grids_ref.1) | copy-start | bytes 3110404
  3.4 8.7 %collective-permute-start = (f32[32,384]{1,0:T(8,128)S(1)}, f32[32,384]{1,0:T(8,128)S(1)}, u32[]{:S(2)}, u32[]{:S(2)}) collective-permute-start(f32[32,384]{1,0:T(8,128)S(1)} %get-tuple-element.15), channel_id=1, source_target_pairs={{0,2},{1,3},{2,0},{3,1},{4,6},{5,7},{6,4},{7,5},{8,10},{9,11},{10,... | collective-permute-start | bytes 147464 | tf_op jit(solution)/shard_map/ppermute | solution.py:296
  6.6 5.5 %collective-permute-start.1 = (f32[32,384]{1,0:T(8,128)S(1)}, f32[32,384]{1,0:T(8,128)S(1)}, u32[]{:S(2)}, u32[]{:S(2)}) collective-permute-start(f32[32,384]{1,0:T(8,128)S(1)} %get-tuple-element.16), channel_id=1, source_target_pairs={{0,1},{1,2},{2,3},{3,0},{4,5},{5,6},{6,7},{7,4},{8,9},{9,10},{10,1... | collective-permute-start | bytes 147464 | tf_op jit(solution)/shard_map/ppermute | solution.py:296
  7.3 4.8 %collective-permute-start.2 = (f32[32,384]{1,0:T(8,128)S(1)}, f32[32,384]{1,0:T(8,128)S(1)}, u32[]{:S(2)}, u32[]{:S(2)}) collective-permute-start(f32[32,384]{1,0:T(8,128)S(1)} %get-tuple-element.17), channel_id=1, source_target_pairs={{0,3},{1,0},{2,1},{3,2},{4,7},{5,4},{6,5},{7,6},{8,11},{9,8},{10,9... | collective-permute-start | bytes 147464 | tf_op jit(solution)/shard_map/ppermute | solution.py:296
  12.1 5.6 %collective-permute-start.3 = (f32[16,384]{1,0:T(8,128)S(1)}, f32[16,384]{1,0:T(8,128)S(1)}, u32[]{:S(2)}, u32[]{:S(2)}) collective-permute-start(f32[16,384]{1,0:T(8,128)S(1)} %get-tuple-element.20), channel_id=1, source_target_pairs={{0,4},{1,5},{2,6},{3,7},{4,0},{5,1},{6,2},{7,3},{8,12},{9,13},{10,... | collective-permute-start | bytes 73736 | tf_op jit(solution)/shard_map/ppermute | solution.py:30
  17.7 7.2 %collective-permute-start.4 = (f32[8,384]{1,0:T(8,128)S(1)}, f32[8,384]{1,0:T(8,128)S(1)}, u32[]{:S(2)}, u32[]{:S(2)}) collective-permute-start(f32[8,384]{1,0:T(8,128)S(1)} %get-tuple-element.22), channel_id=1, source_target_pairs={{0,12},{1,13},{2,14},{3,15},{4,8},{5,9},{6,10},{7,11},{8,4},{9,5},... | collective-permute-start | bytes 36872 | tf_op jit(solution)/shard_map/ppermute | solution.py:30
  25.7 1.5 %collective-permute-start.5 = (f32[4,10880]{1,0:T(4,128)S(1)}, f32[4,10880]{1,0:T(4,128)S(1)}, u32[]{:S(2)}, u32[]{:S(2)}) collective-permute-start(f32[4,10880]{1,0:T(4,128)S(1)} %shard_map.66.after_ref), channel_id=1, source_target_pairs={{0,16},{16,0},{32,48},{48,32},{64,80},{80,64},{96,112},{112,96},{1... | collective-permute-start | bytes 522248 | tf_op jit(solution)/shard_map/ppermute | solution.py:30
  27.2 8.9 %collective-permute-start.6 = (f32[4,10880]{1,0:T(4,128)S(1)}, f32[4,10880]{1,0:T(4,128)S(1)}, u32[]{:S(2)}, u32[]{:S(2)}) collective-permute-start(f32[4,10880]{1,0:T(4,128)S(1)} %add.6.first_ref), channel_id=1, source_target_pairs={{0,64},{16,80},{32,96},{48,112},{64,0},{80,16},{96,32},{112,48},{1... | collective-permute-start | bytes 522248 | tf_op jit(solution)/shard_map/ppermute | solution.py:362
  28.7 8.1 %collective-permute-start.7 = (f32[4,10880]{1,0:T(4,128)S(1)}, f32[4,10880]{1,0:T(4,128)S(1)}, u32[]{:S(2)}, u32[]{:S(2)}) collective-permute-start(f32[4,10880]{1,0:T(4,128)S(1)} %add.6.first_ref), channel_id=1, source_target_pairs={{0,32},{16,48},{32,64},{48,80},{64,96},{80,112},{96,0},{112,16},{1... | collective-permute-start | bytes 522248 | tf_op jit(solution)/shard_map/ppermute | solution.py:362
  30.8 8.2 %collective-permute-start.8 = (f32[4,10880]{1,0:T(4,128)S(1)}, f32[4,10880]{1,0:T(4,128)S(1)}, u32[]{:S(2)}, u32[]{:S(2)}) collective-permute-start(f32[4,10880]{1,0:T(4,128)S(1)} %add.6.first_ref), channel_id=1, source_target_pairs={{0,96},{16,112},{32,0},{48,16},{64,32},{80,48},{96,64},{112,80},{1... | collective-permute-start | bytes 522248 | tf_op jit(solution)/shard_map/ppermute | solution.py:362
  39.0 6.1 %collective-permute-start.9 = (f32[4,10880]{1,0:T(4,128)S(1)}, f32[4,10880]{1,0:T(4,128)S(1)}, u32[]{:S(2)}, u32[]{:S(2)}) collective-permute-start(f32[4,10880]{1,0:T(4,128)S(1)} %shard_map.68), channel_id=1, source_target_pairs={{0,128},{16,144},{32,160},{48,176},{64,192},{80,208},{96,224},{112... | collective-permute-start | bytes 522248 | tf_op jit(solution)/shard_map/ppermute | solution.py:30
  45.2 1.6 %collective-permute-start.10 = (f32[4,10880]{1,0:T(4,128)S(1)}, f32[4,10880]{1,0:T(4,128)S(1)}, u32[]{:S(2)}, u32[]{:S(2)}) collective-permute-start(f32[4,10880]{1,0:T(4,128)S(1)} %add.7.coeffs_ref), channel_id=1, source_target_pairs={{0,16},{16,0},{32,48},{48,32},{64,80},{80,64},{96,112},{112,96},{1... | collective-permute-start | bytes 522248 | tf_op jit(solution)/shard_map/ppermute | solution.py:30
  48.4 9.3 %collective-permute-start.11 = (f32[24,384]{1,0:T(8,128)S(1)}, f32[24,384]{1,0:T(8,128)S(1)}, u32[]{:S(2)}, u32[]{:S(2)}) collective-permute-start(f32[24,384]{1,0:T(8,128)S(1)} %shard_map.70), channel_id=1, source_target_pairs={{0,8},{1,9},{2,10},{3,11},{4,12},{5,13},{6,14},{7,15},{8,0},{9,1},... | collective-permute-start | bytes 110600 | tf_op jit(solution)/shard_map/ppermute | solution.py:296
  53.6 6.1 %collective-permute-start.12 = (f32[24,384]{1,0:T(8,128)S(1)}, f32[24,384]{1,0:T(8,128)S(1)}, u32[]{:S(2)}, u32[]{:S(2)}) collective-permute-start(f32[24,384]{1,0:T(8,128)S(1)} %shard_map.70), channel_id=1, source_target_pairs={{0,4},{1,5},{2,6},{3,7},{4,8},{5,9},{6,10},{7,11},{8,12},{9,13},{1... | collective-permute-start | bytes 110600 | tf_op jit(solution)/shard_map/ppermute | solution.py:296
  55.0 5.0 %collective-permute-start.13 = (f32[24,384]{1,0:T(8,128)S(1)}, f32[24,384]{1,0:T(8,128)S(1)}, u32[]{:S(2)}, u32[]{:S(2)}) collective-permute-start(f32[24,384]{1,0:T(8,128)S(1)} %shard_map.70), channel_id=1, source_target_pairs={{0,12},{1,13},{2,14},{3,15},{4,0},{5,1},{6,2},{7,3},{8,4},{9,5},{1... | collective-permute-start | bytes 110600 | tf_op jit(solution)/shard_map/ppermute | solution.py:296
  60.0 7.7 %collective-permute-start.14 = (f32[4,24,384]{2,1,0:T(8,128)S(1)}, f32[4,24,384]{2,1,0:T(8,128)S(1)}, u32[]{:S(2)}, u32[]{:S(2)}) collective-permute-start(f32[4,24,384]{2,1,0:T(8,128)S(1)} %pad_maximum_fusion.refs_0_), channel_id=1, source_target_pairs={{0,2},{1,3},{2,0},{3,1},{4,6},{5,7},{6,4},{7,5},{8,10},{9,11},{10,... | collective-permute-start | bytes 442376 | tf_op jit(solution)/shard_map/ppermute | solution.py:296
  61.4 7.8 %collective-permute-start.15 = (f32[4,24,384]{2,1,0:T(8,128)S(1)}, f32[4,24,384]{2,1,0:T(8,128)S(1)}, u32[]{:S(2)}, u32[]{:S(2)}) collective-permute-start(f32[4,24,384]{2,1,0:T(8,128)S(1)} %pad_maximum_fusion.refs_0_), channel_id=1, source_target_pairs={{0,1},{1,2},{2,3},{3,0},{4,5},{5,6},{6,7},{7,4},{8,9},{9,10},{10,1... | collective-permute-start | bytes 442376 | tf_op jit(solution)/shard_map/ppermute | solution.py:296
  64.0 5.6 %collective-permute-start.16 = (f32[4,24,384]{2,1,0:T(8,128)S(1)}, f32[4,24,384]{2,1,0:T(8,128)S(1)}, u32[]{:S(2)}, u32[]{:S(2)}) collective-permute-start(f32[4,24,384]{2,1,0:T(8,128)S(1)} %pad_maximum_fusion.refs_0_), channel_id=1, source_target_pairs={{0,3},{1,0},{2,1},{3,2},{4,7},{5,4},{6,5},{7,6},{8,11},{9,8},{10,9... | collective-permute-start | bytes 442376 | tf_op jit(solution)/shard_map/ppermute | solution.py:296

commit v4 on v3

--- a/solution.py
+++ b/solution.py
@@ -22,7 +22,7 @@
 MASKS = (0, 3, 1, 2)
 
 SINE_SERIES = tuple(
-    (-1.0) ** n * (2.0 * math.pi) ** (2 * n + 1) / math.factorial(2 * n + 1) for n in range(8)
+    (-1.0) ** n * (2.0 * math.pi) ** (2 * n + 1) / math.factorial(2 * n + 1) for n in range(7)
 )
 
 
@@ -48,15 +48,14 @@
     return v * total
 
 
-def cosine_of(orders, quarter, first):
-    longitude = first + lax.broadcasted_iota(jnp.int32, (1, MERIDIANS), 1)
-    product = orders * longitude
-    cycles = (product.astype(jnp.float32) * (1.0 / MERIDIAN_AMOUNT)).astype(jnp.int32)
-    turns = (product - cycles * MERIDIAN_AMOUNT + quarter * (MERIDIAN_AMOUNT // 4)).astype(
-        jnp.float32
-    ) * (1.0 / MERIDIAN_AMOUNT)
-    turns = turns - jnp.round(turns)
-    return sine_turns(0.25 - jnp.abs(turns))
+def cosine_of(orders, quarter, block):
+    longitude = lax.broadcasted_iota(jnp.int32, (1, MERIDIANS), 1).astype(jnp.float32)
+    begin = (orders * (block * MERIDIANS)) % MERIDIAN_AMOUNT + quarter * (MERIDIAN_AMOUNT // 4)
+    product = orders.astype(jnp.float32) * longitude
+    cycles = jnp.round(product * (1.0 / MERIDIAN_AMOUNT))
+    rest = (product - cycles * MERIDIAN_AMOUNT) + begin.astype(jnp.float32)
+    turns = rest * (1.0 / MERIDIAN_AMOUNT)
+    return sine_turns(0.25 - jnp.abs(turns - jnp.round(turns)))
 
 
 def entry(values, index):
@@ -67,16 +66,23 @@
     )
 
 
-def prepare_kernel(small_ref, wave_ref, info_ref, orders_ref):
+def prepare_kernel(small_ref, wave_ref):
+    ord_index = lax.axis_index("ord")
+    row = lax.broadcasted_iota(jnp.int32, (ROWS, 1), 0)
+    target = (ord_index // 4 ^ entry(MASKS, (row // 8) % 4)) * 4 + (
+        ord_index + entry(STEPS, row // 32)
+    ) % 4
+    orders = row_orders(small_ref[0:1, :], small_ref[1:2, :], target * 4 + (row // 2) % 4)
+    wave = cosine_of(orders, row % 2, ord_index)
+    wave_ref[...] = (wave * (1.0 / math.sqrt(MERIDIAN_AMOUNT))).astype(jnp.bfloat16)
+
+
+def info_kernel(small_ref, _, info_ref, orders_ref):
     ord_index, lat_index = lax.axis_index("ord"), lax.axis_index("lat")
     core = lat_index % 2
     modes, mapping = small_ref[0:1, :], small_ref[1:2, :]
     row = lax.broadcasted_iota(jnp.int32, (ROWS, 1), 0)
     step_y, step_z = entry(STEPS, row // 32), entry(STEPS, (row // 8) % 4)
-    target = (ord_index // 4 ^ entry(MASKS, (row // 8) % 4)) * 4 + (ord_index + step_y) % 4
-    orders = row_orders(modes, mapping, target * 4 + (row // 2) % 4)
-    wave = cosine_of(orders, row % 2, ord_index * MERIDIANS)
-    wave_ref[...] = (wave * (1.0 / math.sqrt(MERIDIAN_AMOUNT))).astype(jnp.bfloat16)
     source = (ord_index // 4 + 4 - step_z) % 4 * 4 + (ord_index + 4 - step_y) % 4
     slot = source * 4 + ((row // 4) % 2 + core) % 2 * 2 + (row // 2) % 2
     orders_ref[...] = jnp.broadcast_to(row_orders(modes, mapping, slot), (ROWS, 128))
@@ -126,7 +132,7 @@
 
 def table_kernel(orders_ref, after_ref, out_ref):
     row = lax.broadcasted_iota(jnp.int32, (ROWS, 1), 0)
-    first = lax.axis_index("ord") * MERIDIANS
+    first = lax.axis_index("ord")
     orders = orders_ref[:, 0:1]
     fraction = orders.astype(jnp.float32) * (1.0 / LMAX)
     wave = cosine_of(orders, row % 2, first) * (1.0 / math.sqrt(BAND))
@@ -160,21 +166,52 @@
     out_ref[:, PACK:] = jnp.zeros((4, PADDED - PACK), jnp.float32)
 
 
-def add_kernel(first_ref, second_ref, third_ref, fourth_ref, _, out_ref):
-    out_ref[...] = (first_ref[...] + second_ref[...]) + (third_ref[...] + fourth_ref[...])
-
-
-def synthesis_kernel(which, coeffs_ref, info_ref, table_ref, *rest):
+def turn_kernel(own_ref, other_ref, _, own_out_ref, other_out_ref):
+    step = 1536
+    for table_ref, out_ref in ((own_ref, own_out_ref), (other_ref, other_out_ref)):
+        for start in range(0, WHOLE, step):
+            out_ref[start : start + step, :] = table_ref[:, start : start + step].T
+        rest = jnp.concatenate(
+            [table_ref[:, WHOLE:], jnp.zeros((RINGS, PADDED - PACK), jnp.bfloat16)], axis=1
+        )
+        out_ref[WHOLE:, :] = rest.T
+
+
+def add_kernel(first_ref, second_ref, *rest):
+    out_ref = rest[-1]
+    out_ref[...] = first_ref[...] + second_ref[...]
+
+
+def factor_kernel(which, info_ref, _, out_ref):
     order = info_ref[2 + which : 3 + which, 0:1].astype(jnp.int32)
     row = lax.broadcasted_iota(jnp.int32, (8, 1), 0)
     upper = (row // 2) % 2 == 1
     first_len = LMAX + 1 - order
     base = jnp.where(upper, -1, order)
-    own_order = jnp.where(upper, LMAX - order, order)
+    own_order = jnp.where(upper, LMAX - order, order).astype(jnp.float32)
     length = jnp.where(upper, order + 1, first_len).astype(jnp.float32)
     begin = jnp.where(upper, first_len, 0)
     end = jnp.where(upper, PACK, first_len)
     scaling = 1.0 / jnp.sqrt(length)
+    step = 1536
+    for start in range(0, PADDED, step):
+        size = min(step, PADDED - start)
+        position = start + lax.broadcasted_iota(jnp.int32, (8, size), 1)
+        inside = (position >= begin) & (position < end)
+        degree = (base + position).astype(jnp.float32)
+        plain = jnp.where(inside, scaling, 0.0)
+        sloped = plain * (degree * (1.0 / LMAX))
+        out_ref[0, :, start : start + size] = plain
+        out_ref[1, :, start : start + size] = sloped
+        out_ref[2, :, start : start + size] = jnp.where(
+            inside & (position < end - 1),
+            (degree + (1.0 + own_order)) * (scaling * (1.0 / LMAX)),
+            0.0,
+        )
+        out_ref[3, :, start : start + size] = sloped * ((degree + 1.0) * (1.0 / LMAX))
+
+
+def synthesis_kernel(which, coeffs_ref, info_ref, table_ref, factor_ref, *rest):
     step = 1536
     synth = jnp.zeros((32, RINGS), jnp.float32)
     for start in range(0, PADDED, step):
@@ -186,28 +223,18 @@
             ahead = jnp.zeros((4, 128), jnp.float32)
         wide = jnp.concatenate([own, ahead], axis=1)
         after = pltpu.roll(wide, size + 127, axis=1)[:, :size]
-        spread = [jnp.concatenate([a[0:2], a[0:2], a[2:4], a[2:4]], axis=0) for a in (own, after)]
-        position = start + lax.broadcasted_iota(jnp.int32, (8, size), 1)
-        inside = (position >= begin) & (position < end)
-        degree = (base + position).astype(jnp.float32)
-        plain = jnp.where(inside, scaling, 0.0)
-        sloped = plain * (degree * (1.0 / LMAX))
-        ahead_factor = jnp.where(
-            inside & (position < end - 1),
-            (degree + (1.0 + own_order.astype(jnp.float32))) * (scaling * (1.0 / LMAX)),
-            0.0,
-        )
-        curved = sloped * ((degree + 1.0) * (1.0 / LMAX))
+        own, after = [
+            jnp.concatenate([a[0:2], a[0:2], a[2:4], a[2:4]], axis=0) for a in (own, after)
+        ]
         weights = jnp.concatenate(
-            [spread[0] * plain, spread[0] * sloped, spread[1] * ahead_factor, spread[0] * curved],
+            [
+                (after if index == 2 else own) * factor_ref[index, :, start : start + size]
+                for index in range(4)
+            ],
             axis=0,
         ).astype(jnp.bfloat16)
-        held = min(size, PACK - start)
-        synth = synth + lax.dot_general(
-            weights[:, :held],
-            table_ref[:, start : start + held],
-            (((1,), (1,)), ((), ())),
-            preferred_element_type=jnp.float32,
+        synth = synth + jnp.dot(
+            weights, table_ref[start : start + size, :], preferred_element_type=jnp.float32
         )
     sine, cosine = info_ref[0:1, :RINGS], info_ref[1:2, :RINGS]
     fields = [synth[0:8], (cosine * synth[8:16] - synth[16:24]) / sine, synth[24:32]]
@@ -238,24 +265,23 @@
         ]
         scaled = first * inverse
         half = (0.5 * scaled) * inverse
-        for index, rows in enumerate((slope, scaled, half, slope * inverse, 0.5 * laplace)):
+        for index, rows in enumerate((slope, 0.5 * laplace, scaled, slope * inverse, half)):
             high = rows.astype(jnp.bfloat16)
             low = (rows - high.astype(jnp.float32)).astype(jnp.bfloat16)
-            left_ref[index, :, 0:ROWS] = high
-            left_ref[index, :, ROWS:] = low
-
-    rows_here = pl.ds(pl.multiple_of(pl.program_id(0) * RINGS, RINGS), RINGS)
-
-    def to_grid(rows, table):
-        return jnp.dot(
-            left_ref[rows, rows_here, :], table_ref[table], preferred_element_type=jnp.float32
-        )
-
-    p = to_grid(0, 0)
-    q = to_grid(1, 1)
-    half_t = to_grid(2, 2)
-    s = to_grid(3, 1)
-    half_l = to_grid(4, 0)
+            for layer in range(2):
+                here = slice(layer * RINGS, (layer + 1) * RINGS)
+                there = slice(index * RINGS, (index + 1) * RINGS)
+                left_ref[layer, there, 0:ROWS] = high[here]
+                left_ref[layer, there, ROWS:] = low[here]
+
+    def to_grids(first, count, table):
+        rows = left_ref[pl.program_id(0), first * RINGS : (first + count) * RINGS, :]
+        product = jnp.dot(rows, table_ref[table], preferred_element_type=jnp.float32)
+        return [product[index * RINGS : (index + 1) * RINGS] for index in range(count)]
+
+    p, half_l = to_grids(0, 2, 0)
+    q, s = to_grids(2, 2, 1)
+    (half_t,) = to_grids(4, 1, 2)
     p2, q2 = p * p, q * q
     outer = 1.0 + q2
     area = outer + p2
@@ -297,18 +323,8 @@
             value, "ord", [(k, k // size * size + (k + stride * step) % size) for k in range(n_ord)]
         )
 
-    wave, info, orders = pl.pallas_call(
-        prepare_kernel,
-        out_shape=[
-            jax.ShapeDtypeStruct((ROWS, meridians), jnp.bfloat16),
-            jax.ShapeDtypeStruct((8, lines), jnp.float32),
-            jax.ShapeDtypeStruct((ROWS, 128), jnp.int32),
-        ],
-        in_specs=[VMEM],
-        out_specs=[VMEM] * 3,
-        cost_estimate=COST,
-        compiler_params=pltpu.CompilerParams(vmem_limit_bytes=24 << 20),
-    )(jnp.stack([span_azimuthal_modes, slot_mapping]))
+    small = jnp.stack([span_azimuthal_modes, slot_mapping])
+    wave = call(prepare_kernel, (ROWS, meridians), jnp.bfloat16, [VMEM], cost_estimate=COST)(small)
     product = pl.pallas_call(
         forward_kernel,
         out_shape=[jax.ShapeDtypeStruct((32, lines), jnp.float32)] * 4,
@@ -316,6 +332,17 @@
         out_specs=[VMEM] * 4,
         compiler_params=pltpu.CompilerParams(vmem_limit_bytes=24 << 20),
     )(wave, altitude_grids)
+    info, orders = pl.pallas_call(
+        info_kernel,
+        out_shape=[
+            jax.ShapeDtypeStruct((8, lines), jnp.float32),
+            jax.ShapeDtypeStruct((ROWS, 128), jnp.int32),
+        ],
+        in_specs=[VMEM, ANY],
+        out_specs=[VMEM] * 2,
+        cost_estimate=COST,
+        compiler_params=pltpu.CompilerParams(vmem_limit_bytes=24 << 20),
+    )(small, product[0])
     parts = [product[0]] + [from_back(product[a], 1, STEPS[a]) for a in (1, 2, 3)]
 
     def hold(which, after):
@@ -338,7 +365,7 @@
             compiler_params=pltpu.CompilerParams(vmem_limit_bytes=24 << 20),
         )(*values, after)
 
-    other_table = hold(1, info)
+    other_table = hold(1, product[0])
     keep, send = summed(gather_kernel, 16, parts, other_table)
     own_table = hold(0, keep)
     keep, send = summed(halve_kernel, 8, [keep, swap(send, "ord", 4)], own_table)
@@ -357,26 +384,47 @@
         orders, outgoing
     )
 
-    def turn(value, step):
+    def exchanged(value, even, odd):
         n = lax.axis_size("lat")
-        return lax.ppermute(value, "lat", [(k, k // 8 * 8 + (k + 2 * step) % 8) for k in range(n)])
-
-    received = [turn(coeffs, step) for step in STEPS[1:]]
-    coeffs = call(add_kernel, (4, PADDED), jnp.float32, [VMEM] * 4 + [ANY])(
-        coeffs, *received, tables
-    )
-    coeffs = coeffs + swap(coeffs, "lat", 8)
+        return lax.ppermute(value, "lat", [(k, k ^ (odd if k % 2 else even)) for k in range(n)])
+
+    def summed_with(value, received, *done):
+        return call(add_kernel, (4, PADDED), jnp.float32, [VMEM] * 2 + [ANY] * len(done))(
+            value, received, *done
+        )
+
+    def factor(which, after):
+        return call(
+            functools.partial(factor_kernel, which),
+            (4, 8, PADDED),
+            jnp.float32,
+            [VMEM, ANY],
+            cost_estimate=COST,
+        )(info, after)
+
+    factors = [factor(which, coeffs) for which in (0, 1)]
+    coeffs = summed_with(coeffs, exchanged(coeffs, 2, 6), *factors)
+    coeffs = summed_with(coeffs, exchanged(coeffs, 6, 8), tables)
+    own_turned, other_turned = pl.pallas_call(
+        turn_kernel,
+        out_shape=[jax.ShapeDtypeStruct((PADDED, rings), jnp.bfloat16)] * 2,
+        in_specs=[VMEM, VMEM, ANY],
+        out_specs=[VMEM] * 2,
+        cost_estimate=COST,
+        compiler_params=pltpu.CompilerParams(vmem_limit_bytes=24 << 20),
+    )(own_table, other_table, coeffs)
+    coeffs = summed_with(coeffs, exchanged(coeffs, 8, 2), own_turned, other_turned)
     other = swap(coeffs, "lat", 1)
 
     mine = call(
-        functools.partial(synthesis_kernel, 0), (12, layers * rings), jnp.float32, [VMEM] * 3
-    )(coeffs, info, own_table)
+        functools.partial(synthesis_kernel, 0), (12, layers * rings), jnp.float32, [VMEM] * 4
+    )(coeffs, info, own_turned, factors[0])
     fields = call(
         functools.partial(synthesis_kernel, 1),
         (24, layers * rings),
         jnp.float32,
-        [VMEM] * 4 + [ANY],
-    )(other, info, other_table, mine, tables)
+        [VMEM] * 5 + [ANY],
+    )(other, info, other_turned, factors[1], mine, tables)
 
     column = jnp.stack([fields] + [from_back(fields, 4, step) for step in STEPS[1:]])
     blocks = [column] + [from_back(column, 1, step) for step in STEPS[1:]]
@@ -388,7 +436,7 @@
         out_shape=[jax.ShapeDtypeStruct((layers, rings, meridians), jnp.bfloat16)] * 2,
         in_specs=[VMEM] * 6,
         out_specs=[block, block],
-        scratch_shapes=[pltpu.VMEM((5, layers * rings, 2 * ROWS), jnp.bfloat16)],
+        scratch_shapes=[pltpu.VMEM((layers, 5 * rings, 2 * ROWS), jnp.bfloat16)],
         compiler_params=pltpu.CompilerParams(vmem_limit_bytes=32 << 20),
     )(*blocks, info, tables)
 

time: 74.4 us -> 72.8 us (0.978)
  starting transfers between devices: 34.4 us -> 32.3 us
  Pallas kernels: 17.7 us -> 19.3 us
    ppermute x5 -> x4, waiting for transfers between devices: 7.04 us -> 2.36 us  [swap(): lax.ppermute(value, axis, [(k, k ^ mask) for k in range(lax.axis_size(axi...]
    ppermute x3, waiting for transfers between devices: 5.64 us -> 10.1 us  [exchanged(): lax.ppermute(value, 'lat', [(k, k ^ (odd if k % 2 else even)) for k in ra...]
    pallas_call x2 -> x8, Pallas kernels: 1.52 us -> 5.31 us  [the longest x1 3 us: on_device(): pl.pallas_call(turn_kernel, out_shape=[jax.ShapeDtypeStruct((PADDED, ring...]
    ppermute x5 -> x4, starting transfers between devices: 10.4 us -> 9.05 us  [swap(): lax.ppermute(value, axis, [(k, k ^ mask) for k in range(lax.axis_size(axi...]
    pallas_call x1, Pallas kernels: 2.54 us -> 1.33 us  [on_device(): call(table_kernel, (3, 2 * ROWS, meridians), jnp.bfloat16, [VMEM, ANY], c...]
  transfers between devices with their start and end apart: 17 -> 16, of which waited for: 11 -> 11; matrix products, arithmetic and copies ran while one was open for 0% -> 0% of each run, Pallas kernels for 12% -> 16%
where the time goes in v4:
time: 72.8 us; the launch traced here: 72.7 us
  starting transfers between devices  32.3 us (44%)
  waiting for transfers between devices  19.5 us (27%)
  Pallas kernels  19.3 us (27%)
  other arithmetic  0.83 us (1%)
  between operations  0.82 us (1%)
    ppermute x9, starting transfers between devices, from_back(): lax.ppermute(value, 'ord', [(k, k // size * size + (k + stride * step) %...  20.4 us
    ppermute x3, waiting for transfers between devices, exchanged(): lax.ppermute(value, 'lat', [(k, k ^ (odd if k % 2 else even)) for k in ra...  10.1 us
    ppermute x4, starting transfers between devices, swap(): lax.ppermute(value, axis, [(k, k ^ mask) for k in range(lax.axis_size(axi...  9.05 us
    ppermute x9, waiting for transfers between devices, from_back(): lax.ppermute(value, 'ord', [(k, k // size * size + (k + stride * step) %...  7.05 us
    pallas_call x2, Pallas kernels, hold(): call(functools.partial(hold_kernel, which), polynomial_values.shape[1:],...  4.4 us
    pallas_call x1, Pallas kernels, on_device(): pl.pallas_call(inverse_kernel, grid=(layers,), out_shape=[jax.ShapeDtypeS...  4 us
    pallas_call x1, Pallas kernels, on_device(): pl.pallas_call(turn_kernel, out_shape=[jax.ShapeDtypeStruct((PADDED, ring...  3 us
    ppermute x3, starting transfers between devices, exchanged(): lax.ppermute(value, 'lat', [(k, k ^ (odd if k % 2 else even)) for k in ra...  2.86 us
  transfers between devices with their start and end apart: 16, of which 11 were waited for; matrix products, arithmetic and copies ran while one was open for 0% of the time, Pallas kernels for 16%

profile of v4, /device:TPU:6, one launch (start us, length us, event | category | flops | bytes accessed | tf_op | source)
XLA Modules:
  0.0 72.7 jit_solution(9039841293842589131)
XLA Ops:
  0.6 0.0 copy-start
  0.6 0.8 %pad_add_fusion.small_ref = s32[2,64]{1,0:T(2,128)S(1)} fusion(s32[1,64]{1,0:T(1,128)} %bitcast.10, s32[1,64]{1,0:T(1,128)} %bitcast.11), kind=kLoop, calls=%fused_computation.1 | loop fusion | flops 128 | bytes 1024 | tf_op jit(solution)/shard_map/stack | solution.py:326
  1.4 1.4 %shard_map.59.wave_ref = bf16[128,1350]{1,0:T(8,128)(2,1)S(1)} custom-call(s32[2,64]{1,0:T(2,128)S(1)} %pad_add_fusion.small_ref), custom_call_target="tpu_custom_call" | custom-call | flops 1000000000 | bytes 4000000 | tf_op jit(solution)/shard_map/pallas_call | solution.py:327
  2.8 0.0 copy-done
  2.8 0.4 shard_map.60
  3.3 3.3 %collective-permute-start = (f32[32,384]{1,0:T(8,128)S(1)}, f32[32,384]{1,0:T(8,128)S(1)}, u32[]{:S(2)}, u32[]{:S(2)}) collective-permute-start(f32[32,384]{1,0:T(8,128)S(1)} %get-tuple-element.15), channel_id=1, source_target_pairs={{0,2},{1,3},{2,0},{3,1},{4,6},{5,7},{6,4},{7,5},{8,10},{9,11},{10,... | collective-permute-start | bytes 147464 | tf_op jit(solution)/shard_map/ppermute | solution.py:322
  6.6 0.7 collective-permute-start.1
  7.2 2.6 %collective-permute-start.2 = (f32[32,384]{1,0:T(8,128)S(1)}, f32[32,384]{1,0:T(8,128)S(1)}, u32[]{:S(2)}, u32[]{:S(2)}) collective-permute-start(f32[32,384]{1,0:T(8,128)S(1)} %get-tuple-element.17), channel_id=1, source_target_pairs={{0,3},{1,0},{2,1},{3,2},{4,7},{5,4},{6,5},{7,6},{8,11},{9,8},{10,9... | collective-permute-start | bytes 147464 | tf_op jit(solution)/shard_map/ppermute | solution.py:322
  9.8 2.2 %shard_map.61._.table_ref.other_ref = bf16[192,10802]{1,0:T(8,128)(2,1)S(1)} custom-call(bf16[2,192,10802]{2,1,0:T(8,128)(2,1)} %table_ref.3, f32[32,384]{1,0:T(8,128)S(1)} %get-tuple-element.14._.first_ref), custom_call_target="tpu_custom_call" | custom-call | flops 1000000000 | bytes 4000000 | tf_op jit(solution)/shard_map/pallas_call | solution.py:349
  12.0 0.0 collective-permute-done.second_ref
  12.0 0.0 collective-permute-done.1.third_ref
  12.0 0.0 collective-permute-done.2.fourth_ref
  12.1 3.4 %collective-permute-start.3 = (f32[16,384]{1,0:T(8,128)S(1)}, f32[16,384]{1,0:T(8,128)S(1)}, u32[]{:S(2)}, u32[]{:S(2)}) collective-permute-start(f32[16,384]{1,0:T(8,128)S(1)} %get-tuple-element.19), channel_id=1, source_target_pairs={{0,4},{1,5},{2,6},{3,7},{4,0},{5,1},{6,2},{7,3},{8,12},{9,13},{10,... | collective-permute-start | bytes 73736 | tf_op jit(solution)/shard_map/ppermute | solution.py:30
  15.4 2.2 %shard_map.63._.table_ref.own_ref = bf16[192,10802]{1,0:T(8,128)(2,1)S(1)} custom-call(bf16[2,192,10802]{2,1,0:T(8,128)(2,1)} %table_ref.3, f32[16,384]{1,0:T(8,128)S(1)} %get-tuple-element.18._.first_ref), custom_call_target="tpu_custom_call" | custom-call | flops 1000000000 | bytes 4000000 | tf_op jit(solution)/shard_map/pallas_call | solution.py:349
  17.6 0.0 collective-permute-done.3.second_ref
  17.6 5.5 %collective-permute-start.4 = (f32[8,384]{1,0:T(8,128)S(1)}, f32[8,384]{1,0:T(8,128)S(1)}, u32[]{:S(2)}, u32[]{:S(2)}) collective-permute-start(f32[8,384]{1,0:T(8,128)S(1)} %get-tuple-element.21), channel_id=1, source_target_pairs={{0,12},{1,13},{2,14},{3,15},{4,8},{5,9},{6,10},{7,11},{8,4},{9,5},... | collective-permute-start | bytes 36872 | tf_op jit(solution)/shard_map/ppermute | solution.py:30
  23.2 0.2 shard_map.65
  23.4 1.4 %collective-permute-done.4.second_ref = f32[8,384]{1,0:T(8,128)S(1)} collective-permute-done((f32[8,384]{1,0:T(8,128)S(1)}, f32[8,384]{1,0:T(8,128)S(1)}, u32[]{:S(2)}, u32[]{:S(2)}) %collective-permute-start.4) | collective-permute-done | bytes 12320 | tf_op jit(solution)/shard_map/ppermute | solution.py:30
  24.9 0.7 %shard_map.67.after_ref = f32[4,10880]{1,0:T(4,128)S(1)} custom-call(f32[8,384]{1,0:T(8,128)S(1)} %get-tuple-element.20.first_ref, f32[8,384]{1,0:T(8,128)S(1)} %collective-permute-done.4.second_ref, f32[8,384]{1,0:T(8,128)S(1)} %get-tuple-element.22.info_ref.refs_4_, bf16[192,10802]{1,0:T(8,128)(2,1)S(1)} %shard_map.61._.table_ref.other_ref), custom_call_target="tpu_custom_call" | custom-call | tf_op jit(solution)/shard_map/pallas_call | solution.py:376
  25.6 0.1 collective-permute-start.5
  25.7 0.7 %shard_map.66 = f32[4,10880]{1,0:T(4,128)S(1)} custom-call(f32[8,384]{1,0:T(8,128)S(1)} %get-tuple-element.20.first_ref, f32[8,384]{1,0:T(8,128)S(1)} %collective-permute-done.4.second_ref, f32[8,384]{1,0:T(8,128)S(1)} %get-tuple-element.22.info_ref.refs_4_, bf16[192,10802]{1,0:T(8,128)(2,1)S(1)} %shard_map.63._.table_ref.own_ref), custom_call_target="tpu_custom_call" | custom-call | tf_op jit(solution)/shard_map/pallas_call | solution.py:376
  26.4 0.7 collective-permute-done.5
  27.1 0.9 %collective-permute-start.6 = (f32[4,10880]{1,0:T(4,128)S(1)}, f32[4,10880]{1,0:T(4,128)S(1)}, u32[]{:S(2)}, u32[]{:S(2)}) collective-permute-start(f32[4,10880]{1,0:T(4,128)S(1)} %add.3._.first_ref), channel_id=1, source_target_pairs={{0,32},{16,112},{32,0},{48,80},{64,96},{80,48},{96,64},{112,16},{1... | collective-permute-start | bytes 522248 | tf_op jit(solution)/shard_map/ppermute | solution.py:389
  28.0 0.3 shard_map.69.rest_1_.factor_ref
  28.3 0.3 shard_map.68.rest_0_.factor_ref
  28.6 4.0 %collective-permute-done.6.second_ref = f32[4,10880]{1,0:T(4,128)S(1)} collective-permute-done((f32[4,10880]{1,0:T(4,128)S(1)}, f32[4,10880]{1,0:T(4,128)S(1)}, u32[]{:S(2)}, u32[]{:S(2)}) %collective-permute-start.6) | collective-permute-done | bytes 174112 | tf_op jit(solution)/shard_map/ppermute | solution.py:389
  32.7 0.6 collective-permute-start.7
  33.2 1.3 %shard_map.71.rest_0_.rest_1_.refs_5_ = bf16[3,256,1350]{2,1,0:T(8,128)(2,1)S(1)} custom-call(s32[128,128]{1,0:T(8,128)S(1)} %get-tuple-element.23.orders_ref, f32[4,10880]{1,0:T(4,128)S(1)} %shard_map.67.after_ref), custom_call_target="tpu_custom_call" | custom-call | flops 1000000000 | bytes 4000000 | tf_op jit(solution)/shard_map/pallas_call | solution.py:383
  34.6 4.8 %collective-permute-done.7.second_ref = f32[4,10880]{1,0:T(4,128)S(1)} collective-permute-done((f32[4,10880]{1,0:T(4,128)S(1)}, f32[4,10880]{1,0:T(4,128)S(1)}, u32[]{:S(2)}, u32[]{:S(2)}) %collective-permute-start.7) | collective-permute-done | bytes 174112 | tf_op jit(solution)/shard_map/ppermute | solution.py:389
  39.4 1.4 %collective-permute-start.8 = (f32[4,10880]{1,0:T(4,128)S(1)}, f32[4,10880]{1,0:T(4,128)S(1)}, u32[]{:S(2)}, u32[]{:S(2)}) collective-permute-start(f32[4,10880]{1,0:T(4,128)S(1)} %shard_map.72._.first_ref), channel_id=1, source_target_pairs={{0,128},{16,48},{32,160},{48,16},{64,192},{80,112},{96,224},{112,8... | collective-permute-start | bytes 522248 | tf_op jit(solution)/shard_map/ppermute | solution.py:389
  40.8 3.0 %shard_map.73 = (bf16[10880,192]{1,0:T(8,128)(2,1)S(1)}, bf16[10880,192]{1,0:T(8,128)(2,1)S(1)}) custom-call(bf16[192,10802]{1,0:T(8,128)(2,1)S(1)} %shard_map.63._.table_ref.own_ref, bf16[192,10802]{1,0:T(8,128)(2,1)S(1)} %shard_map.61._.table_ref.other_ref, f32[4,10880]{1,0:T(4,128)S(1)} %shard_map.72._.first_ref), custom_call_target="tpu_custom_call" | custom-call | flops 1000000000 | bytes 4000000 | tf_op jit(solution)/shard_map/pallas_call | solution.py:408
  43.8 1.3 %collective-permute-done.8.second_ref = f32[4,10880]{1,0:T(4,128)S(1)} collective-permute-done((f32[4,10880]{1,0:T(4,128)S(1)}, f32[4,10880]{1,0:T(4,128)S(1)}, u32[]{:S(2)}, u32[]{:S(2)}) %collective-permute-start.8) | collective-permute-done | bytes 174112 | tf_op jit(solution)/shard_map/ppermute | solution.py:389
  45.1 0.1 collective-permute-start.9
  45.2 1.1 %shard_map.75.rest_0_ = f32[12,384]{1,0:T(8,128)S(1)} custom-call(f32[4,10880]{1,0:T(4,128)S(1)} %shard_map.74.coeffs_ref, f32[8,384]{1,0:T(8,128)S(1)} %get-tuple-element.22.info_ref.refs_4_, bf16[10880,192]{1,0:T(8,128)(2,1)S(1)} %get-tuple-element.24.rest_0_.table_ref, f32[4,8,10880]{2,1,0:T(8,128)S(1)} %shard_map.68.rest_0_.factor_ref), custom_call_target="tpu_custom_call" | custom-call | tf_op jit(solution)/shard_map/pallas_call | solution.py:419
  46.4 0.3 collective-permute-done.9.coeffs_ref
  46.6 1.2 %shard_map.76 = f32[24,384]{1,0:T(8,128)S(1)} custom-call(f32[4,10880]{1,0:T(4,128)S(1)} %collective-permute-done.9.coeffs_ref, f32[8,384]{1,0:T(8,128)S(1)} %get-tuple-element.22.info_ref.refs_4_, bf16[10880,192]{1,0:T(8,128)(2,1)S(1)} %get-tuple-element.25.rest_1_.table_ref, f32[4,8,10880]{2,1,0:T(8,128)S(1)} %shard_map.69.rest_1_.factor_ref, ...), custom_call_target="tpu_custom_call" | custom-call | tf_op jit(solution)/shard_map/pallas_call | solution.py:422
  47.8 5.1 %collective-permute-start.10 = (f32[24,384]{1,0:T(8,128)S(1)}, f32[24,384]{1,0:T(8,128)S(1)}, u32[]{:S(2)}, u32[]{:S(2)}) collective-permute-start(f32[24,384]{1,0:T(8,128)S(1)} %shard_map.76), channel_id=1, source_target_pairs={{0,8},{1,9},{2,10},{3,11},{4,12},{5,13},{6,14},{7,15},{8,0},{9,1},... | collective-permute-start | bytes 110600 | tf_op jit(solution)/shard_map/ppermute | solution.py:322
  52.9 1.5 %collective-permute-start.11 = (f32[24,384]{1,0:T(8,128)S(1)}, f32[24,384]{1,0:T(8,128)S(1)}, u32[]{:S(2)}, u32[]{:S(2)}) collective-permute-start(f32[24,384]{1,0:T(8,128)S(1)} %shard_map.76), channel_id=1, source_target_pairs={{0,4},{1,5},{2,6},{3,7},{4,8},{5,9},{6,10},{7,11},{8,12},{9,13},{1... | collective-permute-start | bytes 110600 | tf_op jit(solution)/shard_map/ppermute | solution.py:322
  54.4 2.7 %collective-permute-start.12 = (f32[24,384]{1,0:T(8,128)S(1)}, f32[24,384]{1,0:T(8,128)S(1)}, u32[]{:S(2)}, u32[]{:S(2)}) collective-permute-start(f32[24,384]{1,0:T(8,128)S(1)} %shard_map.76), channel_id=1, source_target_pairs={{0,12},{1,13},{2,14},{3,15},{4,0},{5,1},{6,2},{7,3},{8,4},{9,5},{1... | collective-permute-start | bytes 110600 | tf_op jit(solution)/shard_map/ppermute | solution.py:322
  57.0 0.0 collective-permute-done.10
  57.1 1.9 %collective-permute-done.11 = f32[24,384]{1,0:T(8,128)S(1)} collective-permute-done((f32[24,384]{1,0:T(8,128)S(1)}, f32[24,384]{1,0:T(8,128)S(1)}, u32[]{:S(2)}, u32[]{:S(2)}) %collective-permute-start.11) | collective-permute-done | bytes 36896 | tf_op jit(solution)/shard_map/ppermute | solution.py:322
  59.0 0.3 collective-permute-done.12
  59.3 1.4 %collective-permute-start.13 = (f32[4,24,384]{2,1,0:T(8,128)S(1)}, f32[4,24,384]{2,1,0:T(8,128)S(1)}, u32[]{:S(2)}, u32[]{:S(2)}) collective-permute-start(f32[4,24,384]{2,1,0:T(8,128)S(1)} %pad_maximum_fusion.refs_0_), channel_id=1, source_target_pairs={{0,2},{1,3},{2,0},{3,1},{4,6},{5,7},{6,4},{7,5},{8,10},{9,11},{10,... | collective-permute-start | bytes 442376 | tf_op jit(solution)/shard_map/ppermute | solution.py:322
  60.6 2.6 %collective-permute-start.14 = (f32[4,24,384]{2,1,0:T(8,128)S(1)}, f32[4,24,384]{2,1,0:T(8,128)S(1)}, u32[]{:S(2)}, u32[]{:S(2)}) collective-permute-start(f32[4,24,384]{2,1,0:T(8,128)S(1)} %pad_maximum_fusion.refs_0_), channel_id=1, source_target_pairs={{0,1},{1,2},{2,3},{3,0},{4,5},{5,6},{6,7},{7,4},{8,9},{9,10},{10,1... | collective-permute-start | bytes 442376 | tf_op jit(solution)/shard_map/ppermute | solution.py:322
  63.3 0.6 collective-permute-start.15
  63.9 3.0 %collective-permute-done.13.refs_1_ = f32[4,24,384]{2,1,0:T(8,128)S(1)} collective-permute-done((f32[4,24,384]{2,1,0:T(8,128)S(1)}, f32[4,24,384]{2,1,0:T(8,128)S(1)}, u32[]{:S(2)}, u32[]{:S(2)}) %collective-permute-start.13) | collective-permute-done | bytes 147488 | tf_op jit(solution)/shard_map/ppermute | solution.py:322
  66.8 1.5 %collective-permute-done.14.refs_2_ = f32[4,24,384]{2,1,0:T(8,128)S(1)} collective-permute-done((f32[4,24,384]{2,1,0:T(8,128)S(1)}, f32[4,24,384]{2,1,0:T(8,128)S(1)}, u32[]{:S(2)}, u32[]{:S(2)}) %collective-permute-start.14) | collective-permute-done | bytes 147488 | tf_op jit(solution)/shard_map/ppermute | solution.py:322
  68.3 0.4 collective-permute-done.15.refs_3_
  68.7 4.0 %shard_map.77 = (bf16[2,192,1350]{2,1,0:T(8,128)(2,1)}, bf16[2,192,1350]{2,1,0:T(8,128)(2,1)}) custom-call(f32[4,24,384]{2,1,0:T(8,128)S(1)} %pad_maximum_fusion.refs_0_, f32[4,24,384]{2,1,0:T(8,128)S(1)} %collective-permute-done.13.refs_1_, f32[4,24,384]{2,1,0:T(8,128)S(1)} %collective-permute-done.14.refs_2_, ...), custom_call_target="tpu_custom_call" | custom-call | tf_op jit(solution)/shard_map/pallas_call | solution.py:433
  (7 shorter events, 0.1 us)
Async XLA Ops:
  0.6 2.2 %copy-start = (bf16[2,192,1350]{2,1,0:T(8,128)(2,1)S(1)}, bf16[2,192,1350]{2,1,0:T(8,128)(2,1)}, u32[]{:S(2)}) copy-start(bf16[2,192,1350]{2,1,0:T(8,128)(2,1)} %grids_ref.1) | copy-start | bytes 3110404
  3.3 8.7 %collective-permute-start = (f32[32,384]{1,0:T(8,128)S(1)}, f32[32,384]{1,0:T(8,128)S(1)}, u32[]{:S(2)}, u32[]{:S(2)}) collective-permute-start(f32[32,384]{1,0:T(8,128)S(1)} %get-tuple-element.15), channel_id=1, source_target_pairs={{0,2},{1,3},{2,0},{3,1},{4,6},{5,7},{6,4},{7,5},{8,10},{9,11},{10,... | collective-permute-start | bytes 147464 | tf_op jit(solution)/shard_map/ppermute | solution.py:322
  6.6 5.5 %collective-permute-start.1 = (f32[32,384]{1,0:T(8,128)S(1)}, f32[32,384]{1,0:T(8,128)S(1)}, u32[]{:S(2)}, u32[]{:S(2)}) collective-permute-start(f32[32,384]{1,0:T(8,128)S(1)} %get-tuple-element.16), channel_id=1, source_target_pairs={{0,1},{1,2},{2,3},{3,0},{4,5},{5,6},{6,7},{7,4},{8,9},{9,10},{10,1... | collective-permute-start | bytes 147464 | tf_op jit(solution)/shard_map/ppermute | solution.py:322
  7.2 4.8 %collective-permute-start.2 = (f32[32,384]{1,0:T(8,128)S(1)}, f32[32,384]{1,0:T(8,128)S(1)}, u32[]{:S(2)}, u32[]{:S(2)}) collective-permute-start(f32[32,384]{1,0:T(8,128)S(1)} %get-tuple-element.17), channel_id=1, source_target_pairs={{0,3},{1,0},{2,1},{3,2},{4,7},{5,4},{6,5},{7,6},{8,11},{9,8},{10,9... | collective-permute-start | bytes 147464 | tf_op jit(solution)/shard_map/ppermute | solution.py:322
  12.1 5.6 %collective-permute-start.3 = (f32[16,384]{1,0:T(8,128)S(1)}, f32[16,384]{1,0:T(8,128)S(1)}, u32[]{:S(2)}, u32[]{:S(2)}) collective-permute-start(f32[16,384]{1,0:T(8,128)S(1)} %get-tuple-element.19), channel_id=1, source_target_pairs={{0,4},{1,5},{2,6},{3,7},{4,0},{5,1},{6,2},{7,3},{8,12},{9,13},{10,... | collective-permute-start | bytes 73736 | tf_op jit(solution)/shard_map/ppermute | solution.py:30
  17.6 7.2 %collective-permute-start.4 = (f32[8,384]{1,0:T(8,128)S(1)}, f32[8,384]{1,0:T(8,128)S(1)}, u32[]{:S(2)}, u32[]{:S(2)}) collective-permute-start(f32[8,384]{1,0:T(8,128)S(1)} %get-tuple-element.21), channel_id=1, source_target_pairs={{0,12},{1,13},{2,14},{3,15},{4,8},{5,9},{6,10},{7,11},{8,4},{9,5},... | collective-permute-start | bytes 36872 | tf_op jit(solution)/shard_map/ppermute | solution.py:30
  25.6 1.5 %collective-permute-start.5 = (f32[4,10880]{1,0:T(4,128)S(1)}, f32[4,10880]{1,0:T(4,128)S(1)}, u32[]{:S(2)}, u32[]{:S(2)}) collective-permute-start(f32[4,10880]{1,0:T(4,128)S(1)} %shard_map.67.after_ref), channel_id=1, source_target_pairs={{0,16},{16,0},{32,48},{48,32},{64,80},{80,64},{96,112},{112,96},{1... | collective-permute-start | bytes 522248 | tf_op jit(solution)/shard_map/ppermute | solution.py:30
  27.1 5.5 %collective-permute-start.6 = (f32[4,10880]{1,0:T(4,128)S(1)}, f32[4,10880]{1,0:T(4,128)S(1)}, u32[]{:S(2)}, u32[]{:S(2)}) collective-permute-start(f32[4,10880]{1,0:T(4,128)S(1)} %add.3._.first_ref), channel_id=1, source_target_pairs={{0,32},{16,112},{32,0},{48,80},{64,96},{80,48},{96,64},{112,16},{1... | collective-permute-start | bytes 522248 | tf_op jit(solution)/shard_map/ppermute | solution.py:389
  32.7 6.7 %collective-permute-start.7 = (f32[4,10880]{1,0:T(4,128)S(1)}, f32[4,10880]{1,0:T(4,128)S(1)}, u32[]{:S(2)}, u32[]{:S(2)}) collective-permute-start(f32[4,10880]{1,0:T(4,128)S(1)} %shard_map.70.first_ref), channel_id=1, source_target_pairs={{0,96},{16,144},{32,64},{48,176},{64,32},{80,208},{96,0},{112,240}... | collective-permute-start | bytes 522248 | tf_op jit(solution)/shard_map/ppermute | solution.py:389
  39.4 5.7 %collective-permute-start.8 = (f32[4,10880]{1,0:T(4,128)S(1)}, f32[4,10880]{1,0:T(4,128)S(1)}, u32[]{:S(2)}, u32[]{:S(2)}) collective-permute-start(f32[4,10880]{1,0:T(4,128)S(1)} %shard_map.72._.first_ref), channel_id=1, source_target_pairs={{0,128},{16,48},{32,160},{48,16},{64,192},{80,112},{96,224},{112,8... | collective-permute-start | bytes 522248 | tf_op jit(solution)/shard_map/ppermute | solution.py:389
  45.1 1.5 %collective-permute-start.9 = (f32[4,10880]{1,0:T(4,128)S(1)}, f32[4,10880]{1,0:T(4,128)S(1)}, u32[]{:S(2)}, u32[]{:S(2)}) collective-permute-start(f32[4,10880]{1,0:T(4,128)S(1)} %shard_map.74.coeffs_ref), channel_id=1, source_target_pairs={{0,16},{16,0},{32,48},{48,32},{64,80},{80,64},{96,112},{112,96},{1... | collective-permute-start | bytes 522248 | tf_op jit(solution)/shard_map/ppermute | solution.py:30
  47.8 9.3 %collective-permute-start.10 = (f32[24,384]{1,0:T(8,128)S(1)}, f32[24,384]{1,0:T(8,128)S(1)}, u32[]{:S(2)}, u32[]{:S(2)}) collective-permute-start(f32[24,384]{1,0:T(8,128)S(1)} %shard_map.76), channel_id=1, source_target_pairs={{0,8},{1,9},{2,10},{3,11},{4,12},{5,13},{6,14},{7,15},{8,0},{9,1},... | collective-permute-start | bytes 110600 | tf_op jit(solution)/shard_map/ppermute | solution.py:322
  52.9 6.1 %collective-permute-start.11 = (f32[24,384]{1,0:T(8,128)S(1)}, f32[24,384]{1,0:T(8,128)S(1)}, u32[]{:S(2)}, u32[]{:S(2)}) collective-permute-start(f32[24,384]{1,0:T(8,128)S(1)} %shard_map.76), channel_id=1, source_target_pairs={{0,4},{1,5},{2,6},{3,7},{4,8},{5,9},{6,10},{7,11},{8,12},{9,13},{1... | collective-permute-start | bytes 110600 | tf_op jit(solution)/shard_map/ppermute | solution.py:322
  54.4 4.9 %collective-permute-start.12 = (f32[24,384]{1,0:T(8,128)S(1)}, f32[24,384]{1,0:T(8,128)S(1)}, u32[]{:S(2)}, u32[]{:S(2)}) collective-permute-start(f32[24,384]{1,0:T(8,128)S(1)} %shard_map.76), channel_id=1, source_target_pairs={{0,12},{1,13},{2,14},{3,15},{4,0},{5,1},{6,2},{7,3},{8,4},{9,5},{1... | collective-permute-start | bytes 110600 | tf_op jit(solution)/shard_map/ppermute | solution.py:322
  59.3 7.6 %collective-permute-start.13 = (f32[4,24,384]{2,1,0:T(8,128)S(1)}, f32[4,24,384]{2,1,0:T(8,128)S(1)}, u32[]{:S(2)}, u32[]{:S(2)}) collective-permute-start(f32[4,24,384]{2,1,0:T(8,128)S(1)} %pad_maximum_fusion.refs_0_), channel_id=1, source_target_pairs={{0,2},{1,3},{2,0},{3,1},{4,6},{5,7},{6,4},{7,5},{8,10},{9,11},{10,... | collective-permute-start | bytes 442376 | tf_op jit(solution)/shard_map/ppermute | solution.py:322
  60.6 7.7 %collective-permute-start.14 = (f32[4,24,384]{2,1,0:T(8,128)S(1)}, f32[4,24,384]{2,1,0:T(8,128)S(1)}, u32[]{:S(2)}, u32[]{:S(2)}) collective-permute-start(f32[4,24,384]{2,1,0:T(8,128)S(1)} %pad_maximum_fusion.refs_0_), channel_id=1, source_target_pairs={{0,1},{1,2},{2,3},{3,0},{4,5},{5,6},{6,7},{7,4},{8,9},{9,10},{10,1... | collective-permute-start | bytes 442376 | tf_op jit(solution)/shard_map/ppermute | solution.py:322
  63.3 5.5 %collective-permute-start.15 = (f32[4,24,384]{2,1,0:T(8,128)S(1)}, f32[4,24,384]{2,1,0:T(8,128)S(1)}, u32[]{:S(2)}, u32[]{:S(2)}) collective-permute-start(f32[4,24,384]{2,1,0:T(8,128)S(1)} %pad_maximum_fusion.refs_0_), channel_id=1, source_target_pairs={{0,3},{1,0},{2,1},{3,2},{4,7},{5,4},{6,5},{7,6},{8,11},{9,8},{10,9... | collective-permute-start | bytes 442376 | tf_op jit(solution)/shard_map/ppermute | solution.py:322

commit v5 on v4

--- a/solution.py
+++ b/solution.py
@@ -20,6 +20,7 @@
 ROWS = 2 * BAND
 STEPS = (0, 2, 1, 3)
 MASKS = (0, 3, 1, 2)
+COLUMNS = 256
 
 SINE_SERIES = tuple(
     (-1.0) ** n * (2.0 * math.pi) ** (2 * n + 1) / math.factorial(2 * n + 1) for n in range(7)
@@ -274,21 +275,24 @@
                 left_ref[layer, there, 0:ROWS] = high[here]
                 left_ref[layer, there, ROWS:] = low[here]
 
-    def to_grids(first, count, table):
-        rows = left_ref[pl.program_id(0), first * RINGS : (first + count) * RINGS, :]
-        product = jnp.dot(rows, table_ref[table], preferred_element_type=jnp.float32)
-        return [product[index * RINGS : (index + 1) * RINGS] for index in range(count)]
-
-    p, half_l = to_grids(0, 2, 0)
-    q, s = to_grids(2, 2, 1)
-    (half_t,) = to_grids(4, 1, 2)
-    p2, q2 = p * p, q * q
-    outer = 1.0 + q2
-    area = outer + p2
-    root = lax.rsqrt(area)
-    steep_ref[0] = (area * root).astype(jnp.bfloat16)
-    top = (q2 - p2) * half_t - outer * half_l - (p * q) * s
-    bend_ref[0] = (top * (root * root * root)).astype(jnp.bfloat16)
+    for start in range(0, MERIDIANS, COLUMNS):
+        here = slice(start, min(start + COLUMNS, MERIDIANS))
+
+        def to_grids(first, count, table):
+            rows = left_ref[pl.program_id(0), first * RINGS : (first + count) * RINGS, :]
+            product = jnp.dot(rows, table_ref[table, :, here], preferred_element_type=jnp.float32)
+            return [product[index * RINGS : (index + 1) * RINGS] for index in range(count)]
+
+        p, half_l = to_grids(0, 2, 0)
+        q, s = to_grids(2, 2, 1)
+        (half_t,) = to_grids(4, 1, 2)
+        p2, q2 = p * p, q * q
+        outer = 1.0 + q2
+        area = outer + p2
+        root = lax.rsqrt(area)
+        steep_ref[0, :, here] = (area * root).astype(jnp.bfloat16)
+        top = (q2 - p2) * half_t - outer * half_l - (p * q) * s
+        bend_ref[0, :, here] = (top * (root * root * root)).astype(jnp.bfloat16)
 
 
 VMEM = pl.BlockSpec(memory_space=pltpu.VMEM)

time: 72.8 us -> 72.5 us (level)
  no operation moved by 1% of the time
where the time goes in v5:
time: 72.5 us; the launch traced here: 72.3 us
  starting transfers between devices  32.3 us (45%)
  waiting for transfers between devices  19.5 us (27%)
  Pallas kernels  18.9 us (26%)
  other arithmetic  0.83 us (1%)
  between operations  0.82 us (1%)
    ppermute x9, starting transfers between devices, from_back(): lax.ppermute(value, 'ord', [(k, k // size * size + (k + stride * step) %...  20.4 us
    ppermute x3, waiting for transfers between devices, exchanged(): lax.ppermute(value, 'lat', [(k, k ^ (odd if k % 2 else even)) for k in ra...  10.1 us
    ppermute x4, starting transfers between devices, swap(): lax.ppermute(value, axis, [(k, k ^ mask) for k in range(lax.axis_size(axi...  9.05 us
    ppermute x9, waiting for transfers between devices, from_back(): lax.ppermute(value, 'ord', [(k, k // size * size + (k + stride * step) %...  7.05 us
    pallas_call x2, Pallas kernels, hold(): call(functools.partial(hold_kernel, which), polynomial_values.shape[1:],...  4.4 us
    pallas_call x1, Pallas kernels, on_device(): pl.pallas_call(inverse_kernel, grid=(layers,), out_shape=[jax.ShapeDtypeS...  3.62 us
    pallas_call x1, Pallas kernels, on_device(): pl.pallas_call(turn_kernel, out_shape=[jax.ShapeDtypeStruct((PADDED, ring...  3 us
    ppermute x3, starting transfers between devices, exchanged(): lax.ppermute(value, 'lat', [(k, k ^ (odd if k % 2 else even)) for k in ra...  2.86 us
  transfers between devices with their start and end apart: 16, of which 11 were waited for; matrix products, arithmetic and copies ran while one was open for 0% of the time, Pallas kernels for 16%

profile of v5, /device:TPU:6, one launch (start us, length us, event | category | flops | bytes accessed | tf_op | source)
XLA Modules:
  0.0 72.3 jit_solution(2221937950096955344)
XLA Ops:
  0.6 0.0 copy-start
  0.6 0.8 %pad_add_fusion.small_ref = s32[2,64]{1,0:T(2,128)S(1)} fusion(s32[1,64]{1,0:T(1,128)} %bitcast.10, s32[1,64]{1,0:T(1,128)} %bitcast.11), kind=kLoop, calls=%fused_computation.1 | loop fusion | flops 128 | bytes 1024 | tf_op jit(solution)/shard_map/stack | solution.py:330
  1.4 1.4 %shard_map.59.wave_ref = bf16[128,1350]{1,0:T(8,128)(2,1)S(1)} custom-call(s32[2,64]{1,0:T(2,128)S(1)} %pad_add_fusion.small_ref), custom_call_target="tpu_custom_call" | custom-call | flops 1000000000 | bytes 4000000 | tf_op jit(solution)/shard_map/pallas_call | solution.py:331
  2.8 0.0 copy-done
  2.8 0.4 shard_map.60
  3.3 3.3 %collective-permute-start = (f32[32,384]{1,0:T(8,128)S(1)}, f32[32,384]{1,0:T(8,128)S(1)}, u32[]{:S(2)}, u32[]{:S(2)}) collective-permute-start(f32[32,384]{1,0:T(8,128)S(1)} %get-tuple-element.15), channel_id=1, source_target_pairs={{0,2},{1,3},{2,0},{3,1},{4,6},{5,7},{6,4},{7,5},{8,10},{9,11},{10,... | collective-permute-start | bytes 147464 | tf_op jit(solution)/shard_map/ppermute | solution.py:326
  6.6 0.7 collective-permute-start.1
  7.2 2.6 %collective-permute-start.2 = (f32[32,384]{1,0:T(8,128)S(1)}, f32[32,384]{1,0:T(8,128)S(1)}, u32[]{:S(2)}, u32[]{:S(2)}) collective-permute-start(f32[32,384]{1,0:T(8,128)S(1)} %get-tuple-element.17), channel_id=1, source_target_pairs={{0,3},{1,0},{2,1},{3,2},{4,7},{5,4},{6,5},{7,6},{8,11},{9,8},{10,9... | collective-permute-start | bytes 147464 | tf_op jit(solution)/shard_map/ppermute | solution.py:326
  9.8 2.2 %shard_map.61._.table_ref.other_ref = bf16[192,10802]{1,0:T(8,128)(2,1)S(1)} custom-call(bf16[2,192,10802]{2,1,0:T(8,128)(2,1)} %table_ref.3, f32[32,384]{1,0:T(8,128)S(1)} %get-tuple-element.14._.first_ref), custom_call_target="tpu_custom_call" | custom-call | flops 1000000000 | bytes 4000000 | tf_op jit(solution)/shard_map/pallas_call | solution.py:353
  12.0 0.0 collective-permute-done.second_ref
  12.0 0.0 collective-permute-done.1.third_ref
  12.0 0.0 collective-permute-done.2.fourth_ref
  12.1 3.4 %collective-permute-start.3 = (f32[16,384]{1,0:T(8,128)S(1)}, f32[16,384]{1,0:T(8,128)S(1)}, u32[]{:S(2)}, u32[]{:S(2)}) collective-permute-start(f32[16,384]{1,0:T(8,128)S(1)} %get-tuple-element.19), channel_id=1, source_target_pairs={{0,4},{1,5},{2,6},{3,7},{4,0},{5,1},{6,2},{7,3},{8,12},{9,13},{10,... | collective-permute-start | bytes 73736 | tf_op jit(solution)/shard_map/ppermute | solution.py:31
  15.4 2.2 %shard_map.63._.table_ref.own_ref = bf16[192,10802]{1,0:T(8,128)(2,1)S(1)} custom-call(bf16[2,192,10802]{2,1,0:T(8,128)(2,1)} %table_ref.3, f32[16,384]{1,0:T(8,128)S(1)} %get-tuple-element.18._.first_ref), custom_call_target="tpu_custom_call" | custom-call | flops 1000000000 | bytes 4000000 | tf_op jit(solution)/shard_map/pallas_call | solution.py:353
  17.6 0.0 collective-permute-done.3.second_ref
  17.6 5.5 %collective-permute-start.4 = (f32[8,384]{1,0:T(8,128)S(1)}, f32[8,384]{1,0:T(8,128)S(1)}, u32[]{:S(2)}, u32[]{:S(2)}) collective-permute-start(f32[8,384]{1,0:T(8,128)S(1)} %get-tuple-element.21), channel_id=1, source_target_pairs={{0,12},{1,13},{2,14},{3,15},{4,8},{5,9},{6,10},{7,11},{8,4},{9,5},... | collective-permute-start | bytes 36872 | tf_op jit(solution)/shard_map/ppermute | solution.py:31
  23.2 0.2 shard_map.65
  23.4 1.4 %collective-permute-done.4.second_ref = f32[8,384]{1,0:T(8,128)S(1)} collective-permute-done((f32[8,384]{1,0:T(8,128)S(1)}, f32[8,384]{1,0:T(8,128)S(1)}, u32[]{:S(2)}, u32[]{:S(2)}) %collective-permute-start.4) | collective-permute-done | bytes 12320 | tf_op jit(solution)/shard_map/ppermute | solution.py:31
  24.9 0.7 %shard_map.67.after_ref = f32[4,10880]{1,0:T(4,128)S(1)} custom-call(f32[8,384]{1,0:T(8,128)S(1)} %get-tuple-element.20.first_ref, f32[8,384]{1,0:T(8,128)S(1)} %collective-permute-done.4.second_ref, f32[8,384]{1,0:T(8,128)S(1)} %get-tuple-element.22.info_ref.refs_4_, bf16[192,10802]{1,0:T(8,128)(2,1)S(1)} %shard_map.61._.table_ref.other_ref), custom_call_target="tpu_custom_call" | custom-call | tf_op jit(solution)/shard_map/pallas_call | solution.py:380
  25.6 0.1 collective-permute-start.5
  25.7 0.7 %shard_map.66 = f32[4,10880]{1,0:T(4,128)S(1)} custom-call(f32[8,384]{1,0:T(8,128)S(1)} %get-tuple-element.20.first_ref, f32[8,384]{1,0:T(8,128)S(1)} %collective-permute-done.4.second_ref, f32[8,384]{1,0:T(8,128)S(1)} %get-tuple-element.22.info_ref.refs_4_, bf16[192,10802]{1,0:T(8,128)(2,1)S(1)} %shard_map.63._.table_ref.own_ref), custom_call_target="tpu_custom_call" | custom-call | tf_op jit(solution)/shard_map/pallas_call | solution.py:380
  26.4 0.7 collective-permute-done.5
  27.1 0.9 %collective-permute-start.6 = (f32[4,10880]{1,0:T(4,128)S(1)}, f32[4,10880]{1,0:T(4,128)S(1)}, u32[]{:S(2)}, u32[]{:S(2)}) collective-permute-start(f32[4,10880]{1,0:T(4,128)S(1)} %add.3._.first_ref), channel_id=1, source_target_pairs={{0,32},{16,112},{32,0},{48,80},{64,96},{80,48},{96,64},{112,16},{1... | collective-permute-start | bytes 522248 | tf_op jit(solution)/shard_map/ppermute | solution.py:393
  28.0 0.3 shard_map.69.rest_1_.factor_ref
  28.3 0.3 shard_map.68.rest_0_.factor_ref
  28.6 4.0 %collective-permute-done.6.second_ref = f32[4,10880]{1,0:T(4,128)S(1)} collective-permute-done((f32[4,10880]{1,0:T(4,128)S(1)}, f32[4,10880]{1,0:T(4,128)S(1)}, u32[]{:S(2)}, u32[]{:S(2)}) %collective-permute-start.6) | collective-permute-done | bytes 174112 | tf_op jit(solution)/shard_map/ppermute | solution.py:393
  32.7 0.6 collective-permute-start.7
  33.2 1.3 %shard_map.71.rest_0_.rest_1_.refs_5_ = bf16[3,256,1350]{2,1,0:T(8,128)(2,1)S(1)} custom-call(s32[128,128]{1,0:T(8,128)S(1)} %get-tuple-element.23.orders_ref, f32[4,10880]{1,0:T(4,128)S(1)} %shard_map.67.after_ref), custom_call_target="tpu_custom_call" | custom-call | flops 1000000000 | bytes 4000000 | tf_op jit(solution)/shard_map/pallas_call | solution.py:387
  34.6 4.8 %collective-permute-done.7.second_ref = f32[4,10880]{1,0:T(4,128)S(1)} collective-permute-done((f32[4,10880]{1,0:T(4,128)S(1)}, f32[4,10880]{1,0:T(4,128)S(1)}, u32[]{:S(2)}, u32[]{:S(2)}) %collective-permute-start.7) | collective-permute-done | bytes 174112 | tf_op jit(solution)/shard_map/ppermute | solution.py:393
  39.4 1.4 %collective-permute-start.8 = (f32[4,10880]{1,0:T(4,128)S(1)}, f32[4,10880]{1,0:T(4,128)S(1)}, u32[]{:S(2)}, u32[]{:S(2)}) collective-permute-start(f32[4,10880]{1,0:T(4,128)S(1)} %shard_map.72._.first_ref), channel_id=1, source_target_pairs={{0,128},{16,48},{32,160},{48,16},{64,192},{80,112},{96,224},{112,8... | collective-permute-start | bytes 522248 | tf_op jit(solution)/shard_map/ppermute | solution.py:393
  40.8 3.0 %shard_map.73 = (bf16[10880,192]{1,0:T(8,128)(2,1)S(1)}, bf16[10880,192]{1,0:T(8,128)(2,1)S(1)}) custom-call(bf16[192,10802]{1,0:T(8,128)(2,1)S(1)} %shard_map.63._.table_ref.own_ref, bf16[192,10802]{1,0:T(8,128)(2,1)S(1)} %shard_map.61._.table_ref.other_ref, f32[4,10880]{1,0:T(4,128)S(1)} %shard_map.72._.first_ref), custom_call_target="tpu_custom_call" | custom-call | flops 1000000000 | bytes 4000000 | tf_op jit(solution)/shard_map/pallas_call | solution.py:412
  43.8 1.3 %collective-permute-done.8.second_ref = f32[4,10880]{1,0:T(4,128)S(1)} collective-permute-done((f32[4,10880]{1,0:T(4,128)S(1)}, f32[4,10880]{1,0:T(4,128)S(1)}, u32[]{:S(2)}, u32[]{:S(2)}) %collective-permute-start.8) | collective-permute-done | bytes 174112 | tf_op jit(solution)/shard_map/ppermute | solution.py:393
  45.1 0.1 collective-permute-start.9
  45.2 1.1 %shard_map.75.rest_0_ = f32[12,384]{1,0:T(8,128)S(1)} custom-call(f32[4,10880]{1,0:T(4,128)S(1)} %shard_map.74.coeffs_ref, f32[8,384]{1,0:T(8,128)S(1)} %get-tuple-element.22.info_ref.refs_4_, bf16[10880,192]{1,0:T(8,128)(2,1)S(1)} %get-tuple-element.24.rest_0_.table_ref, f32[4,8,10880]{2,1,0:T(8,128)S(1)} %shard_map.68.rest_0_.factor_ref), custom_call_target="tpu_custom_call" | custom-call | tf_op jit(solution)/shard_map/pallas_call | solution.py:423
  46.4 0.3 collective-permute-done.9.coeffs_ref
  46.6 1.2 %shard_map.76 = f32[24,384]{1,0:T(8,128)S(1)} custom-call(f32[4,10880]{1,0:T(4,128)S(1)} %collective-permute-done.9.coeffs_ref, f32[8,384]{1,0:T(8,128)S(1)} %get-tuple-element.22.info_ref.refs_4_, bf16[10880,192]{1,0:T(8,128)(2,1)S(1)} %get-tuple-element.25.rest_1_.table_ref, f32[4,8,10880]{2,1,0:T(8,128)S(1)} %shard_map.69.rest_1_.factor_ref, ...), custom_call_target="tpu_custom_call" | custom-call | tf_op jit(solution)/shard_map/pallas_call | solution.py:426
  47.8 5.1 %collective-permute-start.10 = (f32[24,384]{1,0:T(8,128)S(1)}, f32[24,384]{1,0:T(8,128)S(1)}, u32[]{:S(2)}, u32[]{:S(2)}) collective-permute-start(f32[24,384]{1,0:T(8,128)S(1)} %shard_map.76), channel_id=1, source_target_pairs={{0,8},{1,9},{2,10},{3,11},{4,12},{5,13},{6,14},{7,15},{8,0},{9,1},... | collective-permute-start | bytes 110600 | tf_op jit(solution)/shard_map/ppermute | solution.py:326
  52.9 1.5 %collective-permute-start.11 = (f32[24,384]{1,0:T(8,128)S(1)}, f32[24,384]{1,0:T(8,128)S(1)}, u32[]{:S(2)}, u32[]{:S(2)}) collective-permute-start(f32[24,384]{1,0:T(8,128)S(1)} %shard_map.76), channel_id=1, source_target_pairs={{0,4},{1,5},{2,6},{3,7},{4,8},{5,9},{6,10},{7,11},{8,12},{9,13},{1... | collective-permute-start | bytes 110600 | tf_op jit(solution)/shard_map/ppermute | solution.py:326
  54.4 2.7 %collective-permute-start.12 = (f32[24,384]{1,0:T(8,128)S(1)}, f32[24,384]{1,0:T(8,128)S(1)}, u32[]{:S(2)}, u32[]{:S(2)}) collective-permute-start(f32[24,384]{1,0:T(8,128)S(1)} %shard_map.76), channel_id=1, source_target_pairs={{0,12},{1,13},{2,14},{3,15},{4,0},{5,1},{6,2},{7,3},{8,4},{9,5},{1... | collective-permute-start | bytes 110600 | tf_op jit(solution)/shard_map/ppermute | solution.py:326
  57.0 0.0 collective-permute-done.10
  57.1 1.9 %collective-permute-done.11 = f32[24,384]{1,0:T(8,128)S(1)} collective-permute-done((f32[24,384]{1,0:T(8,128)S(1)}, f32[24,384]{1,0:T(8,128)S(1)}, u32[]{:S(2)}, u32[]{:S(2)}) %collective-permute-start.11) | collective-permute-done | bytes 36896 | tf_op jit(solution)/shard_map/ppermute | solution.py:326
  59.0 0.3 collective-permute-done.12
  59.3 1.4 %collective-permute-start.13 = (f32[4,24,384]{2,1,0:T(8,128)S(1)}, f32[4,24,384]{2,1,0:T(8,128)S(1)}, u32[]{:S(2)}, u32[]{:S(2)}) collective-permute-start(f32[4,24,384]{2,1,0:T(8,128)S(1)} %pad_maximum_fusion.refs_0_), channel_id=1, source_target_pairs={{0,2},{1,3},{2,0},{3,1},{4,6},{5,7},{6,4},{7,5},{8,10},{9,11},{10,... | collective-permute-start | bytes 442376 | tf_op jit(solution)/shard_map/ppermute | solution.py:326
  60.6 2.6 %collective-permute-start.14 = (f32[4,24,384]{2,1,0:T(8,128)S(1)}, f32[4,24,384]{2,1,0:T(8,128)S(1)}, u32[]{:S(2)}, u32[]{:S(2)}) collective-permute-start(f32[4,24,384]{2,1,0:T(8,128)S(1)} %pad_maximum_fusion.refs_0_), channel_id=1, source_target_pairs={{0,1},{1,2},{2,3},{3,0},{4,5},{5,6},{6,7},{7,4},{8,9},{9,10},{10,1... | collective-permute-start | bytes 442376 | tf_op jit(solution)/shard_map/ppermute | solution.py:326
  63.3 0.6 collective-permute-start.15
  63.9 3.0 %collective-permute-done.13.refs_1_ = f32[4,24,384]{2,1,0:T(8,128)S(1)} collective-permute-done((f32[4,24,384]{2,1,0:T(8,128)S(1)}, f32[4,24,384]{2,1,0:T(8,128)S(1)}, u32[]{:S(2)}, u32[]{:S(2)}) %collective-permute-start.13) | collective-permute-done | bytes 147488 | tf_op jit(solution)/shard_map/ppermute | solution.py:326
  66.8 1.5 %collective-permute-done.14.refs_2_ = f32[4,24,384]{2,1,0:T(8,128)S(1)} collective-permute-done((f32[4,24,384]{2,1,0:T(8,128)S(1)}, f32[4,24,384]{2,1,0:T(8,128)S(1)}, u32[]{:S(2)}, u32[]{:S(2)}) %collective-permute-start.14) | collective-permute-done | bytes 147488 | tf_op jit(solution)/shard_map/ppermute | solution.py:326
  68.3 0.4 collective-permute-done.15.refs_3_
  68.7 3.6 %shard_map.77 = (bf16[2,192,1350]{2,1,0:T(8,128)(2,1)}, bf16[2,192,1350]{2,1,0:T(8,128)(2,1)}) custom-call(f32[4,24,384]{2,1,0:T(8,128)S(1)} %pad_maximum_fusion.refs_0_, f32[4,24,384]{2,1,0:T(8,128)S(1)} %collective-permute-done.13.refs_1_, f32[4,24,384]{2,1,0:T(8,128)S(1)} %collective-permute-done.14.refs_2_, ...), custom_call_target="tpu_custom_call" | custom-call | tf_op jit(solution)/shard_map/pallas_call | solution.py:437
  (7 shorter events, 0.1 us)
Async XLA Ops:
  0.6 2.2 %copy-start = (bf16[2,192,1350]{2,1,0:T(8,128)(2,1)S(1)}, bf16[2,192,1350]{2,1,0:T(8,128)(2,1)}, u32[]{:S(2)}) copy-start(bf16[2,192,1350]{2,1,0:T(8,128)(2,1)} %grids_ref.1) | copy-start | bytes 3110404
  3.3 8.7 %collective-permute-start = (f32[32,384]{1,0:T(8,128)S(1)}, f32[32,384]{1,0:T(8,128)S(1)}, u32[]{:S(2)}, u32[]{:S(2)}) collective-permute-start(f32[32,384]{1,0:T(8,128)S(1)} %get-tuple-element.15), channel_id=1, source_target_pairs={{0,2},{1,3},{2,0},{3,1},{4,6},{5,7},{6,4},{7,5},{8,10},{9,11},{10,... | collective-permute-start | bytes 147464 | tf_op jit(solution)/shard_map/ppermute | solution.py:326
  6.6 5.5 %collective-permute-start.1 = (f32[32,384]{1,0:T(8,128)S(1)}, f32[32,384]{1,0:T(8,128)S(1)}, u32[]{:S(2)}, u32[]{:S(2)}) collective-permute-start(f32[32,384]{1,0:T(8,128)S(1)} %get-tuple-element.16), channel_id=1, source_target_pairs={{0,1},{1,2},{2,3},{3,0},{4,5},{5,6},{6,7},{7,4},{8,9},{9,10},{10,1... | collective-permute-start | bytes 147464 | tf_op jit(solution)/shard_map/ppermute | solution.py:326
  7.2 4.8 %collective-permute-start.2 = (f32[32,384]{1,0:T(8,128)S(1)}, f32[32,384]{1,0:T(8,128)S(1)}, u32[]{:S(2)}, u32[]{:S(2)}) collective-permute-start(f32[32,384]{1,0:T(8,128)S(1)} %get-tuple-element.17), channel_id=1, source_target_pairs={{0,3},{1,0},{2,1},{3,2},{4,7},{5,4},{6,5},{7,6},{8,11},{9,8},{10,9... | collective-permute-start | bytes 147464 | tf_op jit(solution)/shard_map/ppermute | solution.py:326
  12.1 5.6 %collective-permute-start.3 = (f32[16,384]{1,0:T(8,128)S(1)}, f32[16,384]{1,0:T(8,128)S(1)}, u32[]{:S(2)}, u32[]{:S(2)}) collective-permute-start(f32[16,384]{1,0:T(8,128)S(1)} %get-tuple-element.19), channel_id=1, source_target_pairs={{0,4},{1,5},{2,6},{3,7},{4,0},{5,1},{6,2},{7,3},{8,12},{9,13},{10,... | collective-permute-start | bytes 73736 | tf_op jit(solution)/shard_map/ppermute | solution.py:31
  17.6 7.2 %collective-permute-start.4 = (f32[8,384]{1,0:T(8,128)S(1)}, f32[8,384]{1,0:T(8,128)S(1)}, u32[]{:S(2)}, u32[]{:S(2)}) collective-permute-start(f32[8,384]{1,0:T(8,128)S(1)} %get-tuple-element.21), channel_id=1, source_target_pairs={{0,12},{1,13},{2,14},{3,15},{4,8},{5,9},{6,10},{7,11},{8,4},{9,5},... | collective-permute-start | bytes 36872 | tf_op jit(solution)/shard_map/ppermute | solution.py:31
  25.6 1.5 %collective-permute-start.5 = (f32[4,10880]{1,0:T(4,128)S(1)}, f32[4,10880]{1,0:T(4,128)S(1)}, u32[]{:S(2)}, u32[]{:S(2)}) collective-permute-start(f32[4,10880]{1,0:T(4,128)S(1)} %shard_map.67.after_ref), channel_id=1, source_target_pairs={{0,16},{16,0},{32,48},{48,32},{64,80},{80,64},{96,112},{112,96},{1... | collective-permute-start | bytes 522248 | tf_op jit(solution)/shard_map/ppermute | solution.py:31
  27.1 5.5 %collective-permute-start.6 = (f32[4,10880]{1,0:T(4,128)S(1)}, f32[4,10880]{1,0:T(4,128)S(1)}, u32[]{:S(2)}, u32[]{:S(2)}) collective-permute-start(f32[4,10880]{1,0:T(4,128)S(1)} %add.3._.first_ref), channel_id=1, source_target_pairs={{0,32},{16,112},{32,0},{48,80},{64,96},{80,48},{96,64},{112,16},{1... | collective-permute-start | bytes 522248 | tf_op jit(solution)/shard_map/ppermute | solution.py:393
  32.7 6.7 %collective-permute-start.7 = (f32[4,10880]{1,0:T(4,128)S(1)}, f32[4,10880]{1,0:T(4,128)S(1)}, u32[]{:S(2)}, u32[]{:S(2)}) collective-permute-start(f32[4,10880]{1,0:T(4,128)S(1)} %shard_map.70.first_ref), channel_id=1, source_target_pairs={{0,96},{16,144},{32,64},{48,176},{64,32},{80,208},{96,0},{112,240}... | collective-permute-start | bytes 522248 | tf_op jit(solution)/shard_map/ppermute | solution.py:393
  39.4 5.7 %collective-permute-start.8 = (f32[4,10880]{1,0:T(4,128)S(1)}, f32[4,10880]{1,0:T(4,128)S(1)}, u32[]{:S(2)}, u32[]{:S(2)}) collective-permute-start(f32[4,10880]{1,0:T(4,128)S(1)} %shard_map.72._.first_ref), channel_id=1, source_target_pairs={{0,128},{16,48},{32,160},{48,16},{64,192},{80,112},{96,224},{112,8... | collective-permute-start | bytes 522248 | tf_op jit(solution)/shard_map/ppermute | solution.py:393
  45.1 1.5 %collective-permute-start.9 = (f32[4,10880]{1,0:T(4,128)S(1)}, f32[4,10880]{1,0:T(4,128)S(1)}, u32[]{:S(2)}, u32[]{:S(2)}) collective-permute-start(f32[4,10880]{1,0:T(4,128)S(1)} %shard_map.74.coeffs_ref), channel_id=1, source_target_pairs={{0,16},{16,0},{32,48},{48,32},{64,80},{80,64},{96,112},{112,96},{1... | collective-permute-start | bytes 522248 | tf_op jit(solution)/shard_map/ppermute | solution.py:31
  47.8 9.3 %collective-permute-start.10 = (f32[24,384]{1,0:T(8,128)S(1)}, f32[24,384]{1,0:T(8,128)S(1)}, u32[]{:S(2)}, u32[]{:S(2)}) collective-permute-start(f32[24,384]{1,0:T(8,128)S(1)} %shard_map.76), channel_id=1, source_target_pairs={{0,8},{1,9},{2,10},{3,11},{4,12},{5,13},{6,14},{7,15},{8,0},{9,1},... | collective-permute-start | bytes 110600 | tf_op jit(solution)/shard_map/ppermute | solution.py:326
  52.9 6.1 %collective-permute-start.11 = (f32[24,384]{1,0:T(8,128)S(1)}, f32[24,384]{1,0:T(8,128)S(1)}, u32[]{:S(2)}, u32[]{:S(2)}) collective-permute-start(f32[24,384]{1,0:T(8,128)S(1)} %shard_map.76), channel_id=1, source_target_pairs={{0,4},{1,5},{2,6},{3,7},{4,8},{5,9},{6,10},{7,11},{8,12},{9,13},{1... | collective-permute-start | bytes 110600 | tf_op jit(solution)/shard_map/ppermute | solution.py:326
  54.4 4.9 %collective-permute-start.12 = (f32[24,384]{1,0:T(8,128)S(1)}, f32[24,384]{1,0:T(8,128)S(1)}, u32[]{:S(2)}, u32[]{:S(2)}) collective-permute-start(f32[24,384]{1,0:T(8,128)S(1)} %shard_map.76), channel_id=1, source_target_pairs={{0,12},{1,13},{2,14},{3,15},{4,0},{5,1},{6,2},{7,3},{8,4},{9,5},{1... | collective-permute-start | bytes 110600 | tf_op jit(solution)/shard_map/ppermute | solution.py:326
  59.3 7.6 %collective-permute-start.13 = (f32[4,24,384]{2,1,0:T(8,128)S(1)}, f32[4,24,384]{2,1,0:T(8,128)S(1)}, u32[]{:S(2)}, u32[]{:S(2)}) collective-permute-start(f32[4,24,384]{2,1,0:T(8,128)S(1)} %pad_maximum_fusion.refs_0_), channel_id=1, source_target_pairs={{0,2},{1,3},{2,0},{3,1},{4,6},{5,7},{6,4},{7,5},{8,10},{9,11},{10,... | collective-permute-start | bytes 442376 | tf_op jit(solution)/shard_map/ppermute | solution.py:326
  60.6 7.7 %collective-permute-start.14 = (f32[4,24,384]{2,1,0:T(8,128)S(1)}, f32[4,24,384]{2,1,0:T(8,128)S(1)}, u32[]{:S(2)}, u32[]{:S(2)}) collective-permute-start(f32[4,24,384]{2,1,0:T(8,128)S(1)} %pad_maximum_fusion.refs_0_), channel_id=1, source_target_pairs={{0,1},{1,2},{2,3},{3,0},{4,5},{5,6},{6,7},{7,4},{8,9},{9,10},{10,1... | collective-permute-start | bytes 442376 | tf_op jit(solution)/shard_map/ppermute | solution.py:326
  63.3 5.5 %collective-permute-start.15 = (f32[4,24,384]{2,1,0:T(8,128)S(1)}, f32[4,24,384]{2,1,0:T(8,128)S(1)}, u32[]{:S(2)}, u32[]{:S(2)}) collective-permute-start(f32[4,24,384]{2,1,0:T(8,128)S(1)} %pad_maximum_fusion.refs_0_), channel_id=1, source_target_pairs={{0,3},{1,0},{2,1},{3,2},{4,7},{5,4},{6,5},{7,6},{8,11},{9,8},{10,9... | collective-permute-start | bytes 442376 | tf_op jit(solution)/shard_map/ppermute | solution.py:326
